TPU v7x, 512 devices: a whole 4x8x8 slice. The times are simulated.
512 devices in a mesh: gx: 16 (over z, x_lo), gy: 32 (over y, x_hi, core).
Axes of the slice: x: 4 (x_hi: 2, x_lo: 2; x = x_hi * 2 + x_lo), y: 8, z: 8, core: 2. Of those that a mesh axis runs over, the one named last changes fastest.
Arguments:
- inputs: bfloat16 [1024, 8192], P('gy', 'gx'), may hold values from -6 to 6
- gate_weight: bfloat16 [8192, 16384], P('gx', 'gy'), may hold values from -0.0625 to 0.0625
- up_weight: bfloat16 [8192, 16384], P('gx', 'gy'), may hold values from -0.0625 to 0.0625
- down_weight: bfloat16 [16384, 8192], P('gy', 'gx'), may hold values from -0.046875 to 0.046875
- cotangent: bfloat16 [1024, 8192], P('gy', 'gx'), may hold values from -6 to 6
Outputs:
- input_grad: bfloat16 [1024, 8192], P('gy', 'gx')
- gate_grad: bfloat16 [8192, 16384], P('gx', 'gy')
- up_grad: bfloat16 [8192, 16384], P('gx', 'gy')
- down_grad: bfloat16 [16384, 8192], P('gy', 'gx')
All inputs are finite; a program needn't handle non-finite values.
Results may differ from a plain program's by a relative error of at most 0.0049.
Values may be sent and summed in bfloat16 or wider, within the bound.
No kernel may reach another device: no remote copies, remote signals or barrier semaphores. Data moves between devices by JAX's collectives and lax.ppermute only.
A program may use at most 64 MiB of HBM per device.

v0:
```python
import jax
import jax.numpy as jnp
from jax import lax
from jax.sharding import PartitionSpec as P


def elementwise(gate, upper, hidden_grad):
    sig = jax.nn.sigmoid(gate)
    hidden = (gate * sig * upper).astype(jnp.bfloat16)
    gate_delta = (hidden_grad * upper * sig * (1.0 + gate * (1.0 - sig))).astype(jnp.bfloat16)
    up_delta = (hidden_grad * gate * sig).astype(jnp.bfloat16)
    return (hidden, gate_delta, up_delta)


def per_device(inputs, gate_weight, up_weight, down_weight, cotangent):
    fcon = (((1,), (1,)), ((), ()))
    tcon = (((0,), (0,)), ((), ()))
    all_inputs, all_cotangent = (
        lax.all_gather(inputs, "gy", axis=0, tiled=True),
        lax.all_gather(cotangent, "gy", axis=0, tiled=True),
    )
    gate_part = jnp.dot(all_inputs, gate_weight, preferred_element_type=jnp.float32)
    upper_part = jnp.dot(all_inputs, up_weight, preferred_element_type=jnp.float32)
    grad_part = lax.dot_general(
        all_cotangent, down_weight, fcon, preferred_element_type=jnp.float32
    )
    gate, upper, hidden_grad = lax.psum((gate_part, upper_part, grad_part), "gx")
    hidden, gate_delta, up_delta = elementwise(gate, upper, hidden_grad)
    down_grad = lax.dot_general(
        hidden, all_cotangent, tcon, preferred_element_type=jnp.float32
    ).astype(jnp.bfloat16)
    gate_grad = lax.dot_general(
        all_inputs, gate_delta, tcon, preferred_element_type=jnp.float32
    ).astype(jnp.bfloat16)
    up_grad = lax.dot_general(
        all_inputs, up_delta, tcon, preferred_element_type=jnp.float32
    ).astype(jnp.bfloat16)
    total = lax.dot_general(gate_delta, gate_weight, fcon, preferred_element_type=jnp.float32)
    input_grad = lax.psum_scatter(
        total + lax.dot_general(up_delta, up_weight, fcon, preferred_element_type=jnp.float32),
        "gy",
        scatter_dimension=0,
        tiled=True,
    )
    return (input_grad.astype(jnp.bfloat16), gate_grad, up_grad, down_grad)


def solution(mesh):
    in_specs = (P("gy", "gx"), P("gx", "gy"), P("gx", "gy"), P("gy", "gx"), P("gy", "gx"))
    out_specs = (P("gy", "gx"), P("gx", "gy"), P("gx", "gy"), P("gy", "gx"))
    return jax.shard_map(
        per_device, mesh=mesh, in_specs=in_specs, out_specs=out_specs, check_vma=False
    )
```

profile of v0, /device:TPU:1, one launch (start us, length us, event | category | flops | bytes accessed | tf_op | source)
XLA Modules:
  0.0 612.8 jit_solution(12614478969231618911)
XLA Ops:
  7.2 0.0 all-gather.5.cloned.1.call-start
  7.2 0.7 all-gather.5.cloned.1.call-update
  7.9 0.0 all-gather.3.cloned.1.call-start
  8.0 0.7 all-gather.3.cloned.1.call-update
  8.7 0.0 all-reduce.3.cloned.1.call-start
  8.7 91.5 %all-gather.5.cloned.1.call-done = bf16[1024,512]{1,0:T(8,128)(2,1)} async-done(((bf16[32,512]{1,0:T(8,128)(2,1)}), bf16[1024,512]{1,0:T(8,128)(2,1)}) %all-gather.5.cloned.1.call-update) | async-done | bytes 1048592 | tf_op jit(solution)/shard_map/all_gather | solution.py:19
  100.2 3.4 fusion.5
  103.5 2.0 fusion.4
  105.6 77.9 %all-gather.3.cloned.1.call-done = bf16[1024,512]{1,0:T(8,128)(2,1)} async-done(((bf16[32,512]{1,0:T(8,128)(2,1)}), bf16[1024,512]{1,0:T(8,128)(2,1)}) %all-gather.3.cloned.1.call-update) | async-done | bytes 1048592 | tf_op jit(solution)/shard_map/all_gather | solution.py:20
  183.5 3.3 fusion.3
  186.8 0.0 all-reduce.3.cloned.1.call-update
  186.9 0.0 reduce-scatter.2.cloned.1.call-start
  186.9 287.4 %all-reduce.3.cloned.1.call-done = (f32[1024,512]{1,0:T(8,128)}, f32[1024,512]{1,0:T(8,128)}, f32[1024,512]{1,0:T(8,128)}) async-done(((f32[1024,512]{1,0:T(8,128)}, f32[1024,512]{1,0:T(8,128)}, f32[1024,512]{1,0:T(8,128)}), (f32[1024,512]{1,0:T(8,128)}, f32[1024,512]{1,0:T(8,128)}, f32[1024,512]{1,0:T(8,128)})) %all-reduce.3.cloned.1.call-update) | async-done | bytes 6291472 | tf_op jit(solution)/shard_map/psum | solution.py:27
  474.3 4.0 multiply_convert_fusion.1
  478.3 0.7 fusion.6
  479.1 0.3 copy-done.2
  479.3 2.1 convolution_add_fusion
  481.5 0.7 fusion
  482.2 1.0 copy.9
  483.2 2.0 fusion.1
  485.3 1.0 copy.10
  486.3 3.8 convolution_convert_fusion
  490.1 114.8 %reduce-scatter.2.cloned.1.call-done = f32[32,512]{1,0:T(8,128)} async-done(((f32[1024,512]{1,0:T(8,128)}), f32[32,512]{1,0:T(8,128)}) %reduce-scatter.2.cloned.1.call-update) | async-done | bytes 65552 | tf_op jit(solution)/shard_map/reduce_scatter | solution.py:39
  604.8 1.5 convert_element_type.29
  (12 shorter events, 0.0 us)
Async XLA Ops:
  7.2 93.0 %copy-start = (bf16[512,512]{1,0:T(8,128)(2,1)S(1)}, bf16[512,512]{1,0:T(8,128)(2,1)}, u32[]{:S(2)}) copy-start(bf16[512,512]{1,0:T(8,128)(2,1)} %param.6) | copy-start | bytes 1572868
  7.2 96.4 %copy-start.3 = (bf16[512,512]{1,0:T(8,128)(2,1)S(1)}, bf16[512,512]{1,0:T(8,128)(2,1)}, u32[]{:S(2)}) copy-start(bf16[512,512]{1,0:T(8,128)(2,1)} %param.7) | copy-start | bytes 1572868
  7.2 93.0 %all-gather.5.cloned.1.call-start = ((), (), s32[]{:S(2)}) async-start(), calls=%async_computation.2 | async-start | bytes 1081344 | tf_op jit(solution)/shard_map/all_gather | solution.py:19
  7.9 175.6 %all-gather.3.cloned.1.call-start = ((), (), s32[]{:S(2)}) async-start(), calls=%async_computation.1 | async-start | bytes 1081344 | tf_op jit(solution)/shard_map/all_gather | solution.py:20
  8.7 465.6 %all-reduce.3.cloned.1.call-start = ((), (), s32[]{:S(2)}) async-start(), calls=%async_computation.4 | async-start | bytes 12582912 | tf_op jit(solution)/shard_map/psum | solution.py:27
  100.2 3.4 copy-start.1
  103.5 80.0 %copy-start.5 = (bf16[512,512]{1,0:T(8,128)(2,1)S(1)}, bf16[512,512]{1,0:T(8,128)(2,1)}, u32[]{:S(2)}) copy-start(bf16[512,512]{1,0:T(8,128)(2,1)} %param.8) | copy-start | bytes 1572868
  186.9 417.9 %reduce-scatter.2.cloned.1.call-start = ((), (), s32[]{:S(2)}) async-start(), calls=%async_computation.3 | async-start | bytes 2162688 | tf_op jit(solution)/shard_map/reduce_scatter | solution.py:39
  478.3 1.0 copy-start.2
  483.2 3.1 copy-start.4
Sparse Core Ops, SparseCore 0:
  11.4 88.7 all-gather.4
  103.5 79.9 all-gather.2
  187.0 287.2 all-reduce.2
  481.6 123.1 reduce-scatter.1
where the time goes:
time: 617 us; the launch traced here: 613 us
  waiting for transfers between devices  573 us (93%)
  matrix products  18.1 us (3%)
  between operations  13.8 us (2%)
    psum x1, waiting for transfers between devices, per_device(): lax.psum((gate_part, upper_part, grad_part), 'gx')  287 us
    reduce_scatter x1, waiting for transfers between devices, per_device(): lax.psum_scatter(total + lax.dot_general(up_delta, up_weight, fcon, prefe...  115 us
    all_gather x1, waiting for transfers between devices, per_device(): lax.all_gather(inputs, 'gy', axis=0, tiled=True)  91.5 us
    all_gather x1, waiting for transfers between devices, per_device(): lax.all_gather(cotangent, 'gy', axis=0, tiled=True)  77.9 us
  transfers between devices with their start and end apart: 4, of which 4 were waited for; matrix products, arithmetic and copies ran while one was open for 2% of the time, Pallas kernels for 0%

commit v1 on v0

v1 whole, which is shorter than its diff:
```python
import jax
import jax.numpy as jnp
from jax import lax
from jax.sharding import Mesh
from jax.sharding import PartitionSpec as P

AXES = ("z", "xl", "y", "xh", "core")
GX, GY = ("z", "xl"), ("y", "xh", "core")
SCALE = 16.0
F32, BF16, F16 = jnp.float32, jnp.bfloat16, jnp.float16


def dot(a, b, ca, cb):
    return lax.dot_general(a, b, (((ca,), (cb,)), ((), ())), preferred_element_type=F32)


def swap(x, axis):
    return lax.ppermute(x, axis, [(0, 1), (1, 0)])


def spread(x, axis, n):
    return lax.all_to_all(jnp.broadcast_to(x[None], (n,) + x.shape), axis, 0, 0, tiled=True)


def per_device(nz, ny, x, wg, wu, wd, c):
    rows, width = x.shape
    fwidth = wg.shape[1]
    z_f = fwidth // nz
    xl, xh, core = lax.axis_index("xl"), lax.axis_index("xh"), lax.axis_index("core")

    pair = jnp.concatenate([x, c], axis=0)
    own = lax.ppermute(pair, ("xl", "xh"), [(0, 0), (3, 2), (1, 1), (2, 3)])
    oth = lax.ppermute(pair, ("xl", "xh"), [(2, 0), (1, 2), (3, 1), (0, 3)])
    wg2, wu2, wd2 = swap(wg, "xl"), swap(wu, "xl"), swap(wd, "xl")
    both = jnp.concatenate([own, oth], axis=1)

    def gather_tokens(t):
        t = spread(t, "y", ny).reshape(ny * rows, 2 * width)
        return lax.all_gather(t, "core", axis=0, tiled=True)

    xs = gather_tokens(both[:rows])
    cs = gather_tokens(both[rows:])
    xo, xt, co, ct = xs[:, :width], xs[:, width:], cs[:, :width], cs[:, width:]
    half = xs.shape[0]

    def sum_over_z(part):
        part = (part * SCALE).astype(F16).reshape(nz, z_f, half)
        return lax.all_to_all(part, "z", 0, 0, tiled=True).astype(F32).sum(0) * (1.0 / SCALE)

    gate = sum_over_z(dot(wg, xo, 0, 1) + dot(wg2, xt, 0, 1))
    upper = sum_over_z(dot(wu, xo, 0, 1) + dot(wu2, xt, 0, 1))
    hidden_grad = sum_over_z(dot(wd, co, 1, 1) + dot(wd2, ct, 1, 1))
    xr, cr = swap(xt, "xl"), swap(ct, "xl")

    sig = jax.nn.sigmoid(gate)
    hidden = (gate * sig * upper).astype(BF16)
    gate_delta = (hidden_grad * upper * sig * (1.0 + gate * (1.0 - sig))).astype(BF16)
    up_delta = (hidden_grad * gate * sig).astype(BF16)

    def gather_hidden(t):
        t = spread(t, "z", nz).reshape(fwidth, half)
        return t, swap(t, "xl")

    gdo, gdr = gather_hidden(gate_delta)
    udo, udr = gather_hidden(up_delta)
    hio, hir = gather_hidden(hidden)

    total_o = dot(gdo, wg, 0, 1) + dot(udo, wu, 0, 1)
    total_r = dot(gdr, wg, 0, 1) + dot(udr, wu, 0, 1)
    total_o = total_o.reshape(2, ny, rows, width)
    total_r = total_r.reshape(2, ny, rows, width)
    same = (xh ^ xl) == 0
    first = core == 0
    halves = jnp.stack([jnp.where(same, total_o, total_r), jnp.where(same, total_r, total_o)], axis=2)
    keep = jnp.where(first, halves[0], halves[1])
    send = jnp.where(first, halves[1], halves[0])
    total = (keep + swap(send, "core")).astype(BF16).reshape(2 * ny, rows, width)
    input_grad = lax.all_to_all(total, ("y", "xh"), 0, 0, tiled=True).astype(F32).sum(0).astype(BF16)

    down_grad = (dot(hio, co, 1, 0) + dot(hir, cr, 1, 0)).astype(BF16)
    gate_grad = (dot(xo, gdo, 0, 1) + dot(xr, gdr, 0, 1)).astype(BF16)
    up_grad = (dot(xo, udo, 0, 1) + dot(xr, udr, 0, 1)).astype(BF16)
    return (input_grad, gate_grad, up_grad, down_grad)


def solution(mesh):
    nz, ny = mesh.shape["gx"] // 2, mesh.shape["gy"] // 4
    grid = Mesh(mesh.devices.reshape(nz, 2, ny, 2, 2), AXES)
    in_specs = (P(GY, GX), P(GX, GY), P(GX, GY), P(GY, GX), P(GY, GX))
    out_specs = (P(GY, GX), P(GX, GY), P(GX, GY), P(GY, GX))
    return jax.shard_map(
        lambda *args: per_device(nz, ny, *args),
        mesh=grid,
        in_specs=in_specs,
        out_specs=out_specs,
        check_vma=False,
    )
```

time: 617 us -> 243 us (0.39)
  waiting for transfers between devices: 573 us -> 67.8 us
  starting transfers between devices: 0.16 us -> 84 us
  blocking collectives: 0 us -> 36 us
  matrix products: 18.1 us -> 25.8 us
    psum x1 -> x0, waiting for transfers between devices: 287 us -> none  [per_device(): lax.psum((gate_part, upper_part, grad_part), 'gx')]
    all_gather x2, waiting for transfers between devices: 169 us -> 14.3 us  [gather_tokens(): return lax.all_gather(t, 'core', axis=0, tiled=True)]
    reduce_scatter x1 -> x0, waiting for transfers between devices: 115 us -> none  [per_device(): lax.psum_scatter(total + lax.dot_general(up_delta, up_weight, fcon, prefe...]
    ppermute x0 -> x11, starting transfers between devices: none -> 43.8 us  [the longest x9 35.5 us: swap(): return lax.ppermute(x, axis, [(0, 1), (1, 0)])]
    all_to_all x0 -> x7, starting transfers between devices: none -> 40.1 us  [the longest x3 18.9 us: sum_over_z(): lax.all_to_all(part, 'z', 0, 0, tiled=True).astype(F32).sum(0)]
    all_to_all x0 -> x2, blocking collectives: none -> 36 us  [spread(): lax.all_to_all(jnp.broadcast_to(x[None], (n,) + x.shape), axis, 0, 0, til...]
    ppermute x0 -> x11, waiting for transfers between devices: none -> 31.8 us  [the longest x9 30.5 us: swap(): return lax.ppermute(x, axis, [(0, 1), (1, 0)])]
    all_to_all x0 -> x7, waiting for transfers between devices: none -> 21.7 us  [the longest x3 12.1 us: sum_over_z(): lax.all_to_all(part, 'z', 0, 0, tiled=True).astype(F32).sum(0)]
  transfers between devices with their start and end apart: 4 -> 20, of which waited for: 4 -> 9; matrix products, arithmetic and copies ran while one was open for 2% -> 14% of each run, Pallas kernels for 0% -> 0%
where the time goes in v1:
time: 243 us; the launch traced here: 240 us
  starting transfers between devices  84 us (35%)
  waiting for transfers between devices  67.8 us (28%)
  blocking collectives  36 us (15%)
  matrix products  25.8 us (11%)
  between operations  14.5 us (6%)
  local copies, waits for them, and re-layouts  6.39 us (3%)
  other arithmetic  5.62 us (2%)
    all_to_all x2, blocking collectives, spread(): lax.all_to_all(jnp.broadcast_to(x[None], (n,) + x.shape), axis, 0, 0, til...  36 us
    ppermute x9, starting transfers between devices, swap(): return lax.ppermute(x, axis, [(0, 1), (1, 0)])  35.5 us
    ppermute x9, waiting for transfers between devices, swap(): return lax.ppermute(x, axis, [(0, 1), (1, 0)])  30.5 us
    dot_general x16, matrix products, dot(): lax.dot_general(a, b, (((ca,), (cb,)), ((), ())), preferred_element_type=...  25.8 us
    all_to_all x3, starting transfers between devices, sum_over_z(): lax.all_to_all(part, 'z', 0, 0, tiled=True).astype(F32).sum(0)  18.9 us
    all_gather x2, waiting for transfers between devices, gather_tokens(): return lax.all_gather(t, 'core', axis=0, tiled=True)  14.3 us
    all_to_all x3, waiting for transfers between devices, sum_over_z(): lax.all_to_all(part, 'z', 0, 0, tiled=True).astype(F32).sum(0)  12.1 us
    all_to_all x3, starting transfers between devices, spread(): lax.all_to_all(jnp.broadcast_to(x[None], (n,) + x.shape), axis, 0, 0, til...  11.1 us
  transfers between devices with their start and end apart: 20, of which 9 were waited for; matrix products, arithmetic and copies ran while one was open for 14% of the time, Pallas kernels for 0%

profile of v1, /device:TPU:1, one launch (start us, length us, event | category | flops | bytes accessed | tf_op | source)
XLA Modules:
  0.0 240.0 jit_solution(10228540957585600334)
XLA Ops:
  9.4 7.6 %collective-permute-start.1 = (bf16[64,512]{1,0:T(8,128)(2,1)S(1)}, bf16[64,512]{1,0:T(8,128)(2,1)S(1)}, u32[]{:S(2)}, u32[]{:S(2)}) collective-permute-start(bf16[64,512]{1,0:T(8,128)(2,1)S(1)} %constant_dynamic-update-slice_fusion), channel_id=1, source_target_pairs={{32,0},{2,32},{34,2},{0,34},{33,1},{3,33},{35,3},{1,35},{36,4},{6,... | collective-permute-start | bytes 196616 | tf_op jit(solution)/shard_map/ppermute | solution.py:33
  18.4 21.3 %all_to_all.45 = bf16[8,32,1024]{2,1,0:T(8,128)(2,1)} all-to-all(bf16[8,32,1024]{2,1,0:T(8,128)(2,1)S(1)} %broadcast_in_dim.11), channel_id=1, replica_groups=mesh['z'=8,'xl'=2,'y'=8,'xh'=2,'core'=2] {'y'}, dimensions={0} | all-to-all | bytes 1048576 | tf_op jit(solution)/shard_map/all_to_all | solution.py:22
  40.6 3.5 %all-to-all-start = ((bf16[8,32,1024]{2,1,0:T(8,128)(2,1)}), bf16[8,32,1024]{2,1,0:T(8,128)(2,1)S(1)}, u32[]{:S(2)}, u32[]{:S(2)}) async-start(bf16[8,32,1024]{2,1,0:T(8,128)(2,1)} %broadcast_in_dim.10), calls=%async_computation | async-start | bytes 1048576 | tf_op jit(solution)/shard_map/all_to_all | solution.py:22
  47.1 14.2 %all-gather.5.cloned.1.call-done = bf16[512,1024]{1,0:T(8,128)(2,1)} async-done(((bf16[256,1024]{1,0:T(8,128)(2,1)}), bf16[512,1024]{1,0:T(8,128)(2,1)}) %all-gather.5.cloned.1.call-update) | async-done | bytes 1048592 | tf_op jit(solution)/shard_map/all_gather | solution.py:39
  64.3 6.2 %all-to-all-start.4 = ((f16[8,64,512]{2,1,0:T(8,128)(2,1)}), f16[8,64,512]{2,1,0:T(8,128)(2,1)S(1)}, u32[]{:S(2)}, u32[]{:S(2)}) async-start(f16[8,64,512]{2,1,0:T(8,128)(2,1)} %bitcast.7), calls=%async_computation.4 | async-start | bytes 1048576 | tf_op jit(solution)/shard_map/all_to_all | solution.py:48
  70.6 3.1 %collective-permute-start.3 = (bf16[512,512]{1,0:T(8,128)(2,1)S(1)}, bf16[512,512]{1,0:T(8,128)(2,1)}, u32[]{:S(2)}, u32[]{:S(2)}) collective-permute-start(bf16[512,512]{1,0:T(8,128)(2,1)S(1)} %copy-done.4), channel_id=1, source_target_pairs={{0,32},{32,0},{1,33},{33,1},{2,34},{34,2},{3,35},{35,3},{4,36},{36... | collective-permute-start | bytes 1572872 | tf_op jit(solution)/shard_map/ppermute | solution.py:18
  74.2 9.5 %collective-permute-done.3 = bf16[512,512]{1,0:T(8,128)(2,1)} collective-permute-done((bf16[512,512]{1,0:T(8,128)(2,1)S(1)}, bf16[512,512]{1,0:T(8,128)(2,1)}, u32[]{:S(2)}, u32[]{:S(2)}) %collective-permute-start.3) | collective-permute-done | bytes 524320 | tf_op jit(solution)/shard_map/ppermute | solution.py:18
  86.0 6.3 %all-to-all-start.3 = ((f16[8,64,512]{2,1,0:T(8,128)(2,1)}), f16[8,64,512]{2,1,0:T(8,128)(2,1)S(1)}, u32[]{:S(2)}, u32[]{:S(2)}) async-start(f16[8,64,512]{2,1,0:T(8,128)(2,1)} %bitcast.5), calls=%async_computation.3 | async-start | bytes 1048576 | tf_op jit(solution)/shard_map/all_to_all | solution.py:48
  92.3 3.2 %collective-permute-start.2 = (bf16[512,512]{1,0:T(8,128)(2,1)}, bf16[512,512]{1,0:T(8,128)(2,1)}, u32[]{:S(2)}, u32[]{:S(2)}) collective-permute-start(bf16[512,512]{1,0:T(8,128)(2,1)} %param.8), channel_id=1, source_target_pairs={{0,32},{32,0},{1,33},{33,1},{2,34},{34,2},{3,35},{35,3},{4,36},{36... | collective-permute-start | bytes 1572872 | tf_op jit(solution)/shard_map/ppermute | solution.py:18
  97.3 6.8 %collective-permute-done.2 = bf16[512,512]{1,0:T(8,128)(2,1)} collective-permute-done((bf16[512,512]{1,0:T(8,128)(2,1)}, bf16[512,512]{1,0:T(8,128)(2,1)}, u32[]{:S(2)}, u32[]{:S(2)}) %collective-permute-start.2) | collective-permute-done | bytes 524320 | tf_op jit(solution)/shard_map/ppermute | solution.py:18
  106.5 6.4 %all-to-all-start.1 = ((f16[8,64,512]{2,1,0:T(8,128)(2,1)}), f16[8,64,512]{2,1,0:T(8,128)(2,1)}, u32[]{:S(2)}, u32[]{:S(2)}) async-start(f16[8,64,512]{2,1,0:T(8,128)(2,1)} %bitcast.2), calls=%async_computation.1 | async-start | bytes 1048576 | tf_op jit(solution)/shard_map/all_to_all | solution.py:48
  113.0 12.1 %all-to-all-done.1 = f16[8,64,512]{2,1,0:T(8,128)(2,1)} async-done(((f16[8,64,512]{2,1,0:T(8,128)(2,1)}), f16[8,64,512]{2,1,0:T(8,128)(2,1)}, u32[]{:S(2)}, u32[]{:S(2)}) %all-to-all-start.1) | async-done | bytes 524320 | tf_op jit(solution)/shard_map/all_to_all | solution.py:48
  126.4 14.7 %all_to_all.46 = bf16[8,64,512]{2,1,0:T(8,128)(2,1)S(1)} all-to-all(bf16[8,64,512]{2,1,0:T(8,128)(2,1)S(1)} %broadcast_in_dim.13), channel_id=1, replica_groups=mesh['z'=8,'xl'=2,'y'=8,'xh'=2,'core'=2] {'z'}, dimensions={0} | all-to-all | bytes 1048576 | tf_op jit(solution)/shard_map/all_to_all | solution.py:22
  142.0 3.5 %all-to-all-start.5 = ((bf16[8,64,512]{2,1,0:T(8,128)(2,1)}), bf16[8,64,512]{2,1,0:T(8,128)(2,1)S(1)}, u32[]{:S(2)}, u32[]{:S(2)}) async-start(bf16[8,64,512]{2,1,0:T(8,128)(2,1)} %broadcast_in_dim.12), calls=%async_computation.5 | async-start | bytes 1048576 | tf_op jit(solution)/shard_map/all_to_all | solution.py:22
  145.5 3.3 %collective-permute-start.6 = (bf16[512,512]{1,0:T(8,128)(2,1)S(1)}, bf16[512,512]{1,0:T(8,128)(2,1)}, u32[]{:S(2)}, u32[]{:S(2)}) collective-permute-start(bf16[512,512]{1,0:T(8,128)(2,1)S(1)} %bitcast.54), channel_id=1, source_target_pairs={{0,32},{32,0},{1,33},{33,1},{2,34},{34,2},{3,35},{35,3},{4,36},{36... | collective-permute-start | bytes 1572872 | tf_op jit(solution)/shard_map/ppermute | solution.py:18
  148.8 8.9 %all-to-all-done.5 = bf16[8,64,512]{2,1,0:T(8,128)(2,1)S(1)} async-done(((bf16[8,64,512]{2,1,0:T(8,128)(2,1)}), bf16[8,64,512]{2,1,0:T(8,128)(2,1)S(1)}, u32[]{:S(2)}, u32[]{:S(2)}) %all-to-all-start.5) | async-done | bytes 524320 | tf_op jit(solution)/shard_map/all_to_all | solution.py:22
  158.6 4.1 %all-to-all-start.8 = ((bf16[8,64,512]{2,1,0:T(8,128)(2,1)}), bf16[8,64,512]{2,1,0:T(8,128)(2,1)}, u32[]{:S(2)}, u32[]{:S(2)}) async-start(bf16[8,64,512]{2,1,0:T(8,128)(2,1)} %broadcast_in_dim.14), calls=%async_computation.8 | async-start | bytes 1048576 | tf_op jit(solution)/shard_map/all_to_all | solution.py:22
  162.8 3.3 %collective-permute-start.5 = (bf16[512,512]{1,0:T(8,128)(2,1)S(1)}, bf16[512,512]{1,0:T(8,128)(2,1)S(1)}, u32[]{:S(2)}, u32[]{:S(2)}) collective-permute-start(bf16[512,512]{1,0:T(8,128)(2,1)S(1)} %bitcast.57), channel_id=1, source_target_pairs={{0,32},{32,0},{1,33},{33,1},{2,34},{34,2},{3,35},{35,3},{4,36},{36... | collective-permute-start | bytes 1572872 | tf_op jit(solution)/shard_map/ppermute | solution.py:18
  168.6 4.0 %collective-permute-done.5 = bf16[512,512]{1,0:T(8,128)(2,1)S(1)} collective-permute-done((bf16[512,512]{1,0:T(8,128)(2,1)S(1)}, bf16[512,512]{1,0:T(8,128)(2,1)S(1)}, u32[]{:S(2)}, u32[]{:S(2)}) %collective-permute-start.5) | collective-permute-done | bytes 524320 | tf_op jit(solution)/shard_map/ppermute | solution.py:18
  174.7 11.0 %collective-permute-start.7 = (f32[8,2,32,512]{3,2,1,0:T(8,128)}, f32[8,2,32,512]{3,2,1,0:T(8,128)}, u32[]{:S(2)}, u32[]{:S(2)}) collective-permute-start(f32[8,2,32,512]{3,2,1,0:T(8,128)} %select_bitcast_fusion), channel_id=1, source_target_pairs={{0,1},{1,0},{2,3},{3,2},{4,5},{5,4},{6,7},{7,6},{8,9},{9,8},{10,11... | collective-permute-start | bytes 3145736 | tf_op jit(solution)/shard_map/ppermute | solution.py:18
  186.5 3.3 %collective-permute-start.8 = (bf16[512,512]{1,0:T(8,128)(2,1)}, bf16[512,512]{1,0:T(8,128)(2,1)}, u32[]{:S(2)}, u32[]{:S(2)}) collective-permute-start(bf16[512,512]{1,0:T(8,128)(2,1)} %slice.39), channel_id=1, source_target_pairs={{0,32},{32,0},{1,33},{33,1},{2,34},{34,2},{3,35},{35,3},{4,36},{36... | collective-permute-start | bytes 1572872 | tf_op jit(solution)/shard_map/ppermute | solution.py:18
  192.7 3.4 %collective-permute-start.9 = (bf16[512,512]{1,0:T(8,128)(2,1)}, bf16[512,512]{1,0:T(8,128)(2,1)}, u32[]{:S(2)}, u32[]{:S(2)}) collective-permute-start(bf16[512,512]{1,0:T(8,128)(2,1)} %bitcast.17), channel_id=1, source_target_pairs={{0,32},{32,0},{1,33},{33,1},{2,34},{34,2},{3,35},{35,3},{4,36},{36... | collective-permute-start | bytes 1572872 | tf_op jit(solution)/shard_map/ppermute | solution.py:18
  202.5 10.1 %all-to-all-start.7 = ((bf16[16,32,512]{2,1,0:T(8,128)(2,1)}), bf16[16,32,512]{2,1,0:T(8,128)(2,1)S(1)}, u32[]{:S(2)}, u32[]{:S(2)}) async-start(bf16[16,32,512]{2,1,0:T(8,128)(2,1)} %bitcast.62), calls=%async_computation.7 | async-start | bytes 1048576 | tf_op jit(solution)/shard_map/all_to_all | solution.py:78
  219.1 10.2 %collective-permute-done.9 = bf16[512,512]{1,0:T(8,128)(2,1)} collective-permute-done((bf16[512,512]{1,0:T(8,128)(2,1)}, bf16[512,512]{1,0:T(8,128)(2,1)}, u32[]{:S(2)}, u32[]{:S(2)}) %collective-permute-start.9) | collective-permute-done | bytes 524320 | tf_op jit(solution)/shard_map/ppermute | solution.py:18
  (85 shorter events, 45.5 us)
Async XLA Ops:
  7.2 54.2 %all-gather.5.cloned.1.call-start = ((), (), s32[]{:S(2)}) async-start(), calls=%async_computation.10 | async-start | bytes 1572864 | tf_op jit(solution)/shard_map/all_gather | solution.py:39
  8.7 8.3 %collective-permute-start = (bf16[64,512]{1,0:T(8,128)(2,1)S(1)}, bf16[64,512]{1,0:T(8,128)(2,1)S(1)}, u32[]{:S(2)}, u32[]{:S(2)}) collective-permute-start(bf16[64,512]{1,0:T(8,128)(2,1)S(1)} %constant_dynamic-update-slice_fusion), channel_id=1, source_target_pairs={{0,0},{34,32},{2,2},{32,34},{1,1},{35,33},{3,3},{33,35},{4,4},{38,... | collective-permute-start | bytes 196616 | tf_op jit(solution)/shard_map/ppermute | solution.py:32
  9.4 8.9 %collective-permute-start.1 = (bf16[64,512]{1,0:T(8,128)(2,1)S(1)}, bf16[64,512]{1,0:T(8,128)(2,1)S(1)}, u32[]{:S(2)}, u32[]{:S(2)}) collective-permute-start(bf16[64,512]{1,0:T(8,128)(2,1)S(1)} %constant_dynamic-update-slice_fusion), channel_id=1, source_target_pairs={{32,0},{2,32},{34,2},{0,34},{33,1},{3,33},{35,3},{1,35},{36,4},{6,... | collective-permute-start | bytes 196616 | tf_op jit(solution)/shard_map/ppermute | solution.py:33
  40.6 23.7 %all-to-all-start = ((bf16[8,32,1024]{2,1,0:T(8,128)(2,1)}), bf16[8,32,1024]{2,1,0:T(8,128)(2,1)S(1)}, u32[]{:S(2)}, u32[]{:S(2)}) async-start(bf16[8,32,1024]{2,1,0:T(8,128)(2,1)} %broadcast_in_dim.10), calls=%async_computation | async-start | bytes 1048576 | tf_op jit(solution)/shard_map/all_to_all | solution.py:22
  44.1 18.9 %collective-permute-start.4 = (bf16[512,512]{1,0:T(8,128)(2,1)S(1)}, bf16[512,512]{1,0:T(8,128)(2,1)S(1)}, u32[]{:S(2)}, u32[]{:S(2)}) collective-permute-start(bf16[512,512]{1,0:T(8,128)(2,1)S(1)} %copy-done.5), channel_id=1, source_target_pairs={{0,32},{32,0},{1,33},{33,1},{2,34},{34,2},{3,35},{35,3},{4,36},{36... | collective-permute-start | bytes 1572872 | tf_op jit(solution)/shard_map/ppermute | solution.py:18
  64.3 9.4 %copy-start.12 = (bf16[8,32,1024]{2,1,0:T(8,128)(2,1)}, bf16[8,32,1024]{2,1,0:T(8,128)(2,1)S(1)}, u32[]{:S(2)}) copy-start(bf16[8,32,1024]{2,1,0:T(8,128)(2,1)S(1)} %all-to-all-done) | copy-start | bytes 1572868
  64.3 21.7 %all-to-all-start.4 = ((f16[8,64,512]{2,1,0:T(8,128)(2,1)}), f16[8,64,512]{2,1,0:T(8,128)(2,1)S(1)}, u32[]{:S(2)}, u32[]{:S(2)}) async-start(f16[8,64,512]{2,1,0:T(8,128)(2,1)} %bitcast.7), calls=%async_computation.4 | async-start | bytes 1048576 | tf_op jit(solution)/shard_map/all_to_all | solution.py:48
  70.5 25.1 %all-gather.3.cloned.1.call-start = ((), (), s32[]{:S(2)}) async-start(), calls=%async_computation.9 | async-start | bytes 1572864 | tf_op jit(solution)/shard_map/all_gather | solution.py:39
  70.6 13.1 %collective-permute-start.3 = (bf16[512,512]{1,0:T(8,128)(2,1)S(1)}, bf16[512,512]{1,0:T(8,128)(2,1)}, u32[]{:S(2)}, u32[]{:S(2)}) collective-permute-start(bf16[512,512]{1,0:T(8,128)(2,1)S(1)} %copy-done.4), channel_id=1, source_target_pairs={{0,32},{32,0},{1,33},{33,1},{2,34},{34,2},{3,35},{35,3},{4,36},{36... | collective-permute-start | bytes 1572872 | tf_op jit(solution)/shard_map/ppermute | solution.py:18
  86.0 20.5 %all-to-all-start.3 = ((f16[8,64,512]{2,1,0:T(8,128)(2,1)}), f16[8,64,512]{2,1,0:T(8,128)(2,1)S(1)}, u32[]{:S(2)}, u32[]{:S(2)}) async-start(f16[8,64,512]{2,1,0:T(8,128)(2,1)} %bitcast.5), calls=%async_computation.3 | async-start | bytes 1048576 | tf_op jit(solution)/shard_map/all_to_all | solution.py:48
  92.3 11.8 %collective-permute-start.2 = (bf16[512,512]{1,0:T(8,128)(2,1)}, bf16[512,512]{1,0:T(8,128)(2,1)}, u32[]{:S(2)}, u32[]{:S(2)}) collective-permute-start(bf16[512,512]{1,0:T(8,128)(2,1)} %param.8), channel_id=1, source_target_pairs={{0,32},{32,0},{1,33},{33,1},{2,34},{34,2},{3,35},{35,3},{4,36},{36... | collective-permute-start | bytes 1572872 | tf_op jit(solution)/shard_map/ppermute | solution.py:18
  106.5 18.6 %all-to-all-start.1 = ((f16[8,64,512]{2,1,0:T(8,128)(2,1)}), f16[8,64,512]{2,1,0:T(8,128)(2,1)}, u32[]{:S(2)}, u32[]{:S(2)}) async-start(f16[8,64,512]{2,1,0:T(8,128)(2,1)} %bitcast.2), calls=%async_computation.1 | async-start | bytes 1048576 | tf_op jit(solution)/shard_map/all_to_all | solution.py:48
  141.1 25.4 %copy-start.1 = (bf16[8,64,512]{2,1,0:T(8,128)(2,1)}, bf16[8,64,512]{2,1,0:T(8,128)(2,1)S(1)}, u32[]{:S(2)}) copy-start(bf16[8,64,512]{2,1,0:T(8,128)(2,1)S(1)} %all_to_all.46) | copy-start | bytes 1572868
  142.0 15.7 %all-to-all-start.5 = ((bf16[8,64,512]{2,1,0:T(8,128)(2,1)}), bf16[8,64,512]{2,1,0:T(8,128)(2,1)S(1)}, u32[]{:S(2)}, u32[]{:S(2)}) async-start(bf16[8,64,512]{2,1,0:T(8,128)(2,1)} %broadcast_in_dim.12), calls=%async_computation.5 | async-start | bytes 1048576 | tf_op jit(solution)/shard_map/all_to_all | solution.py:22
  145.5 21.5 %collective-permute-start.6 = (bf16[512,512]{1,0:T(8,128)(2,1)S(1)}, bf16[512,512]{1,0:T(8,128)(2,1)}, u32[]{:S(2)}, u32[]{:S(2)}) collective-permute-start(bf16[512,512]{1,0:T(8,128)(2,1)S(1)} %bitcast.54), channel_id=1, source_target_pairs={{0,32},{32,0},{1,33},{33,1},{2,34},{34,2},{3,35},{35,3},{4,36},{36... | collective-permute-start | bytes 1572872 | tf_op jit(solution)/shard_map/ppermute | solution.py:18
  158.6 34.1 %all-to-all-start.8 = ((bf16[8,64,512]{2,1,0:T(8,128)(2,1)}), bf16[8,64,512]{2,1,0:T(8,128)(2,1)}, u32[]{:S(2)}, u32[]{:S(2)}) async-start(bf16[8,64,512]{2,1,0:T(8,128)(2,1)} %broadcast_in_dim.14), calls=%async_computation.8 | async-start | bytes 1048576 | tf_op jit(solution)/shard_map/all_to_all | solution.py:22
  162.8 9.9 %collective-permute-start.5 = (bf16[512,512]{1,0:T(8,128)(2,1)S(1)}, bf16[512,512]{1,0:T(8,128)(2,1)S(1)}, u32[]{:S(2)}, u32[]{:S(2)}) collective-permute-start(bf16[512,512]{1,0:T(8,128)(2,1)S(1)} %bitcast.57), channel_id=1, source_target_pairs={{0,32},{32,0},{1,33},{33,1},{2,34},{34,2},{3,35},{35,3},{4,36},{36... | collective-permute-start | bytes 1572872 | tf_op jit(solution)/shard_map/ppermute | solution.py:18
  174.7 15.1 %copy-start.10 = (bf16[512,1024]{1,0:T(8,128)(2,1)S(1)}, bf16[512,1024]{1,0:T(8,128)(2,1)}, u32[]{:S(2)}) copy-start(bf16[512,1024]{1,0:T(8,128)(2,1)} %all-gather.3.cloned.1.call-done) | copy-start | bytes 3145732
  174.7 25.5 %collective-permute-start.7 = (f32[8,2,32,512]{3,2,1,0:T(8,128)}, f32[8,2,32,512]{3,2,1,0:T(8,128)}, u32[]{:S(2)}, u32[]{:S(2)}) collective-permute-start(f32[8,2,32,512]{3,2,1,0:T(8,128)} %select_bitcast_fusion), channel_id=1, source_target_pairs={{0,1},{1,0},{2,3},{3,2},{4,5},{5,4},{6,7},{7,6},{8,9},{9,8},{10,11... | collective-permute-start | bytes 3145736 | tf_op jit(solution)/shard_map/ppermute | solution.py:18
  186.5 27.7 %collective-permute-start.8 = (bf16[512,512]{1,0:T(8,128)(2,1)}, bf16[512,512]{1,0:T(8,128)(2,1)}, u32[]{:S(2)}, u32[]{:S(2)}) collective-permute-start(bf16[512,512]{1,0:T(8,128)(2,1)} %slice.39), channel_id=1, source_target_pairs={{0,32},{32,0},{1,33},{33,1},{2,34},{34,2},{3,35},{35,3},{4,36},{36... | collective-permute-start | bytes 1572872 | tf_op jit(solution)/shard_map/ppermute | solution.py:18
  190.7 28.5 %collective-permute-start.10 = (bf16[512,512]{1,0:T(8,128)(2,1)}, bf16[512,512]{1,0:T(8,128)(2,1)}, u32[]{:S(2)}, u32[]{:S(2)}) collective-permute-start(bf16[512,512]{1,0:T(8,128)(2,1)} %slice.36), channel_id=1, source_target_pairs={{0,32},{32,0},{1,33},{33,1},{2,34},{34,2},{3,35},{35,3},{4,36},{36... | collective-permute-start | bytes 1572872 | tf_op jit(solution)/shard_map/ppermute | solution.py:18
  192.7 36.6 %collective-permute-start.9 = (bf16[512,512]{1,0:T(8,128)(2,1)}, bf16[512,512]{1,0:T(8,128)(2,1)}, u32[]{:S(2)}, u32[]{:S(2)}) collective-permute-start(bf16[512,512]{1,0:T(8,128)(2,1)} %bitcast.17), channel_id=1, source_target_pairs={{0,32},{32,0},{1,33},{33,1},{2,34},{34,2},{3,35},{35,3},{4,36},{36... | collective-permute-start | bytes 1572872 | tf_op jit(solution)/shard_map/ppermute | solution.py:18
  202.5 10.1 %copy-start.11 = (bf16[512,1024]{1,0:T(8,128)(2,1)S(1)}, bf16[512,1024]{1,0:T(8,128)(2,1)}, u32[]{:S(2)}) copy-start(bf16[512,1024]{1,0:T(8,128)(2,1)} %all-gather.3.cloned.1.call-done) | copy-start | bytes 3145732
  202.5 29.9 %all-to-all-start.7 = ((bf16[16,32,512]{2,1,0:T(8,128)(2,1)}), bf16[16,32,512]{2,1,0:T(8,128)(2,1)S(1)}, u32[]{:S(2)}, u32[]{:S(2)}) async-start(bf16[16,32,512]{2,1,0:T(8,128)(2,1)} %bitcast.62), calls=%async_computation.7 | async-start | bytes 1048576 | tf_op jit(solution)/shard_map/all_to_all | solution.py:78
  (11 other events, 49.1 us)
Sparse Core Ops, SparseCore 0:
  39.8 21.4 all-gather.4
  74.0 20.9 all-gather.2

commit v2 on v1

v2 whole, which is shorter than its diff:
```python
import jax
import jax.numpy as jnp
from jax import lax
from jax.sharding import Mesh
from jax.sharding import PartitionSpec as P

AXES = ("z", "xl", "y", "xh", "core")
GX, GY = ("z", "xl"), ("y", "xh", "core")
SCALE = 16.0
F32, BF16, F16 = jnp.float32, jnp.bfloat16, jnp.float16


def dot(a, b, ca, cb):
    return lax.dot_general(a, b, (((ca,), (cb,)), ((), ())), preferred_element_type=F32)


def swap(x, axis):
    return lax.ppermute(x, axis, [(0, 1), (1, 0)])


def tie(*arrays):
    return lax.optimization_barrier(arrays)


def turn(x, by):
    n = x.shape[0]
    return lax.dynamic_slice_in_dim(jnp.concatenate([x, x], axis=0), by, n, axis=0)


def per_device(nz, ny, x, wg, wu, wd, c):
    rows, width = x.shape
    fwidth = wg.shape[1]
    zf = fwidth // nz
    z = lax.axis_index("z")
    right = [(i, (i + 1) % nz) for i in range(nz)]
    left = [(i, (i - 1) % nz) for i in range(nz)]

    pair = jnp.concatenate([x, c], axis=1)
    pair = jnp.broadcast_to(pair[None], (2 * ny,) + pair.shape)
    pair = lax.all_to_all(pair, ("y", "xh"), 0, 0, tiled=True).reshape(2 * ny * rows, 2 * width)
    xs, cs = pair[:, :width], pair[:, width:]
    half = xs.shape[0]

    def by_z(*weights):
        return turn(jnp.stack([w.reshape(nz, zf, width) for w in weights], axis=1), z).reshape(nz, -1, width)

    wgu = by_z(wg.T, swap(wg, "core").T, wu.T, swap(wu, "core").T)
    wdd = by_z(wd, swap(wd, "core"))
    gu = (dot(wgu.reshape(-1, width), xs, 1, 1) * SCALE).reshape(nz, 4 * zf, half)
    hg = (dot(wdd.reshape(-1, width), cs, 1, 1) * SCALE).reshape(nz, 2 * zf, half)

    def part(k):
        return jnp.concatenate([gu[k], hg[k]], axis=0)

    far = nz // 2
    cut = 3 * zf
    r = lax.ppermute(part(far)[:cut].astype(F16), "z", right).astype(F32)
    l = lax.ppermute(part(far)[cut:].astype(F16), "z", left).astype(F32)
    r = jnp.pad(r, ((0, cut), (0, 0)))
    l = jnp.pad(l, ((cut, 0), (0, 0)))
    for k in range(far - 1, 0, -1):
        r = lax.ppermute((part(k) + r).astype(F16), "z", right).astype(F32)
        l = lax.ppermute((part(nz - k) + l).astype(F16), "z", left).astype(F32)
    total = part(0) + r + l
    total = (total + swap(total.astype(F16), "xl").astype(F32)) * (1.0 / SCALE)
    gate, upper, hidden_grad = total[: 2 * zf], total[2 * zf : 4 * zf], total[4 * zf :]

    sig = jax.nn.sigmoid(gate)
    hidden = (gate * sig * upper).astype(BF16)
    gate_delta = (hidden_grad * upper * sig * (1.0 + gate * (1.0 - sig))).astype(BF16)
    up_delta = (hidden_grad * gate * sig).astype(BF16)

    chunk = [None] * nz
    chunk[0] = jnp.concatenate([gate_delta, up_delta, hidden], axis=0)
    for k in range(1, far):
        chunk[nz - k] = lax.ppermute(chunk[(nz - k + 1) % nz], "z", right)
        chunk[k] = lax.ppermute(chunk[k - 1], "z", left)
    chunk[far] = jnp.concatenate(
        [
            lax.ppermute(chunk[far + 1][:cut], "z", right),
            lax.ppermute(chunk[far - 1][cut:], "z", left),
        ],
        axis=0,
    )
    total = jnp.zeros((half, width), F32)
    for k in [0] + [j for i in range(1, far) for j in (nz - i, i)] + [far]:
        total = total + dot(chunk[k][: 4 * zf], wgu[k], 0, 0)
    total = total.astype(BF16).reshape(2 * ny, rows, width)
    total, *chunk = tie(total, *chunk)
    input_grad = lax.all_to_all(total, ("y", "xh"), 0, 0, tiled=True).astype(F32).sum(0).astype(BF16)

    deltas = jnp.concatenate([t[: 4 * zf] for t in chunk], axis=0)
    hidden = jnp.concatenate([t[4 * zf :] for t in chunk], axis=0)

    def both_cores(grads, n):
        grads = grads.reshape(nz, n, 2, zf, width)
        grads = (grads[:, :, 0] + swap(grads[:, :, 1], "core")).astype(BF16)
        grads = turn(grads, (nz - z) % nz)
        return [grads[:, i].reshape(fwidth, width) for i in range(n)]

    gate_grad, up_grad = both_cores(dot(deltas, xs, 1, 0), 2)
    (down_grad,) = both_cores(dot(hidden, cs, 1, 0), 1)
    return (input_grad, gate_grad.T, up_grad.T, down_grad)


def solution(mesh):
    nz, ny = mesh.shape["gx"] // 2, mesh.shape["gy"] // 4
    grid = Mesh(mesh.devices.reshape(nz, 2, ny, 2, 2), AXES)
    in_specs = (P(GY, GX), P(GX, GY), P(GX, GY), P(GY, GX), P(GY, GX))
    out_specs = (P(GY, GX), P(GX, GY), P(GX, GY), P(GY, GX))
    return jax.shard_map(
        lambda *args: per_device(nz, ny, *args),
        mesh=grid,
        in_specs=in_specs,
        out_specs=out_specs,
        check_vma=False,
    )
```

time: 243 us -> 211 us (0.87)
  blocking collectives: 36 us -> 0 us
  starting transfers between devices: 84 us -> 103 us
  matrix products: 25.8 us -> 9.26 us
  between operations: 14.5 us -> 1.33 us
  other arithmetic: 5.62 us -> 13.7 us
  local copies, waits for them, and re-layouts: 6.39 us -> 11.9 us
    ppermute x2 -> x16, starting transfers between devices: 8.24 us -> 61.1 us  [the longest x3 15.6 us: per_device(): chunk[k] = lax.ppermute(chunk[k - 1], 'z', left)]
    all_to_all x2 -> x0, blocking collectives: 36 us -> none  [spread(): lax.all_to_all(jnp.broadcast_to(x[None], (n,) + x.shape), axis, 0, 0, til...]
    ppermute x2 -> x16, waiting for transfers between devices: 1.29 us -> 35.7 us  [the longest x3 12 us: per_device(): chunk[k] = lax.ppermute(chunk[k - 1], 'z', left)]
    ppermute x9 -> x6, waiting for transfers between devices: 30.5 us -> 6.29 us  [swap(): return lax.ppermute(x, axis, [(0, 1), (1, 0)])]
    all_to_all x6 -> x1, starting transfers between devices: 30.1 us -> 10.2 us  [per_device(): lax.all_to_all(pair, ('y', 'xh'), 0, 0, tiled=True)]
    all_to_all x1, waiting for transfers between devices: 0.69 us -> 17.3 us  [per_device(): lax.all_to_all(total, ('y', 'xh'), 0, 0, tiled=True).astype(F32).sum(0)]
    dot_general x16 -> x12, matrix products: 25.8 us -> 9.26 us  [dot(): lax.dot_general(a, b, (((ca,), (cb,)), ((), ())), preferred_element_type=...]
    all_gather x2 -> x0, waiting for transfers between devices: 14.3 us -> none  [gather_tokens(): return lax.all_gather(t, 'core', axis=0, tiled=True)]
  transfers between devices with their start and end apart: 20 -> 24, of which waited for: 9 -> 12; matrix products, arithmetic and copies ran while one was open for 14% -> 8% of each run, Pallas kernels for 0% -> 0%
where the time goes in v2:
time: 211 us; the launch traced here: 210 us
  starting transfers between devices  103 us (49%)
  waiting for transfers between devices  70.2 us (33%)
  other arithmetic  13.7 us (6%)
  local copies, waits for them, and re-layouts  11.9 us (6%)
  matrix products  9.26 us (4%)
    ppermute x6, starting transfers between devices, swap(): return lax.ppermute(x, axis, [(0, 1), (1, 0)])  27.9 us
    all_to_all x1, waiting for transfers between devices, per_device(): lax.all_to_all(total, ('y', 'xh'), 0, 0, tiled=True).astype(F32).sum(0)  17.3 us
    ppermute x3, starting transfers between devices, per_device(): chunk[k] = lax.ppermute(chunk[k - 1], 'z', left)  15.6 us
    ppermute x3, starting transfers between devices, per_device(): l = lax.ppermute((part(nz - k) + l).astype(F16), 'z', left).astype(F32)  14 us
    ppermute x3, waiting for transfers between devices, per_device(): chunk[k] = lax.ppermute(chunk[k - 1], 'z', left)  12 us
    ppermute x3, waiting for transfers between devices, per_device(): r = lax.ppermute((part(k) + r).astype(F16), 'z', right).astype(F32)  11.2 us
    all_to_all x1, waiting for transfers between devices, per_device(): lax.all_to_all(pair, ('y', 'xh'), 0, 0, tiled=True)  10.9 us
    ppermute x1, starting transfers between devices, per_device(): l = lax.ppermute(part(far)[cut:].astype(F16), 'z', left).astype(F32)  10.7 us
  transfers between devices with their start and end apart: 24, of which 12 were waited for; matrix products, arithmetic and copies ran while one was open for 8% of the time, Pallas kernels for 0%

profile of v2, /device:TPU:1, one launch (start us, length us, event | category | flops | bytes accessed | tf_op | source)
XLA Modules:
  0.0 209.6 jit_solution(12793671703786540758)
XLA Ops:
  2.6 10.2 %all-to-all-start = ((bf16[16,32,1024]{2,1,0:T(8,128)(2,1)}), bf16[16,32,1024]{2,1,0:T(8,128)(2,1)S(1)}, u32[]{:S(2)}, u32[]{:S(2)}) async-start(bf16[16,32,1024]{2,1,0:T(8,128)(2,1)} %broadcast_in_dim.2), calls=%async_computation | async-start | bytes 2097152 | tf_op jit(solution)/shard_map/all_to_all | solution.py:40
  13.1 2.9 %collective-permute-start.1 = (bf16[512,512]{0,1:T(8,128)(2,1)S(1)}, bf16[512,512]{0,1:T(8,128)(2,1)S(1)}, u32[]{:S(2)}, u32[]{:S(2)}) collective-permute-start(bf16[512,512]{0,1:T(8,128)(2,1)S(1)} %copy.15), channel_id=1, source_target_pairs={{0,1},{1,0},{2,3},{3,2},{4,5},{5,4},{6,7},{7,6},{8,9},{9,8},{10,11... | collective-permute-start | bytes 1572872 | tf_op jit(solution)/shard_map/ppermute | solution.py:18
  21.5 3.0 %fusion.3 = bf16[8,4,64,512]{3,2,0,1:T(8,128)(2,1)S(1)} fusion(s32[]{:T(128)S(6)} %select_n.17, bf16[8,1,64,512]{3,2,0,1:T(8,128)(2,1)} %bitcast.76, bf16[8,1,64,512]{3,2,0,1:T(8,128)(2,1)} %bitcast.88, bf16[8,1,64,512]{3,2,0,1:T(8,128)(2,1)} %bitcast.75, bf16[8,1,64,512]{3,2,0,1:T(8,128)(2,1)} %bitcast.87), kind=kLoop, calls=%fused_computation.12 | loop fusion | flops 7340032 | bytes 4194308 | tf_op jit(solution)/shard_map/concatenate | solution.py:27
  28.7 10.9 %all-to-all-done = bf16[16,32,1024]{2,1,0:T(8,128)(2,1)S(1)} async-done(((bf16[16,32,1024]{2,1,0:T(8,128)(2,1)}), bf16[16,32,1024]{2,1,0:T(8,128)(2,1)S(1)}, u32[]{:S(2)}, u32[]{:S(2)}) %all-to-all-start) | async-done | bytes 1048608 | tf_op jit(solution)/shard_map/all_to_all | solution.py:40
  39.6 3.0 %fusion.55 = (f16[2048,512]{1,0:T(8,128)(2,1)S(1)}, f32[2048,512]{1,0:T(8,128)S(1)}) fusion(bf16[2048,512]{1,0:T(8,128)(2,1)} %bitcast.67, bf16[512,1024]{1,0:T(8,128)(2,1)S(1)} %bitcast.68), kind=kOutput, calls=%fused_computation.114 | convolution fusion | flops 1075838976 | bytes 8912896 | tf_op jit(solution)/shard_map/dot_general | solution.py:14
  43.7 10.7 %collective-permute-start.7 = (f16[192,512]{1,0:T(8,128)(2,1)S(1)}, f16[192,512]{1,0:T(8,128)(2,1)S(1)}, u32[]{:S(2)}, u32[]{:S(2)}) collective-permute-start(f16[192,512]{1,0:T(8,128)(2,1)S(1)} %pad_maximum_fusion.1), channel_id=1, source_target_pairs={{0,448},{64,0},{128,64},{192,128},{256,192},{320,256},{384,320},{4... | collective-permute-start | bytes 589832 | tf_op jit(solution)/shard_map/ppermute | solution.py:58
  56.9 5.1 %collective-permute-done.3 = f16[192,512]{1,0:T(8,128)(2,1)S(1)} collective-permute-done((f16[192,512]{1,0:T(8,128)(2,1)S(1)}, f16[192,512]{1,0:T(8,128)(2,1)S(1)}, u32[]{:S(2)}, u32[]{:S(2)}) %collective-permute-start.3) | collective-permute-done | bytes 196640 | tf_op jit(solution)/shard_map/ppermute | solution.py:57
  64.2 4.6 %collective-permute-start.8 = (f16[384,512]{1,0:T(8,128)(2,1)S(1)}, f16[384,512]{1,0:T(8,128)(2,1)S(1)}, u32[]{:S(2)}, u32[]{:S(2)}) collective-permute-start(f16[384,512]{1,0:T(8,128)(2,1)S(1)} %fusion.25), channel_id=1, source_target_pairs={{0,448},{64,0},{128,64},{192,128},{256,192},{320,256},{384,320},{4... | collective-permute-start | bytes 1179656 | tf_op jit(solution)/shard_map/ppermute | solution.py:63
  68.8 3.1 %collective-permute-done.4 = f16[384,512]{1,0:T(8,128)(2,1)S(1)} collective-permute-done((f16[384,512]{1,0:T(8,128)(2,1)S(1)}, f16[384,512]{1,0:T(8,128)(2,1)S(1)}, u32[]{:S(2)}, u32[]{:S(2)}) %collective-permute-start.4) | collective-permute-done | bytes 393248 | tf_op jit(solution)/shard_map/ppermute | solution.py:62
  74.1 4.6 %collective-permute-start.9 = (f16[384,512]{1,0:T(8,128)(2,1)S(1)}, f16[384,512]{1,0:T(8,128)(2,1)S(1)}, u32[]{:S(2)}, u32[]{:S(2)}) collective-permute-start(f16[384,512]{1,0:T(8,128)(2,1)S(1)} %fusion.24), channel_id=1, source_target_pairs={{0,448},{64,0},{128,64},{192,128},{256,192},{320,256},{384,320},{4... | collective-permute-start | bytes 1179656 | tf_op jit(solution)/shard_map/ppermute | solution.py:63
  78.7 3.6 %collective-permute-done.5 = f16[384,512]{1,0:T(8,128)(2,1)S(1)} collective-permute-done((f16[384,512]{1,0:T(8,128)(2,1)S(1)}, f16[384,512]{1,0:T(8,128)(2,1)S(1)}, u32[]{:S(2)}, u32[]{:S(2)}) %collective-permute-start.5) | collective-permute-done | bytes 393248 | tf_op jit(solution)/shard_map/ppermute | solution.py:62
  84.5 4.8 %collective-permute-start.10 = (f16[384,512]{1,0:T(8,128)(2,1)S(1)}, f16[384,512]{1,0:T(8,128)(2,1)S(1)}, u32[]{:S(2)}, u32[]{:S(2)}) collective-permute-start(f16[384,512]{1,0:T(8,128)(2,1)S(1)} %fusion.23), channel_id=1, source_target_pairs={{0,448},{64,0},{128,64},{192,128},{256,192},{320,256},{384,320},{4... | collective-permute-start | bytes 1179656 | tf_op jit(solution)/shard_map/ppermute | solution.py:63
  89.3 4.5 %collective-permute-done.6 = f16[384,512]{1,0:T(8,128)(2,1)S(1)} collective-permute-done((f16[384,512]{1,0:T(8,128)(2,1)S(1)}, f16[384,512]{1,0:T(8,128)(2,1)S(1)}, u32[]{:S(2)}, u32[]{:S(2)}) %collective-permute-start.6) | collective-permute-done | bytes 393248 | tf_op jit(solution)/shard_map/ppermute | solution.py:62
  98.4 6.3 %collective-permute-done.11 = f16[384,512]{1,0:T(8,128)(2,1)S(1)} collective-permute-done((f16[384,512]{1,0:T(8,128)(2,1)S(1)}, f16[384,512]{1,0:T(8,128)(2,1)S(1)}, u32[]{:S(2)}, u32[]{:S(2)}) %collective-permute-start.11) | collective-permute-done | bytes 393248 | tf_op jit(solution)/shard_map/ppermute | solution.py:18
  105.1 5.2 %collective-permute-start.13 = (bf16[384,512]{1,0:T(8,128)(2,1)S(1)}, bf16[384,512]{1,0:T(8,128)(2,1)S(1)}, u32[]{:S(2)}, u32[]{:S(2)}) collective-permute-start(bf16[384,512]{1,0:T(8,128)(2,1)S(1)} %pad_maximum_fusion), channel_id=1, source_target_pairs={{0,448},{64,0},{128,64},{192,128},{256,192},{320,256},{384,320},{4... | collective-permute-start | bytes 1179656 | tf_op jit(solution)/shard_map/ppermute | solution.py:77
  115.1 5.0 %collective-permute-start.15 = (bf16[384,512]{1,0:T(8,128)(2,1)S(1)}, bf16[384,512]{1,0:T(8,128)(2,1)S(1)}, u32[]{:S(2)}, u32[]{:S(2)}) collective-permute-start(bf16[384,512]{1,0:T(8,128)(2,1)S(1)} %collective-permute-done.13), channel_id=1, source_target_pairs={{0,448},{64,0},{128,64},{192,128},{256,192},{320,256},{384,320},{4... | collective-permute-start | bytes 1179656 | tf_op jit(solution)/shard_map/ppermute | solution.py:77
  122.7 5.3 %collective-permute-done.15 = bf16[384,512]{1,0:T(8,128)(2,1)S(1)} collective-permute-done((bf16[384,512]{1,0:T(8,128)(2,1)S(1)}, bf16[384,512]{1,0:T(8,128)(2,1)S(1)}, u32[]{:S(2)}, u32[]{:S(2)}) %collective-permute-start.15) | collective-permute-done | bytes 393248 | tf_op jit(solution)/shard_map/ppermute | solution.py:77
  128.0 5.3 %collective-permute-start.17 = (bf16[384,512]{1,0:T(8,128)(2,1)S(1)}, bf16[384,512]{1,0:T(8,128)(2,1)S(1)}, u32[]{:S(2)}, u32[]{:S(2)}) collective-permute-start(bf16[384,512]{1,0:T(8,128)(2,1)S(1)} %collective-permute-done.15), channel_id=1, source_target_pairs={{0,448},{64,0},{128,64},{192,128},{256,192},{320,256},{384,320},{4... | collective-permute-start | bytes 1179656 | tf_op jit(solution)/shard_map/ppermute | solution.py:77
  136.0 4.4 %collective-permute-done.17 = bf16[384,512]{1,0:T(8,128)(2,1)S(1)} collective-permute-done((bf16[384,512]{1,0:T(8,128)(2,1)S(1)}, bf16[384,512]{1,0:T(8,128)(2,1)S(1)}, u32[]{:S(2)}, u32[]{:S(2)}) %collective-permute-start.17) | collective-permute-done | bytes 393248 | tf_op jit(solution)/shard_map/ppermute | solution.py:77
  140.3 5.3 %collective-permute-start.19 = (bf16[192,512]{1,0:T(8,128)(2,1)S(1)}, bf16[192,512]{1,0:T(8,128)(2,1)S(1)}, u32[]{:S(2)}, u32[]{:S(2)}) collective-permute-start(bf16[192,512]{1,0:T(8,128)(2,1)S(1)} %slice.317), channel_id=1, source_target_pairs={{0,448},{64,0},{128,64},{192,128},{256,192},{320,256},{384,320},{4... | collective-permute-start | bytes 589832 | tf_op jit(solution)/shard_map/ppermute | solution.py:81
  148.1 5.2 %collective-permute-done.18 = bf16[192,512]{1,0:T(8,128)(2,1)S(1)} collective-permute-done((bf16[192,512]{1,0:T(8,128)(2,1)S(1)}, bf16[192,512]{1,0:T(8,128)(2,1)S(1)}, u32[]{:S(2)}, u32[]{:S(2)}) %collective-permute-start.18) | collective-permute-done | bytes 196640 | tf_op jit(solution)/shard_map/ppermute | solution.py:80
  160.2 16.5 %collective-permute-start.20 = (f32[8,2,64,512]{3,2,0,1:T(8,128)}, f32[8,2,64,512]{3,2,0,1:T(8,128)}, u32[]{:S(2)}, u32[]{:S(2)}) collective-permute-start(f32[8,2,64,512]{3,2,0,1:T(8,128)} %bitcast.65), channel_id=1, source_target_pairs={{0,1},{1,0},{2,3},{3,2},{4,5},{5,4},{6,7},{7,6},{8,9},{9,8},{10,11... | collective-permute-start | bytes 6291464 | tf_op jit(solution)/shard_map/ppermute | solution.py:18
  180.5 4.1 %all-to-all-start.1 = ((bf16[16,32,512]{2,1,0:T(8,128)(2,1)}), bf16[16,32,512]{2,1,0:T(8,128)(2,1)S(1)}, u32[]{:S(2)}, u32[]{:S(2)}) async-start(bf16[16,32,512]{2,1,0:T(8,128)(2,1)} %bitcast.21), calls=%async_computation.1 | async-start | bytes 1048576 | tf_op jit(solution)/shard_map/all_to_all | solution.py:90
  184.6 17.3 %all-to-all-done.1 = bf16[16,32,512]{2,1,0:T(8,128)(2,1)S(1)} async-done(((bf16[16,32,512]{2,1,0:T(8,128)(2,1)}), bf16[16,32,512]{2,1,0:T(8,128)(2,1)S(1)}, u32[]{:S(2)}, u32[]{:S(2)}) %all-to-all-start.1) | async-done | bytes 524320 | tf_op jit(solution)/shard_map/all_to_all | solution.py:90
  (106 shorter events, 57.3 us)
Async XLA Ops:
  2.6 37.0 %all-to-all-start = ((bf16[16,32,1024]{2,1,0:T(8,128)(2,1)}), bf16[16,32,1024]{2,1,0:T(8,128)(2,1)S(1)}, u32[]{:S(2)}, u32[]{:S(2)}) async-start(bf16[16,32,1024]{2,1,0:T(8,128)(2,1)} %broadcast_in_dim.2), calls=%async_computation | async-start | bytes 2097152 | tf_op jit(solution)/shard_map/all_to_all | solution.py:40
  13.1 7.5 %collective-permute-start.1 = (bf16[512,512]{0,1:T(8,128)(2,1)S(1)}, bf16[512,512]{0,1:T(8,128)(2,1)S(1)}, u32[]{:S(2)}, u32[]{:S(2)}) collective-permute-start(bf16[512,512]{0,1:T(8,128)(2,1)S(1)} %copy.15), channel_id=1, source_target_pairs={{0,1},{1,0},{2,3},{3,2},{4,5},{5,4},{6,7},{7,6},{8,9},{9,8},{10,11... | collective-permute-start | bytes 1572872 | tf_op jit(solution)/shard_map/ppermute | solution.py:18
  16.2 4.4 %collective-permute-start = (bf16[512,512]{0,1:T(8,128)(2,1)S(1)}, bf16[512,512]{0,1:T(8,128)(2,1)S(1)}, u32[]{:S(2)}, u32[]{:S(2)}) collective-permute-start(bf16[512,512]{0,1:T(8,128)(2,1)S(1)} %copy.13), channel_id=1, source_target_pairs={{0,1},{1,0},{2,3},{3,2},{4,5},{5,4},{6,7},{7,6},{8,9},{9,8},{10,11... | collective-permute-start | bytes 1572872 | tf_op jit(solution)/shard_map/ppermute | solution.py:18
  18.1 8.0 %collective-permute-start.2 = (bf16[512,512]{1,0:T(8,128)(2,1)}, bf16[512,512]{1,0:T(8,128)(2,1)}, u32[]{:S(2)}, u32[]{:S(2)}) collective-permute-start(bf16[512,512]{1,0:T(8,128)(2,1)} %param.8), channel_id=1, source_target_pairs={{0,1},{1,0},{2,3},{3,2},{4,5},{5,4},{6,7},{7,6},{8,9},{9,8},{10,11... | collective-permute-start | bytes 1572872 | tf_op jit(solution)/shard_map/ppermute | solution.py:18
  43.7 20.3 %collective-permute-start.7 = (f16[192,512]{1,0:T(8,128)(2,1)S(1)}, f16[192,512]{1,0:T(8,128)(2,1)S(1)}, u32[]{:S(2)}, u32[]{:S(2)}) collective-permute-start(f16[192,512]{1,0:T(8,128)(2,1)S(1)} %pad_maximum_fusion.1), channel_id=1, source_target_pairs={{0,448},{64,0},{128,64},{192,128},{256,192},{320,256},{384,320},{4... | collective-permute-start | bytes 589832 | tf_op jit(solution)/shard_map/ppermute | solution.py:58
  54.4 7.6 %collective-permute-start.3 = (f16[192,512]{1,0:T(8,128)(2,1)S(1)}, f16[192,512]{1,0:T(8,128)(2,1)S(1)}, u32[]{:S(2)}, u32[]{:S(2)}) collective-permute-start(f16[192,512]{1,0:T(8,128)(2,1)S(1)} %slice.291), channel_id=1, source_target_pairs={{0,64},{64,128},{128,192},{192,256},{256,320},{320,384},{384,448},... | collective-permute-start | bytes 589832 | tf_op jit(solution)/shard_map/ppermute | solution.py:57
  62.1 9.7 %collective-permute-start.4 = (f16[384,512]{1,0:T(8,128)(2,1)S(1)}, f16[384,512]{1,0:T(8,128)(2,1)S(1)}, u32[]{:S(2)}, u32[]{:S(2)}) collective-permute-start(f16[384,512]{1,0:T(8,128)(2,1)S(1)} %fusion.22), channel_id=1, source_target_pairs={{0,64},{64,128},{128,192},{192,256},{256,320},{320,384},{384,448},... | collective-permute-start | bytes 1179656 | tf_op jit(solution)/shard_map/ppermute | solution.py:62
  64.2 9.7 %collective-permute-start.8 = (f16[384,512]{1,0:T(8,128)(2,1)S(1)}, f16[384,512]{1,0:T(8,128)(2,1)S(1)}, u32[]{:S(2)}, u32[]{:S(2)}) collective-permute-start(f16[384,512]{1,0:T(8,128)(2,1)S(1)} %fusion.25), channel_id=1, source_target_pairs={{0,448},{64,0},{128,64},{192,128},{256,192},{320,256},{384,320},{4... | collective-permute-start | bytes 1179656 | tf_op jit(solution)/shard_map/ppermute | solution.py:63
  72.0 10.3 %collective-permute-start.5 = (f16[384,512]{1,0:T(8,128)(2,1)S(1)}, f16[384,512]{1,0:T(8,128)(2,1)S(1)}, u32[]{:S(2)}, u32[]{:S(2)}) collective-permute-start(f16[384,512]{1,0:T(8,128)(2,1)S(1)} %fusion.21), channel_id=1, source_target_pairs={{0,64},{64,128},{128,192},{192,256},{256,320},{320,384},{384,448},... | collective-permute-start | bytes 1179656 | tf_op jit(solution)/shard_map/ppermute | solution.py:62
  74.1 10.3 %collective-permute-start.9 = (f16[384,512]{1,0:T(8,128)(2,1)S(1)}, f16[384,512]{1,0:T(8,128)(2,1)S(1)}, u32[]{:S(2)}, u32[]{:S(2)}) collective-permute-start(f16[384,512]{1,0:T(8,128)(2,1)S(1)} %fusion.24), channel_id=1, source_target_pairs={{0,448},{64,0},{128,64},{192,128},{256,192},{320,256},{384,320},{4... | collective-permute-start | bytes 1179656 | tf_op jit(solution)/shard_map/ppermute | solution.py:63
  82.4 11.4 %collective-permute-start.6 = (f16[384,512]{1,0:T(8,128)(2,1)S(1)}, f16[384,512]{1,0:T(8,128)(2,1)S(1)}, u32[]{:S(2)}, u32[]{:S(2)}) collective-permute-start(f16[384,512]{1,0:T(8,128)(2,1)S(1)} %fusion.20), channel_id=1, source_target_pairs={{0,64},{64,128},{128,192},{192,256},{256,320},{320,384},{384,448},... | collective-permute-start | bytes 1179656 | tf_op jit(solution)/shard_map/ppermute | solution.py:62
  84.5 11.5 %collective-permute-start.10 = (f16[384,512]{1,0:T(8,128)(2,1)S(1)}, f16[384,512]{1,0:T(8,128)(2,1)S(1)}, u32[]{:S(2)}, u32[]{:S(2)}) collective-permute-start(f16[384,512]{1,0:T(8,128)(2,1)S(1)} %fusion.23), channel_id=1, source_target_pairs={{0,448},{64,0},{128,64},{192,128},{256,192},{320,256},{384,320},{4... | collective-permute-start | bytes 1179656 | tf_op jit(solution)/shard_map/ppermute | solution.py:63
  96.2 8.5 %collective-permute-start.11 = (f16[384,512]{1,0:T(8,128)(2,1)S(1)}, f16[384,512]{1,0:T(8,128)(2,1)S(1)}, u32[]{:S(2)}, u32[]{:S(2)}) collective-permute-start(f16[384,512]{1,0:T(8,128)(2,1)S(1)} %fusion.48), channel_id=1, source_target_pairs={{0,32},{32,0},{1,33},{33,1},{2,34},{34,2},{3,35},{35,3},{4,36},{36... | collective-permute-start | bytes 1179656 | tf_op jit(solution)/shard_map/ppermute | solution.py:18
  105.1 10.0 %collective-permute-start.13 = (bf16[384,512]{1,0:T(8,128)(2,1)S(1)}, bf16[384,512]{1,0:T(8,128)(2,1)S(1)}, u32[]{:S(2)}, u32[]{:S(2)}) collective-permute-start(bf16[384,512]{1,0:T(8,128)(2,1)S(1)} %pad_maximum_fusion), channel_id=1, source_target_pairs={{0,448},{64,0},{128,64},{192,128},{256,192},{320,256},{384,320},{4... | collective-permute-start | bytes 1179656 | tf_op jit(solution)/shard_map/ppermute | solution.py:77
  110.4 9.7 %collective-permute-start.12 = (bf16[384,512]{1,0:T(8,128)(2,1)S(1)}, bf16[384,512]{1,0:T(8,128)(2,1)S(1)}, u32[]{:S(2)}, u32[]{:S(2)}) collective-permute-start(bf16[384,512]{1,0:T(8,128)(2,1)S(1)} %pad_maximum_fusion), channel_id=1, source_target_pairs={{0,64},{64,128},{128,192},{192,256},{256,320},{320,384},{384,448},... | collective-permute-start | bytes 1179656 | tf_op jit(solution)/shard_map/ppermute | solution.py:76
  115.1 12.9 %collective-permute-start.15 = (bf16[384,512]{1,0:T(8,128)(2,1)S(1)}, bf16[384,512]{1,0:T(8,128)(2,1)S(1)}, u32[]{:S(2)}, u32[]{:S(2)}) collective-permute-start(bf16[384,512]{1,0:T(8,128)(2,1)S(1)} %collective-permute-done.13), channel_id=1, source_target_pairs={{0,448},{64,0},{128,64},{192,128},{256,192},{320,256},{384,320},{4... | collective-permute-start | bytes 1179656 | tf_op jit(solution)/shard_map/ppermute | solution.py:77
  120.1 13.2 %collective-permute-start.14 = (bf16[384,512]{1,0:T(8,128)(2,1)S(1)}, bf16[384,512]{1,0:T(8,128)(2,1)S(1)}, u32[]{:S(2)}, u32[]{:S(2)}) collective-permute-start(bf16[384,512]{1,0:T(8,128)(2,1)S(1)} %collective-permute-done.12), channel_id=1, source_target_pairs={{0,64},{64,128},{128,192},{192,256},{256,320},{320,384},{384,448},... | collective-permute-start | bytes 1179656 | tf_op jit(solution)/shard_map/ppermute | solution.py:76
  128.0 12.3 %collective-permute-start.17 = (bf16[384,512]{1,0:T(8,128)(2,1)S(1)}, bf16[384,512]{1,0:T(8,128)(2,1)S(1)}, u32[]{:S(2)}, u32[]{:S(2)}) collective-permute-start(bf16[384,512]{1,0:T(8,128)(2,1)S(1)} %collective-permute-done.15), channel_id=1, source_target_pairs={{0,448},{64,0},{128,64},{192,128},{256,192},{320,256},{384,320},{4... | collective-permute-start | bytes 1179656 | tf_op jit(solution)/shard_map/ppermute | solution.py:77
  133.3 12.3 %collective-permute-start.16 = (bf16[384,512]{1,0:T(8,128)(2,1)S(1)}, bf16[384,512]{1,0:T(8,128)(2,1)S(1)}, u32[]{:S(2)}, u32[]{:S(2)}) collective-permute-start(bf16[384,512]{1,0:T(8,128)(2,1)S(1)} %collective-permute-done.14), channel_id=1, source_target_pairs={{0,64},{64,128},{128,192},{192,256},{256,320},{320,384},{384,448},... | collective-permute-start | bytes 1179656 | tf_op jit(solution)/shard_map/ppermute | solution.py:76
  140.3 13.0 %collective-permute-start.19 = (bf16[192,512]{1,0:T(8,128)(2,1)S(1)}, bf16[192,512]{1,0:T(8,128)(2,1)S(1)}, u32[]{:S(2)}, u32[]{:S(2)}) collective-permute-start(bf16[192,512]{1,0:T(8,128)(2,1)S(1)} %slice.317), channel_id=1, source_target_pairs={{0,448},{64,0},{128,64},{192,128},{256,192},{320,256},{384,320},{4... | collective-permute-start | bytes 589832 | tf_op jit(solution)/shard_map/ppermute | solution.py:81
  145.7 7.6 %collective-permute-start.18 = (bf16[192,512]{1,0:T(8,128)(2,1)S(1)}, bf16[192,512]{1,0:T(8,128)(2,1)S(1)}, u32[]{:S(2)}, u32[]{:S(2)}) collective-permute-start(bf16[192,512]{1,0:T(8,128)(2,1)S(1)} %slice.316), channel_id=1, source_target_pairs={{0,64},{64,128},{128,192},{192,256},{256,320},{320,384},{384,448},... | collective-permute-start | bytes 589832 | tf_op jit(solution)/shard_map/ppermute | solution.py:80
  160.2 45.0 %collective-permute-start.20 = (f32[8,2,64,512]{3,2,0,1:T(8,128)}, f32[8,2,64,512]{3,2,0,1:T(8,128)}, u32[]{:S(2)}, u32[]{:S(2)}) collective-permute-start(f32[8,2,64,512]{3,2,0,1:T(8,128)} %bitcast.65), channel_id=1, source_target_pairs={{0,1},{1,0},{2,3},{3,2},{4,5},{5,4},{6,7},{7,6},{8,9},{9,8},{10,11... | collective-permute-start | bytes 6291464 | tf_op jit(solution)/shard_map/ppermute | solution.py:18
  178.6 24.1 %collective-permute-start.21 = (f32[8,1,64,512]{3,2,0,1:T(8,128)}, f32[8,1,64,512]{3,2,0,1:T(8,128)}, u32[]{:S(2)}, u32[]{:S(2)}) collective-permute-start(f32[8,1,64,512]{3,2,0,1:T(8,128)} %slice_bitcast_fusion), channel_id=1, source_target_pairs={{0,1},{1,0},{2,3},{3,2},{4,5},{5,4},{6,7},{7,6},{8,9},{9,8},{10,11... | collective-permute-start | bytes 3145736 | tf_op jit(solution)/shard_map/ppermute | solution.py:18
  180.5 21.5 %all-to-all-start.1 = ((bf16[16,32,512]{2,1,0:T(8,128)(2,1)}), bf16[16,32,512]{2,1,0:T(8,128)(2,1)S(1)}, u32[]{:S(2)}, u32[]{:S(2)}) async-start(bf16[16,32,512]{2,1,0:T(8,128)(2,1)} %bitcast.21), calls=%async_computation.1 | async-start | bytes 1048576 | tf_op jit(solution)/shard_map/all_to_all | solution.py:90
  (8 other events, 45.9 us)

commit v3 on v2

v3 whole, which is shorter than its diff:
```python
import functools

import jax
import jax.numpy as jnp
from jax import lax
from jax.experimental import pallas as pl
from jax.experimental.pallas import tpu as pltpu
from jax.sharding import Mesh
from jax.sharding import PartitionSpec as P

AXES = ("z", "xl", "y", "xh", "core")
GX, GY = ("z", "xl"), ("y", "xh", "core")
SCALE = 16.0
F32, BF16, F16 = jnp.float32, jnp.bfloat16, jnp.float16


def dot(a, b, ca, cb):
    return lax.dot_general(a, b, (((ca,), (cb,)), ((), ())), preferred_element_type=F32)


def swap(x, axis):
    return lax.ppermute(x, axis, [(0, 1), (1, 0)])


def tie(*arrays):
    return lax.optimization_barrier(arrays)


def turn(x, by):
    n = x.shape[0]
    return lax.dynamic_slice_in_dim(jnp.concatenate([x, x], axis=0), by, n, axis=0)


def grads_kernel(nz, zf, *refs):
    chunks, (x_ref, c_ref, own_ref, send_ref) = refs[:nz], refs[nz:]
    z = lax.axis_index("z")
    for k in range(nz):
        at = lax.rem(z + k, nz)
        gu = jnp.dot(chunks[k][: 4 * zf, :], x_ref[...], preferred_element_type=F32)
        dn = jnp.dot(chunks[k][4 * zf :, :], c_ref[...], preferred_element_type=F32)
        own_ref[at, : 2 * zf, :] = gu[: 2 * zf]
        own_ref[at, 2 * zf :, :] = dn[:zf]
        send_ref[at, : 2 * zf, :] = gu[2 * zf :].astype(BF16)
        send_ref[at, 2 * zf :, :] = dn[zf:].astype(BF16)


def weight_grads(chunks, xs, cs, zf):
    shape = (len(chunks), 3 * zf, xs.shape[1])
    return pl.pallas_call(
        functools.partial(grads_kernel, len(chunks), zf),
        out_shape=(jax.ShapeDtypeStruct(shape, F32), jax.ShapeDtypeStruct(shape, BF16)),
        compiler_params=pltpu.CompilerParams(vmem_limit_bytes=40 * 2**20),
    )(*chunks, xs, cs)


def finish_kernel(zf, own_ref, got_ref, gate_ref, up_ref, down_ref):
    both = (own_ref[...] + got_ref[...].astype(F32)).astype(BF16)
    gate_ref[...] = jnp.concatenate([both[0, :zf], both[1, :zf]], axis=0).T
    up_ref[...] = jnp.concatenate([both[0, zf : 2 * zf], both[1, zf : 2 * zf]], axis=0).T
    down_ref[...] = jnp.concatenate([both[0, 2 * zf :], both[1, 2 * zf :]], axis=0)


def finish(own, got):
    nz, n, width = own.shape
    zf = n // 3
    block = pl.BlockSpec((2, n, width), lambda i: (i, 0, 0))
    across = pl.BlockSpec((width, 2 * zf), lambda i: (0, i))
    return pl.pallas_call(
        functools.partial(finish_kernel, zf),
        grid=(nz // 2,),
        in_specs=[block, block],
        out_specs=[across, across, pl.BlockSpec((2 * zf, width), lambda i: (i, 0))],
        out_shape=[
            jax.ShapeDtypeStruct((width, nz * zf), BF16),
            jax.ShapeDtypeStruct((width, nz * zf), BF16),
            jax.ShapeDtypeStruct((nz * zf, width), BF16),
        ],
    )(own, got)


def per_device(nz, ny, x, wg, wu, wd, c):
    rows, width = x.shape
    fwidth = wg.shape[1]
    zf = fwidth // nz
    z = lax.axis_index("z")
    right = [(i, (i + 1) % nz) for i in range(nz)]
    left = [(i, (i - 1) % nz) for i in range(nz)]

    pair = jnp.concatenate([x, c], axis=1)
    pair = jnp.broadcast_to(pair[None], (ny,) + pair.shape)
    pair = lax.all_to_all(pair, "y", 0, 0, tiled=True).reshape(ny * rows, 2 * width)
    pair = jnp.concatenate([pair, swap(pair, "xh")], axis=0)
    xs, cs = pair[:, :width], pair[:, width:]
    half = xs.shape[0]

    def by_z(*weights):
        return turn(jnp.stack([w.reshape(nz, zf, width) for w in weights], axis=1), z).reshape(nz, -1, width)

    wgu = by_z(wg.T, wu.T, swap(wg, "core").T, swap(wu, "core").T)
    wdd = by_z(wd, swap(wd, "core"))
    far = nz // 2


    def part_far():
        return dot(wgu[far], xs, 1, 1) * SCALE, dot(wdd[far], cs, 1, 1) * SCALE

    gu = (dot(wgu.reshape(-1, width), xs, 1, 1) * SCALE).reshape(nz, 4 * zf, half)
    hg = (dot(wdd.reshape(-1, width), cs, 1, 1) * SCALE).reshape(nz, 2 * zf, half)

    def part(k):
        return jnp.concatenate([gu[k], hg[k]], axis=0)

    cut = 3 * zf
    first = jnp.concatenate(part_far(), axis=0).astype(F16)
    r = lax.ppermute(first[:cut], "z", right).astype(F32)
    l = lax.ppermute(first[cut:], "z", left).astype(F32)
    r = jnp.pad(r, ((0, cut), (0, 0)))
    l = jnp.pad(l, ((cut, 0), (0, 0)))
    for k in range(far - 1, 0, -1):
        r = lax.ppermute((part(k) + r).astype(F16), "z", right).astype(F32)
        l = lax.ppermute((part(nz - k) + l).astype(F16), "z", left).astype(F32)
    total = part(0) + r + l
    total = (total + swap(total.astype(F16), "xl").astype(F32)) * (1.0 / SCALE)
    gate_upper = total[: 4 * zf].reshape(2, 2, zf, half)
    gate, upper = gate_upper[:, 0], gate_upper[:, 1]
    hidden_grad = total[4 * zf :].reshape(2, zf, half)

    sig = jax.nn.sigmoid(gate)
    hidden = (gate * sig * upper).astype(BF16)
    gate_delta = (hidden_grad * upper * sig * (1.0 + gate * (1.0 - sig))).astype(BF16)
    up_delta = (hidden_grad * gate * sig).astype(BF16)

    chunk = [None] * nz
    deltas = jnp.stack([gate_delta, up_delta], axis=1).reshape(4 * zf, half)
    chunk[0] = jnp.concatenate([deltas, hidden.reshape(2 * zf, half)], axis=0)
    for k in range(1, far):
        chunk[nz - k] = lax.ppermute(chunk[(nz - k + 1) % nz], "z", right)
        chunk[k] = lax.ppermute(chunk[k - 1], "z", left)
    chunk[far] = jnp.concatenate(
        [
            lax.ppermute(chunk[far + 1][:cut], "z", right),
            lax.ppermute(chunk[far - 1][cut:], "z", left),
        ],
        axis=0,
    )
    total = jnp.zeros((half, width), F32)
    for k in [0] + [j for i in range(1, far) for j in (nz - i, i)] + [far]:
        total = total + dot(chunk[k][: 4 * zf], wgu[k], 0, 0)

    total, send, *chunk = tie(total[: half // 2], total[half // 2 :].astype(BF16), *chunk)
    got = swap(send, "xh")
    own, send = weight_grads(chunk, xs, cs, zf)
    got, own, send = tie(got, own, send)
    total = (total + got.astype(F32)).astype(BF16).reshape(ny, rows, width)
    recv = lax.all_to_all(total, "y", 0, 0, tiled=True)
    gate_grad, up_grad, down_grad = finish(own, swap(send, "core"))
    recv, gate_grad, up_grad, down_grad = tie(recv, gate_grad, up_grad, down_grad)
    input_grad = recv.astype(F32).sum(0).astype(BF16)
    return (input_grad, gate_grad, up_grad, down_grad)


def solution(mesh):
    nz, ny = mesh.shape["gx"] // 2, mesh.shape["gy"] // 4
    grid = Mesh(mesh.devices.reshape(nz, 2, ny, 2, 2), AXES)
    in_specs = (P(GY, GX), P(GX, GY), P(GX, GY), P(GY, GX), P(GY, GX))
    out_specs = (P(GY, GX), P(GX, GY), P(GX, GY), P(GY, GX))
    return jax.shard_map(
        lambda *args: per_device(nz, ny, *args),
        mesh=grid,
        in_specs=in_specs,
        out_specs=out_specs,
        check_vma=False,
    )
```

time: 211 us -> 197 us (0.934)
  waiting for transfers between devices: 70.2 us -> 57.1 us
  starting transfers between devices: 103 us -> 112 us
  other arithmetic: 13.7 us -> 7.41 us
  Pallas kernels: 0 us -> 6.04 us
  local copies, waits for them, and re-layouts: 11.9 us -> 6.91 us
  matrix products: 9.26 us -> 5.25 us
    all_to_all x2, waiting for transfers between devices: 28.2 us -> 12.2 us  [the longest x1 6.92 us: per_device(): recv = lax.all_to_all(total, 'y', 0, 0, tiled=True)]
    ppermute x6 -> x7, starting transfers between devices: 27.9 us -> 40 us  [swap(): return lax.ppermute(x, axis, [(0, 1), (1, 0)])]
    ppermute x3, waiting for transfers between devices: 0.02 us -> 10.1 us  [per_device(): chunk[nz - k] = lax.ppermute(chunk[(nz - k + 1) % nz], 'z', right)]
    ppermute x6 -> x7, waiting for transfers between devices: 6.29 us -> 12.5 us  [swap(): return lax.ppermute(x, axis, [(0, 1), (1, 0)])]
    ppermute x3, waiting for transfers between devices: 12 us -> 5.9 us  [per_device(): chunk[k] = lax.ppermute(chunk[k - 1], 'z', left)]
    pallas_call x0 -> x2, Pallas kernels: none -> 6.04 us  [the longest x1 4.24 us: finish(): pl.pallas_call(functools.partial(finish_kernel, zf), grid=(nz // 2,), in_...]
    ppermute x2, waiting for transfers between devices: 5.14 us -> 0.57 us  [the longest x1 0.57 us: per_device(): l = lax.ppermute(first[cut:], 'z', left).astype(F32)]
    dot_general x12, matrix products: 9.26 us -> 5.25 us  [dot(): lax.dot_general(a, b, (((ca,), (cb,)), ((), ())), preferred_element_type=...]
  transfers between devices with their start and end apart: 24 -> 25, of which waited for: 12 -> 15; matrix products, arithmetic and copies ran while one was open for 8% -> 5% of each run, Pallas kernels for 0% -> 3%
where the time goes in v3:
time: 197 us; the launch traced here: 196 us
  starting transfers between devices  112 us (57%)
  waiting for transfers between devices  57.1 us (29%)
  other arithmetic  7.41 us (4%)
  local copies, waits for them, and re-layouts  6.91 us (4%)
  Pallas kernels  6.04 us (3%)
  matrix products  5.25 us (3%)
    ppermute x7, starting transfers between devices, swap(): return lax.ppermute(x, axis, [(0, 1), (1, 0)])  40 us
    ppermute x3, starting transfers between devices, per_device(): l = lax.ppermute((part(nz - k) + l).astype(F16), 'z', left).astype(F32)  15.1 us
    ppermute x3, starting transfers between devices, per_device(): chunk[k] = lax.ppermute(chunk[k - 1], 'z', left)  15 us
    ppermute x7, waiting for transfers between devices, swap(): return lax.ppermute(x, axis, [(0, 1), (1, 0)])  12.5 us
    ppermute x3, waiting for transfers between devices, per_device(): r = lax.ppermute((part(k) + r).astype(F16), 'z', right).astype(F32)  11.6 us
    ppermute x3, waiting for transfers between devices, per_device(): chunk[nz - k] = lax.ppermute(chunk[(nz - k + 1) % nz], 'z', right)  10.1 us
    ppermute x1, starting transfers between devices, per_device(): l = lax.ppermute(first[cut:], 'z', left).astype(F32)  8.59 us
    all_to_all x1, starting transfers between devices, per_device(): lax.all_to_all(pair, 'y', 0, 0, tiled=True).reshape(ny * rows, 2 * width)  7.65 us
  transfers between devices with their start and end apart: 25, of which 15 were waited for; matrix products, arithmetic and copies ran while one was open for 5% of the time, Pallas kernels for 3%

profile of v3, /device:TPU:1, one launch (start us, length us, event | category | flops | bytes accessed | tf_op | source)
XLA Modules:
  0.0 196.3 jit_solution(5954398919659193876)
XLA Ops:
  2.4 7.7 %all-to-all-start = ((bf16[8,32,1024]{2,1,0:T(8,128)(2,1)}), bf16[8,32,1024]{2,1,0:T(8,128)(2,1)S(1)}, u32[]{:S(2)}, u32[]{:S(2)}) async-start(bf16[8,32,1024]{2,1,0:T(8,128)(2,1)} %broadcast_in_dim.2), calls=%async_computation | async-start | bytes 1048576 | tf_op jit(solution)/shard_map/all_to_all | solution.py:91
  10.3 4.6 %collective-permute-start = (bf16[512,512]{0,1:T(8,128)(2,1)S(1)}, bf16[512,512]{0,1:T(8,128)(2,1)S(1)}, u32[]{:S(2)}, u32[]{:S(2)}) collective-permute-start(bf16[512,512]{0,1:T(8,128)(2,1)S(1)} %copy.12), channel_id=1, source_target_pairs={{0,1},{1,0},{2,3},{3,2},{4,5},{5,4},{6,7},{7,6},{8,9},{9,8},{10,11... | collective-permute-start | bytes 1572872 | tf_op jit(solution)/shard_map/ppermute | solution.py:22
  19.5 5.3 %all-to-all-done = bf16[8,32,1024]{2,1,0:T(8,128)(2,1)S(1)} async-done(((bf16[8,32,1024]{2,1,0:T(8,128)(2,1)}), bf16[8,32,1024]{2,1,0:T(8,128)(2,1)S(1)}, u32[]{:S(2)}, u32[]{:S(2)}) %all-to-all-start) | async-done | bytes 524320 | tf_op jit(solution)/shard_map/all_to_all | solution.py:91
  24.8 7.8 %collective-permute-start.2 = (bf16[256,1024]{1,0:T(8,128)(2,1)S(1)}, bf16[256,1024]{1,0:T(8,128)(2,1)S(1)}, u32[]{:S(2)}, u32[]{:S(2)}) collective-permute-start(bf16[256,1024]{1,0:T(8,128)(2,1)S(1)} %bitcast.107), channel_id=1, source_target_pairs={{0,2},{2,0},{1,3},{3,1},{4,6},{6,4},{5,7},{7,5},{8,10},{10,8},{9,1... | collective-permute-start | bytes 1572872 | tf_op jit(solution)/shard_map/ppermute | solution.py:22
  37.4 6.5 %collective-permute-done.2 = bf16[256,1024]{1,0:T(8,128)(2,1)S(1)} collective-permute-done((bf16[256,1024]{1,0:T(8,128)(2,1)S(1)}, bf16[256,1024]{1,0:T(8,128)(2,1)S(1)}, u32[]{:S(2)}, u32[]{:S(2)}) %collective-permute-start.2) | collective-permute-done | bytes 524320 | tf_op jit(solution)/shard_map/ppermute | solution.py:22
  44.8 4.5 %collective-permute-start.4 = (f16[192,512]{1,0:T(8,128)(2,1)S(1)}, f16[192,512]{1,0:T(8,128)(2,1)S(1)}, u32[]{:S(2)}, u32[]{:S(2)}) collective-permute-start(f16[192,512]{1,0:T(8,128)(2,1)S(1)} %get-tuple-element.76), channel_id=1, source_target_pairs={{0,64},{64,128},{128,192},{192,256},{256,320},{320,384},{384,448},... | collective-permute-start | bytes 589832 | tf_op jit(solution)/shard_map/ppermute | solution.py:115
  52.5 8.6 %collective-permute-start.8 = (f16[192,512]{1,0:T(8,128)(2,1)S(1)}, f16[192,512]{1,0:T(8,128)(2,1)S(1)}, u32[]{:S(2)}, u32[]{:S(2)}) collective-permute-start(f16[192,512]{1,0:T(8,128)(2,1)S(1)} %get-tuple-element.77), channel_id=1, source_target_pairs={{0,448},{64,0},{128,64},{192,128},{256,192},{320,256},{384,320},{4... | collective-permute-start | bytes 589832 | tf_op jit(solution)/shard_map/ppermute | solution.py:116
  64.1 5.3 %collective-permute-start.9 = (f16[384,512]{1,0:T(8,128)(2,1)S(1)}, f16[384,512]{1,0:T(8,128)(2,1)S(1)}, u32[]{:S(2)}, u32[]{:S(2)}) collective-permute-start(f16[384,512]{1,0:T(8,128)(2,1)S(1)} %fusion.21), channel_id=1, source_target_pairs={{0,448},{64,0},{128,64},{192,128},{256,192},{320,256},{384,320},{4... | collective-permute-start | bytes 1179656 | tf_op jit(solution)/shard_map/ppermute | solution.py:121
  69.4 4.2 %collective-permute-done.5 = f16[384,512]{1,0:T(8,128)(2,1)S(1)} collective-permute-done((f16[384,512]{1,0:T(8,128)(2,1)S(1)}, f16[384,512]{1,0:T(8,128)(2,1)S(1)}, u32[]{:S(2)}, u32[]{:S(2)}) %collective-permute-start.5) | collective-permute-done | bytes 393248 | tf_op jit(solution)/shard_map/ppermute | solution.py:120
  75.8 5.2 %collective-permute-start.10 = (f16[384,512]{1,0:T(8,128)(2,1)S(1)}, f16[384,512]{1,0:T(8,128)(2,1)S(1)}, u32[]{:S(2)}, u32[]{:S(2)}) collective-permute-start(f16[384,512]{1,0:T(8,128)(2,1)S(1)} %fusion.20), channel_id=1, source_target_pairs={{0,448},{64,0},{128,64},{192,128},{256,192},{320,256},{384,320},{4... | collective-permute-start | bytes 1179656 | tf_op jit(solution)/shard_map/ppermute | solution.py:121
  81.0 3.9 %collective-permute-done.6 = f16[384,512]{1,0:T(8,128)(2,1)S(1)} collective-permute-done((f16[384,512]{1,0:T(8,128)(2,1)S(1)}, f16[384,512]{1,0:T(8,128)(2,1)S(1)}, u32[]{:S(2)}, u32[]{:S(2)}) %collective-permute-start.6) | collective-permute-done | bytes 393248 | tf_op jit(solution)/shard_map/ppermute | solution.py:120
  87.1 4.6 %collective-permute-start.11 = (f16[384,512]{1,0:T(8,128)(2,1)S(1)}, f16[384,512]{1,0:T(8,128)(2,1)S(1)}, u32[]{:S(2)}, u32[]{:S(2)}) collective-permute-start(f16[384,512]{1,0:T(8,128)(2,1)S(1)} %fusion.19), channel_id=1, source_target_pairs={{0,448},{64,0},{128,64},{192,128},{256,192},{320,256},{384,320},{4... | collective-permute-start | bytes 1179656 | tf_op jit(solution)/shard_map/ppermute | solution.py:121
  91.6 3.6 %collective-permute-done.7 = f16[384,512]{1,0:T(8,128)(2,1)S(1)} collective-permute-done((f16[384,512]{1,0:T(8,128)(2,1)S(1)}, f16[384,512]{1,0:T(8,128)(2,1)S(1)}, u32[]{:S(2)}, u32[]{:S(2)}) %collective-permute-start.7) | collective-permute-done | bytes 393248 | tf_op jit(solution)/shard_map/ppermute | solution.py:120
  99.7 5.4 %collective-permute-done.12 = f16[384,512]{1,0:T(8,128)(2,1)S(1)} collective-permute-done((f16[384,512]{1,0:T(8,128)(2,1)S(1)}, f16[384,512]{1,0:T(8,128)(2,1)S(1)}, u32[]{:S(2)}, u32[]{:S(2)}) %collective-permute-start.12) | collective-permute-done | bytes 393248 | tf_op jit(solution)/shard_map/ppermute | solution.py:22
  105.8 5.0 %collective-permute-start.14 = (bf16[384,512]{1,0:T(8,128)(2,1)S(1)}, bf16[384,512]{1,0:T(8,128)(2,1)S(1)}, u32[]{:S(2)}, u32[]{:S(2)}) collective-permute-start(bf16[384,512]{1,0:T(8,128)(2,1)S(1)} %pad_maximum_fusion.1.refs_0_), channel_id=1, source_target_pairs={{0,448},{64,0},{128,64},{192,128},{256,192},{320,256},{384,320},{4... | collective-permute-start | bytes 1179656 | tf_op jit(solution)/shard_map/ppermute | solution.py:138
  115.5 5.0 %collective-permute-start.16 = (bf16[384,512]{1,0:T(8,128)(2,1)S(1)}, bf16[384,512]{1,0:T(8,128)(2,1)S(1)}, u32[]{:S(2)}, u32[]{:S(2)}) collective-permute-start(bf16[384,512]{1,0:T(8,128)(2,1)S(1)} %collective-permute-done.14.refs_1_), channel_id=1, source_target_pairs={{0,448},{64,0},{128,64},{192,128},{256,192},{320,256},{384,320},{4... | collective-permute-start | bytes 1179656 | tf_op jit(solution)/shard_map/ppermute | solution.py:138
  123.1 3.5 %collective-permute-done.16.refs_2_ = bf16[384,512]{1,0:T(8,128)(2,1)S(1)} collective-permute-done((bf16[384,512]{1,0:T(8,128)(2,1)S(1)}, bf16[384,512]{1,0:T(8,128)(2,1)S(1)}, u32[]{:S(2)}, u32[]{:S(2)}) %collective-permute-start.16) | collective-permute-done | bytes 393248 | tf_op jit(solution)/shard_map/ppermute | solution.py:138
  126.6 5.0 %collective-permute-start.18 = (bf16[384,512]{1,0:T(8,128)(2,1)S(1)}, bf16[384,512]{1,0:T(8,128)(2,1)S(1)}, u32[]{:S(2)}, u32[]{:S(2)}) collective-permute-start(bf16[384,512]{1,0:T(8,128)(2,1)S(1)} %collective-permute-done.16.refs_2_), channel_id=1, source_target_pairs={{0,448},{64,0},{128,64},{192,128},{256,192},{320,256},{384,320},{4... | collective-permute-start | bytes 1179656 | tf_op jit(solution)/shard_map/ppermute | solution.py:138
  134.5 9.8 %collective-permute-done.17.refs_5_ = bf16[384,512]{1,0:T(8,128)(2,1)S(1)} collective-permute-done((bf16[384,512]{1,0:T(8,128)(2,1)S(1)}, bf16[384,512]{1,0:T(8,128)(2,1)S(1)}, u32[]{:S(2)}, u32[]{:S(2)}) %collective-permute-start.17) | collective-permute-done | bytes 393248 | tf_op jit(solution)/shard_map/ppermute | solution.py:137
  146.3 4.6 %collective-permute-start.20 = (bf16[192,512]{1,0:T(8,128)(2,1)S(1)}, bf16[192,512]{1,0:T(8,128)(2,1)S(1)}, u32[]{:S(2)}, u32[]{:S(2)}) collective-permute-start(bf16[192,512]{1,0:T(8,128)(2,1)S(1)} %slice.231), channel_id=1, source_target_pairs={{0,448},{64,0},{128,64},{192,128},{256,192},{320,256},{384,320},{4... | collective-permute-start | bytes 589832 | tf_op jit(solution)/shard_map/ppermute | solution.py:142
  155.1 4.6 %collective-permute-start.21 = (bf16[256,512]{1,0:T(8,128)(2,1)S(1)}, bf16[256,512]{1,0:T(8,128)(2,1)S(1)}, u32[]{:S(2)}, u32[]{:S(2)}) collective-permute-start(bf16[256,512]{1,0:T(8,128)(2,1)S(1)} %slice.259), channel_id=1, source_target_pairs={{0,2},{2,0},{1,3},{3,1},{4,6},{6,4},{5,7},{7,5},{8,10},{10,8},{9,1... | collective-permute-start | bytes 786440 | tf_op jit(solution)/shard_map/ppermute | solution.py:22
  163.7 15.4 %collective-permute-start.22 = (bf16[8,192,512]{2,1,0:T(8,128)(2,1)S(1)}, bf16[8,192,512]{2,1,0:T(8,128)(2,1)S(1)}, u32[]{:S(2)}, u32[]{:S(2)}) collective-permute-start(bf16[8,192,512]{2,1,0:T(8,128)(2,1)S(1)} %get-tuple-element.40), channel_id=1, source_target_pairs={{0,1},{1,0},{2,3},{3,2},{4,5},{5,4},{6,7},{7,6},{8,9},{9,8},{10,11... | collective-permute-start | bytes 4718600 | tf_op jit(solution)/shard_map/ppermute | solution.py:22
  184.5 4.2 %shard_map.85 = (bf16[512,512]{1,0:T(8,128)(2,1)}, bf16[512,512]{1,0:T(8,128)(2,1)}, bf16[512,512]{1,0:T(8,128)(2,1)}) custom-call(f32[8,192,512]{2,1,0:T(8,128)} %copy-done, bf16[8,192,512]{2,1,0:T(8,128)(2,1)} %copy-done.3), custom_call_target="tpu_custom_call" | custom-call | tf_op jit(solution)/shard_map/pallas_call | solution.py:68
  188.7 6.9 %all-to-all-done.1 = bf16[8,32,512]{2,1,0:T(8,128)(2,1)S(1)} async-done(((bf16[8,32,512]{2,1,0:T(8,128)(2,1)}), bf16[8,32,512]{2,1,0:T(8,128)(2,1)S(1)}, u32[]{:S(2)}, u32[]{:S(2)}) %all-to-all-start.1) | async-done | bytes 262176 | tf_op jit(solution)/shard_map/all_to_all | solution.py:155
  (92 shorter events, 53.7 us)
Async XLA Ops:
  2.4 22.4 %all-to-all-start = ((bf16[8,32,1024]{2,1,0:T(8,128)(2,1)}), bf16[8,32,1024]{2,1,0:T(8,128)(2,1)S(1)}, u32[]{:S(2)}, u32[]{:S(2)}) async-start(bf16[8,32,1024]{2,1,0:T(8,128)(2,1)} %broadcast_in_dim.2), calls=%async_computation | async-start | bytes 1048576 | tf_op jit(solution)/shard_map/all_to_all | solution.py:91
  10.3 22.4 %collective-permute-start = (bf16[512,512]{0,1:T(8,128)(2,1)S(1)}, bf16[512,512]{0,1:T(8,128)(2,1)S(1)}, u32[]{:S(2)}, u32[]{:S(2)}) collective-permute-start(bf16[512,512]{0,1:T(8,128)(2,1)S(1)} %copy.12), channel_id=1, source_target_pairs={{0,1},{1,0},{2,3},{3,2},{4,5},{5,4},{6,7},{7,6},{8,9},{9,8},{10,11... | collective-permute-start | bytes 1572872 | tf_op jit(solution)/shard_map/ppermute | solution.py:22
  15.2 17.5 %collective-permute-start.1 = (bf16[512,512]{0,1:T(8,128)(2,1)S(1)}, bf16[512,512]{0,1:T(8,128)(2,1)}, u32[]{:S(2)}, u32[]{:S(2)}) collective-permute-start(bf16[512,512]{0,1:T(8,128)(2,1)S(1)} %copy.13), channel_id=1, source_target_pairs={{0,1},{1,0},{2,3},{3,2},{4,5},{5,4},{6,7},{7,6},{8,9},{9,8},{10,11... | collective-permute-start | bytes 1572872 | tf_op jit(solution)/shard_map/ppermute | solution.py:22
  17.1 18.6 %collective-permute-start.3 = (bf16[512,512]{1,0:T(8,128)(2,1)S(1)}, bf16[512,512]{1,0:T(8,128)(2,1)S(1)}, u32[]{:S(2)}, u32[]{:S(2)}) collective-permute-start(bf16[512,512]{1,0:T(8,128)(2,1)S(1)} %copy-done.4), channel_id=1, source_target_pairs={{0,1},{1,0},{2,3},{3,2},{4,5},{5,4},{6,7},{7,6},{8,9},{9,8},{10,11... | collective-permute-start | bytes 1572872 | tf_op jit(solution)/shard_map/ppermute | solution.py:22
  24.8 19.1 %collective-permute-start.2 = (bf16[256,1024]{1,0:T(8,128)(2,1)S(1)}, bf16[256,1024]{1,0:T(8,128)(2,1)S(1)}, u32[]{:S(2)}, u32[]{:S(2)}) collective-permute-start(bf16[256,1024]{1,0:T(8,128)(2,1)S(1)} %bitcast.107), channel_id=1, source_target_pairs={{0,2},{2,0},{1,3},{3,1},{4,6},{6,4},{5,7},{7,5},{8,10},{10,8},{9,1... | collective-permute-start | bytes 1572872 | tf_op jit(solution)/shard_map/ppermute | solution.py:22
  44.8 16.5 %collective-permute-start.4 = (f16[192,512]{1,0:T(8,128)(2,1)S(1)}, f16[192,512]{1,0:T(8,128)(2,1)S(1)}, u32[]{:S(2)}, u32[]{:S(2)}) collective-permute-start(f16[192,512]{1,0:T(8,128)(2,1)S(1)} %get-tuple-element.76), channel_id=1, source_target_pairs={{0,64},{64,128},{128,192},{192,256},{256,320},{320,384},{384,448},... | collective-permute-start | bytes 589832 | tf_op jit(solution)/shard_map/ppermute | solution.py:115
  52.5 11.4 %collective-permute-start.8 = (f16[192,512]{1,0:T(8,128)(2,1)S(1)}, f16[192,512]{1,0:T(8,128)(2,1)S(1)}, u32[]{:S(2)}, u32[]{:S(2)}) collective-permute-start(f16[192,512]{1,0:T(8,128)(2,1)S(1)} %get-tuple-element.77), channel_id=1, source_target_pairs={{0,448},{64,0},{128,64},{192,128},{256,192},{320,256},{384,320},{4... | collective-permute-start | bytes 589832 | tf_op jit(solution)/shard_map/ppermute | solution.py:116
  61.5 12.1 %collective-permute-start.5 = (f16[384,512]{1,0:T(8,128)(2,1)S(1)}, f16[384,512]{1,0:T(8,128)(2,1)S(1)}, u32[]{:S(2)}, u32[]{:S(2)}) collective-permute-start(f16[384,512]{1,0:T(8,128)(2,1)S(1)} %fusion.18), channel_id=1, source_target_pairs={{0,64},{64,128},{128,192},{192,256},{256,320},{320,384},{384,448},... | collective-permute-start | bytes 1179656 | tf_op jit(solution)/shard_map/ppermute | solution.py:120
  64.1 11.5 %collective-permute-start.9 = (f16[384,512]{1,0:T(8,128)(2,1)S(1)}, f16[384,512]{1,0:T(8,128)(2,1)S(1)}, u32[]{:S(2)}, u32[]{:S(2)}) collective-permute-start(f16[384,512]{1,0:T(8,128)(2,1)S(1)} %fusion.21), channel_id=1, source_target_pairs={{0,448},{64,0},{128,64},{192,128},{256,192},{320,256},{384,320},{4... | collective-permute-start | bytes 1179656 | tf_op jit(solution)/shard_map/ppermute | solution.py:121
  73.7 11.2 %collective-permute-start.6 = (f16[384,512]{1,0:T(8,128)(2,1)S(1)}, f16[384,512]{1,0:T(8,128)(2,1)S(1)}, u32[]{:S(2)}, u32[]{:S(2)}) collective-permute-start(f16[384,512]{1,0:T(8,128)(2,1)S(1)} %fusion.17), channel_id=1, source_target_pairs={{0,64},{64,128},{128,192},{192,256},{256,320},{320,384},{384,448},... | collective-permute-start | bytes 1179656 | tf_op jit(solution)/shard_map/ppermute | solution.py:120
  75.8 11.2 %collective-permute-start.10 = (f16[384,512]{1,0:T(8,128)(2,1)S(1)}, f16[384,512]{1,0:T(8,128)(2,1)S(1)}, u32[]{:S(2)}, u32[]{:S(2)}) collective-permute-start(f16[384,512]{1,0:T(8,128)(2,1)S(1)} %fusion.20), channel_id=1, source_target_pairs={{0,448},{64,0},{128,64},{192,128},{256,192},{320,256},{384,320},{4... | collective-permute-start | bytes 1179656 | tf_op jit(solution)/shard_map/ppermute | solution.py:121
  85.0 10.3 %collective-permute-start.7 = (f16[384,512]{1,0:T(8,128)(2,1)S(1)}, f16[384,512]{1,0:T(8,128)(2,1)S(1)}, u32[]{:S(2)}, u32[]{:S(2)}) collective-permute-start(f16[384,512]{1,0:T(8,128)(2,1)S(1)} %fusion.16), channel_id=1, source_target_pairs={{0,64},{64,128},{128,192},{192,256},{256,320},{320,384},{384,448},... | collective-permute-start | bytes 1179656 | tf_op jit(solution)/shard_map/ppermute | solution.py:120
  87.1 9.3 %collective-permute-start.11 = (f16[384,512]{1,0:T(8,128)(2,1)S(1)}, f16[384,512]{1,0:T(8,128)(2,1)S(1)}, u32[]{:S(2)}, u32[]{:S(2)}) collective-permute-start(f16[384,512]{1,0:T(8,128)(2,1)S(1)} %fusion.19), channel_id=1, source_target_pairs={{0,448},{64,0},{128,64},{192,128},{256,192},{320,256},{384,320},{4... | collective-permute-start | bytes 1179656 | tf_op jit(solution)/shard_map/ppermute | solution.py:121
  96.5 8.5 %collective-permute-start.12 = (f16[384,512]{1,0:T(8,128)(2,1)S(1)}, f16[384,512]{1,0:T(8,128)(2,1)S(1)}, u32[]{:S(2)}, u32[]{:S(2)}) collective-permute-start(f16[384,512]{1,0:T(8,128)(2,1)S(1)} %fusion.47), channel_id=1, source_target_pairs={{0,32},{32,0},{1,33},{33,1},{2,34},{34,2},{3,35},{35,3},{4,36},{36... | collective-permute-start | bytes 1179656 | tf_op jit(solution)/shard_map/ppermute | solution.py:22
  105.8 9.7 %collective-permute-start.14 = (bf16[384,512]{1,0:T(8,128)(2,1)S(1)}, bf16[384,512]{1,0:T(8,128)(2,1)S(1)}, u32[]{:S(2)}, u32[]{:S(2)}) collective-permute-start(bf16[384,512]{1,0:T(8,128)(2,1)S(1)} %pad_maximum_fusion.1.refs_0_), channel_id=1, source_target_pairs={{0,448},{64,0},{128,64},{192,128},{256,192},{320,256},{384,320},{4... | collective-permute-start | bytes 1179656 | tf_op jit(solution)/shard_map/ppermute | solution.py:138
  110.8 9.7 %collective-permute-start.13 = (bf16[384,512]{1,0:T(8,128)(2,1)S(1)}, bf16[384,512]{1,0:T(8,128)(2,1)S(1)}, u32[]{:S(2)}, u32[]{:S(2)}) collective-permute-start(bf16[384,512]{1,0:T(8,128)(2,1)S(1)} %pad_maximum_fusion.1.refs_0_), channel_id=1, source_target_pairs={{0,64},{64,128},{128,192},{192,256},{256,320},{320,384},{384,448},... | collective-permute-start | bytes 1179656 | tf_op jit(solution)/shard_map/ppermute | solution.py:137
  115.5 11.1 %collective-permute-start.16 = (bf16[384,512]{1,0:T(8,128)(2,1)S(1)}, bf16[384,512]{1,0:T(8,128)(2,1)S(1)}, u32[]{:S(2)}, u32[]{:S(2)}) collective-permute-start(bf16[384,512]{1,0:T(8,128)(2,1)S(1)} %collective-permute-done.14.refs_1_), channel_id=1, source_target_pairs={{0,448},{64,0},{128,64},{192,128},{256,192},{320,256},{384,320},{4... | collective-permute-start | bytes 1179656 | tf_op jit(solution)/shard_map/ppermute | solution.py:138
  120.5 11.3 %collective-permute-start.15 = (bf16[384,512]{1,0:T(8,128)(2,1)S(1)}, bf16[384,512]{1,0:T(8,128)(2,1)S(1)}, u32[]{:S(2)}, u32[]{:S(2)}) collective-permute-start(bf16[384,512]{1,0:T(8,128)(2,1)S(1)} %collective-permute-done.13.refs_7_), channel_id=1, source_target_pairs={{0,64},{64,128},{128,192},{192,256},{256,320},{320,384},{384,448},... | collective-permute-start | bytes 1179656 | tf_op jit(solution)/shard_map/ppermute | solution.py:137
  126.6 19.7 %collective-permute-start.18 = (bf16[384,512]{1,0:T(8,128)(2,1)S(1)}, bf16[384,512]{1,0:T(8,128)(2,1)S(1)}, u32[]{:S(2)}, u32[]{:S(2)}) collective-permute-start(bf16[384,512]{1,0:T(8,128)(2,1)S(1)} %collective-permute-done.16.refs_2_), channel_id=1, source_target_pairs={{0,448},{64,0},{128,64},{192,128},{256,192},{320,256},{384,320},{4... | collective-permute-start | bytes 1179656 | tf_op jit(solution)/shard_map/ppermute | solution.py:138
  131.9 12.4 %collective-permute-start.17 = (bf16[384,512]{1,0:T(8,128)(2,1)S(1)}, bf16[384,512]{1,0:T(8,128)(2,1)S(1)}, u32[]{:S(2)}, u32[]{:S(2)}) collective-permute-start(bf16[384,512]{1,0:T(8,128)(2,1)S(1)} %collective-permute-done.15.refs_6_), channel_id=1, source_target_pairs={{0,64},{64,128},{128,192},{192,256},{256,320},{320,384},{384,448},... | collective-permute-start | bytes 1179656 | tf_op jit(solution)/shard_map/ppermute | solution.py:137
  144.3 9.9 %collective-permute-start.19 = (bf16[192,512]{1,0:T(8,128)(2,1)S(1)}, bf16[192,512]{1,0:T(8,128)(2,1)S(1)}, u32[]{:S(2)}, u32[]{:S(2)}) collective-permute-start(bf16[192,512]{1,0:T(8,128)(2,1)S(1)} %slice.230), channel_id=1, source_target_pairs={{0,64},{64,128},{128,192},{192,256},{256,320},{320,384},{384,448},... | collective-permute-start | bytes 589832 | tf_op jit(solution)/shard_map/ppermute | solution.py:141
  155.1 8.6 %collective-permute-start.21 = (bf16[256,512]{1,0:T(8,128)(2,1)S(1)}, bf16[256,512]{1,0:T(8,128)(2,1)S(1)}, u32[]{:S(2)}, u32[]{:S(2)}) collective-permute-start(bf16[256,512]{1,0:T(8,128)(2,1)S(1)} %slice.259), channel_id=1, source_target_pairs={{0,2},{2,0},{1,3},{3,1},{4,6},{6,4},{5,7},{7,5},{8,10},{10,8},{9,1... | collective-permute-start | bytes 786440 | tf_op jit(solution)/shard_map/ppermute | solution.py:22
  163.7 19.6 %collective-permute-start.22 = (bf16[8,192,512]{2,1,0:T(8,128)(2,1)S(1)}, bf16[8,192,512]{2,1,0:T(8,128)(2,1)S(1)}, u32[]{:S(2)}, u32[]{:S(2)}) collective-permute-start(bf16[8,192,512]{2,1,0:T(8,128)(2,1)S(1)} %get-tuple-element.40), channel_id=1, source_target_pairs={{0,1},{1,0},{2,3},{3,2},{4,5},{5,4},{6,7},{7,6},{8,9},{9,8},{10,11... | collective-permute-start | bytes 4718600 | tf_op jit(solution)/shard_map/ppermute | solution.py:22
  179.9 15.7 %all-to-all-start.1 = ((bf16[8,32,512]{2,1,0:T(8,128)(2,1)}), bf16[8,32,512]{2,1,0:T(8,128)(2,1)S(1)}, u32[]{:S(2)}, u32[]{:S(2)}) async-start(bf16[8,32,512]{2,1,0:T(8,128)(2,1)} %bitcast.116), calls=%async_computation.1 | async-start | bytes 524288 | tf_op jit(solution)/shard_map/all_to_all | solution.py:155
  (9 other events, 60.2 us)

commit v4 on v3

--- a/solution.py
+++ b/solution.py
@@ -44,6 +44,98 @@
         send_ref[at, 2 * zf :, :] = dn[zf:].astype(BF16)
 
 
+def input_kernel(nz, at, *refs):
+    chunks, (own_ref, oth_ref, out_ref) = refs[:nz], refs[nz:]
+    n, h = out_ref.shape[0], own_ref.shape[1]
+    total = jnp.zeros(out_ref.shape, F32)
+    for k in range(nz):
+        for i, ref in enumerate((own_ref, oth_ref)):
+            deltas = chunks[k][i * h : (i + 1) * h, at : at + n]
+            total += lax.dot_general(
+                deltas, ref[k], (((0,), (0,)), ((), ())), preferred_element_type=F32
+            )
+    out_ref[...] = total.astype(out_ref.dtype)
+
+
+def input_grads(chunks, own, oth, at, n, dtype):
+    return pl.pallas_call(
+        functools.partial(input_kernel, len(chunks), at),
+        out_shape=jax.ShapeDtypeStruct((n, own.shape[2]), dtype),
+        compiler_params=pltpu.CompilerParams(vmem_limit_bytes=40 * 2**20),
+    )(*chunks, own, oth)
+
+
+def weight_grads(chunks, xs, cs, zf):
+    shape = (len(chunks), 3 * zf, xs.shape[1])
+    return pl.pallas_call(
+        functools.partial(grads_kernel, len(chunks), zf),
+        out_shape=(jax.ShapeDtypeStruct(shape, F32), jax.ShapeDtypeStruct(shape, BF16)),
+        compiler_params=pltpu.CompilerParams(vmem_limit_bytes=40 * 2**20),
+    )(*chunks, xs, cs)
+
+
+def finish_kernel(zf, own_ref, got_ref, gate_ref, up_ref, down_ref):
+    for i in range(0, own_ref.shape[0], 2):
+        both = (own_ref[i : i + 2] + got_ref[i : i + 2].astype(F32)).astype(BF16)
+        at = pl.ds(i * zf, 2 * zf)
+        gate_ref[:, at] = jnp.concatenate([both[0, :zf], both[1, :zf]], axis=0).T
+        up_ref[:, at] = jnp.concatenate([both[0, zf : 2 * zf], both[1, zf : 2 * zf]], axis=0).T
+        down_ref[at, :] = jnp.concatenate([both[0, 2 * zf :], both[1, 2 * zf :]], axis=0)
+
+
+def finish(own, got):
+    nz, n, width = own.shape
+    zf = n // 3
+    return pl.pallas_call(
+        functools.partial(finish_kernel, zf),
+        out_shape=[
+            jax.ShapeDtypeStruct((width, nz * zf), BF16),
+            jax.ShapeDtypeStruct((width, nz * zf), BF16),
+            jax.ShapeDtypeStruct((nz * zf, width), BF16),
+        ],
+        compiler_params=pltpu.CompilerParams(vmem_limit_bytes=40 * 2**20),
+    )(own, got)
+
+
+def turn(x, by):
+    n = x.shape[0]
+    return lax.dynamic_slice_in_dim(jnp.concatenate([x, x], axis=0), by, n, axis=0)
+
+
+def grads_kernel(nz, zf, *refs):
+    chunks, (x_ref, c_ref, own_ref, send_ref) = refs[:nz], refs[nz:]
+    z = lax.axis_index("z")
+    for k in range(nz):
+        at = lax.rem(z + k, nz)
+        gu = jnp.dot(chunks[k][: 4 * zf, :], x_ref[...], preferred_element_type=F32)
+        dn = jnp.dot(chunks[k][4 * zf :, :], c_ref[...], preferred_element_type=F32)
+        own_ref[at, : 2 * zf, :] = gu[: 2 * zf]
+        own_ref[at, 2 * zf :, :] = dn[:zf]
+        send_ref[at, : 2 * zf, :] = gu[2 * zf :].astype(BF16)
+        send_ref[at, 2 * zf :, :] = dn[zf:].astype(BF16)
+
+
+def input_kernel(nz, at, *refs):
+    chunks, (own_ref, oth_ref, out_ref) = refs[:nz], refs[nz:]
+    n, h = out_ref.shape[0], own_ref.shape[1]
+    total = jnp.zeros(out_ref.shape, F32)
+    for k in range(nz):
+        for i, ref in enumerate((own_ref, oth_ref)):
+            deltas = chunks[k][i * h : (i + 1) * h, at : at + n]
+            total += lax.dot_general(
+                deltas, ref[k], (((0,), (0,)), ((), ())), preferred_element_type=F32
+            )
+    out_ref[...] = total.astype(out_ref.dtype)
+
+
+def input_grads(chunks, own, oth, at, n, dtype):
+    return pl.pallas_call(
+        functools.partial(input_kernel, len(chunks), at),
+        out_shape=jax.ShapeDtypeStruct((n, own.shape[2]), dtype),
+        compiler_params=pltpu.CompilerParams(vmem_limit_bytes=40 * 2**20),
+    )(*chunks, own, oth)
+
+
 def weight_grads(chunks, xs, cs, zf):
     shape = (len(chunks), 3 * zf, xs.shape[1])
     return pl.pallas_call(
@@ -89,33 +181,35 @@
     pair = jnp.concatenate([x, c], axis=1)
     pair = jnp.broadcast_to(pair[None], (ny,) + pair.shape)
     pair = lax.all_to_all(pair, "y", 0, 0, tiled=True).reshape(ny * rows, 2 * width)
-    pair = jnp.concatenate([pair, swap(pair, "xh")], axis=0)
-    xs, cs = pair[:, :width], pair[:, width:]
-    half = xs.shape[0]
+    other = swap(pair, "xh")
+    part_tokens = pair.shape[0]
+    x0, c0, x1, c1 = pair[:, :width], pair[:, width:], other[:, :width], other[:, width:]
+    xs, cs = jnp.concatenate([x0, x1], axis=0), jnp.concatenate([c0, c1], axis=0)
+    half = 2 * part_tokens
 
     def by_z(*weights):
         return turn(jnp.stack([w.reshape(nz, zf, width) for w in weights], axis=1), z).reshape(nz, -1, width)
 
-    wgu = by_z(wg.T, wu.T, swap(wg, "core").T, swap(wu, "core").T)
-    wdd = by_z(wd, swap(wd, "core"))
+    gu_own, gu_oth = by_z(wg.T, wu.T), by_z(swap(wg, "core").T, swap(wu, "core").T)
+    d_own, d_oth = by_z(wd), by_z(swap(wd, "core"))
     far = nz // 2
 
-
-    def part_far():
-        return dot(wgu[far], xs, 1, 1) * SCALE, dot(wdd[far], cs, 1, 1) * SCALE
-
-    gu = (dot(wgu.reshape(-1, width), xs, 1, 1) * SCALE).reshape(nz, 4 * zf, half)
-    hg = (dot(wdd.reshape(-1, width), cs, 1, 1) * SCALE).reshape(nz, 2 * zf, half)
+    def part_far(t, u):
+        halves = [(gu_own, t), (gu_oth, t), (d_own, u), (d_oth, u)]
+        return jnp.concatenate([dot(w[far], v, 1, 1) for w, v in halves], axis=0) * SCALE
+
+    parts = [
+        (dot(w.reshape(-1, width), t, 1, 1) * SCALE).reshape(nz, -1, half)
+        for w, t in ((gu_own, xs), (gu_oth, xs), (d_own, cs), (d_oth, cs))
+    ]
 
     def part(k):
-        return jnp.concatenate([gu[k], hg[k]], axis=0)
-
-    cut = 3 * zf
-    first = jnp.concatenate(part_far(), axis=0).astype(F16)
-    r = lax.ppermute(first[:cut], "z", right).astype(F32)
-    l = lax.ppermute(first[cut:], "z", left).astype(F32)
-    r = jnp.pad(r, ((0, cut), (0, 0)))
-    l = jnp.pad(l, ((cut, 0), (0, 0)))
+        return jnp.concatenate([p[k] for p in parts], axis=0)
+
+    r = lax.ppermute(part_far(x0, c0).astype(F16), "z", right).astype(F32)
+    l = lax.ppermute(part_far(x1, c1).astype(F16), "z", left).astype(F32)
+    r = jnp.pad(r, ((0, 0), (0, part_tokens)))
+    l = jnp.pad(l, ((0, 0), (part_tokens, 0)))
     for k in range(far - 1, 0, -1):
         r = lax.ppermute((part(k) + r).astype(F16), "z", right).astype(F32)
         l = lax.ppermute((part(nz - k) + l).astype(F16), "z", left).astype(F32)
@@ -138,20 +232,20 @@
         chunk[k] = lax.ppermute(chunk[k - 1], "z", left)
     chunk[far] = jnp.concatenate(
         [
-            lax.ppermute(chunk[far + 1][:cut], "z", right),
-            lax.ppermute(chunk[far - 1][cut:], "z", left),
+            lax.ppermute(chunk[far + 1][:, :part_tokens], "z", right),
+            lax.ppermute(chunk[far - 1][:, part_tokens:], "z", left),
         ],
-        axis=0,
+        axis=1,
     )
-    total = jnp.zeros((half, width), F32)
-    for k in [0] + [j for i in range(1, far) for j in (nz - i, i)] + [far]:
-        total = total + dot(chunk[k][: 4 * zf], wgu[k], 0, 0)
-
-    total, send, *chunk = tie(total[: half // 2], total[half // 2 :].astype(BF16), *chunk)
+
+    send = input_grads(chunk, gu_own, gu_oth, part_tokens, part_tokens, BF16)
+    send, *chunk = tie(send, *chunk)
     got = swap(send, "xh")
     own, send = weight_grads(chunk, xs, cs, zf)
-    got, own, send = tie(got, own, send)
+    total = input_grads(chunk, gu_own, gu_oth, 0, part_tokens, F32)
+    got, total = tie(got, total)
     total = (total + got.astype(F32)).astype(BF16).reshape(ny, rows, width)
+    total, own, send = tie(total, own, send)
     recv = lax.all_to_all(total, "y", 0, 0, tiled=True)
     gate_grad, up_grad, down_grad = finish(own, swap(send, "core"))
     recv, gate_grad, up_grad, down_grad = tie(recv, gate_grad, up_grad, down_grad)

time: 197 us -> 190 us (0.964)
  waiting for transfers between devices: 57.1 us -> 49.4 us
  starting transfers between devices: 112 us -> 108 us
  other arithmetic: 7.41 us -> 10.3 us
  Pallas kernels: 6.04 us -> 8.56 us
    ppermute x3, waiting for transfers between devices: 5.9 us -> 0.01 us  [per_device(): chunk[k] = lax.ppermute(chunk[k - 1], 'z', left)]
    all_to_all x1, waiting for transfers between devices: 5.29 us -> 0.01 us  [per_device(): lax.all_to_all(pair, 'y', 0, 0, tiled=True).reshape(ny * rows, 2 * width)]
    ppermute x7, starting transfers between devices: 40 us -> 35.1 us  [swap(): return lax.ppermute(x, axis, [(0, 1), (1, 0)])]
    concatenate x2 -> x4, other arithmetic: 3.46 us -> 6.4 us  [turn(): jnp.concatenate([x, x], axis=0)]
    pallas_call x0 -> x2, Pallas kernels: none -> 2.52 us  [input_grads(): pl.pallas_call(functools.partial(input_kernel, len(chunks), at), out_shap...]
    ppermute x4, starting transfers between devices: 19.5 us -> 21.9 us  [the longest x1 11.1 us: per_device(): l = lax.ppermute(part_far(x1, c1).astype(F16), 'z', left).astype(F32)]
    ppermute x3, waiting for transfers between devices: 10.1 us -> 12.2 us  [per_device(): chunk[nz - k] = lax.ppermute(chunk[(nz - k + 1) % nz], 'z', right)]
    unnamed x17 -> x13, local copies, waits for them, and re-layouts: 4.74 us -> 4.01 us
  transfers between devices with their start and end apart: 25 -> 25, of which waited for: 15 -> 12; matrix products, arithmetic and copies ran while one was open for 5% -> 8% of each run, Pallas kernels for 3% -> 4%
where the time goes in v4:
time: 190 us; the launch traced here: 189 us
  starting transfers between devices  108 us (57%)
  waiting for transfers between devices  49.4 us (26%)
  other arithmetic  10.3 us (5%)
  Pallas kernels  8.56 us (5%)
  local copies, waits for them, and re-layouts  5.83 us (3%)
  matrix products  4.97 us (3%)
    ppermute x7, starting transfers between devices, swap(): return lax.ppermute(x, axis, [(0, 1), (1, 0)])  35.1 us
    ppermute x3, starting transfers between devices, per_device(): chunk[k] = lax.ppermute(chunk[k - 1], 'z', left)  14.4 us
    ppermute x3, starting transfers between devices, per_device(): l = lax.ppermute((part(nz - k) + l).astype(F16), 'z', left).astype(F32)  13.7 us
    ppermute x3, waiting for transfers between devices, per_device(): r = lax.ppermute((part(k) + r).astype(F16), 'z', right).astype(F32)  13.5 us
    ppermute x3, waiting for transfers between devices, per_device(): chunk[nz - k] = lax.ppermute(chunk[(nz - k + 1) % nz], 'z', right)  12.2 us
    ppermute x1, starting transfers between devices, per_device(): l = lax.ppermute(part_far(x1, c1).astype(F16), 'z', left).astype(F32)  11.1 us
    ppermute x7, waiting for transfers between devices, swap(): return lax.ppermute(x, axis, [(0, 1), (1, 0)])  10.8 us
    all_to_all x1, starting transfers between devices, per_device(): lax.all_to_all(pair, 'y', 0, 0, tiled=True).reshape(ny * rows, 2 * width)  7.65 us
  transfers between devices with their start and end apart: 25, of which 12 were waited for; matrix products, arithmetic and copies ran while one was open for 8% of the time, Pallas kernels for 4%

profile of v4, /device:TPU:1, one launch (start us, length us, event | category | flops | bytes accessed | tf_op | source)
XLA Modules:
  0.0 188.8 jit_solution(17274954965294232327)
XLA Ops:
  2.4 7.7 %all-to-all-start = ((bf16[8,32,1024]{2,1,0:T(8,128)(2,1)}), bf16[8,32,1024]{2,1,0:T(8,128)(2,1)S(1)}, u32[]{:S(2)}, u32[]{:S(2)}) async-start(bf16[8,32,1024]{2,1,0:T(8,128)(2,1)} %broadcast_in_dim.2), calls=%async_computation | async-start | bytes 1048576 | tf_op jit(solution)/shard_map/all_to_all | solution.py:183
  10.2 4.6 %collective-permute-start.2 = (bf16[512,512]{0,1:T(8,128)(2,1)S(1)}, bf16[512,512]{0,1:T(8,128)(2,1)S(1)}, u32[]{:S(2)}, u32[]{:S(2)}) collective-permute-start(bf16[512,512]{0,1:T(8,128)(2,1)S(1)} %copy.26), channel_id=1, source_target_pairs={{0,1},{1,0},{2,3},{3,2},{4,5},{5,4},{6,7},{7,6},{8,9},{9,8},{10,11... | collective-permute-start | bytes 1572872 | tf_op jit(solution)/shard_map/ppermute | solution.py:22
  26.9 5.7 %collective-permute-start = (bf16[256,1024]{1,0:T(8,128)(2,1)S(1)}, bf16[256,1024]{1,0:T(8,128)(2,1)S(1)}, u32[]{:S(2)}, u32[]{:S(2)}) collective-permute-start(bf16[256,1024]{1,0:T(8,128)(2,1)S(1)} %bitcast.98), channel_id=1, source_target_pairs={{0,2},{2,0},{1,3},{3,1},{4,6},{6,4},{5,7},{7,5},{8,10},{10,8},{9,1... | collective-permute-start | bytes 1572872 | tf_op jit(solution)/shard_map/ppermute | solution.py:22
  34.4 4.0 %collective-permute-start.4 = (f16[384,256]{1,0:T(8,128)(2,1)S(1)}, f16[384,256]{1,0:T(8,128)(2,1)S(1)}, u32[]{:S(2)}, u32[]{:S(2)}) collective-permute-start(f16[384,256]{1,0:T(8,128)(2,1)S(1)} %fusion.15), channel_id=1, source_target_pairs={{0,64},{64,128},{128,192},{192,256},{256,320},{320,384},{384,448},... | collective-permute-start | bytes 589832 | tf_op jit(solution)/shard_map/ppermute | solution.py:209
  38.5 5.5 %collective-permute-done = bf16[256,1024]{1,0:T(8,128)(2,1)S(1)} collective-permute-done((bf16[256,1024]{1,0:T(8,128)(2,1)S(1)}, bf16[256,1024]{1,0:T(8,128)(2,1)S(1)}, u32[]{:S(2)}, u32[]{:S(2)}) %collective-permute-start) | collective-permute-done | bytes 524320 | tf_op jit(solution)/shard_map/ppermute | solution.py:22
  44.8 11.1 %collective-permute-start.8 = (f16[384,256]{1,0:T(8,128)(2,1)S(1)}, f16[384,256]{1,0:T(8,128)(2,1)S(1)}, u32[]{:S(2)}, u32[]{:S(2)}) collective-permute-start(f16[384,256]{1,0:T(8,128)(2,1)S(1)} %fusion.16), channel_id=1, source_target_pairs={{0,448},{64,0},{128,64},{192,128},{256,192},{320,256},{384,320},{4... | collective-permute-start | bytes 589832 | tf_op jit(solution)/shard_map/ppermute | solution.py:210
  61.3 4.6 %collective-permute-start.9 = (f16[384,512]{1,0:T(8,128)(2,1)S(1)}, f16[384,512]{1,0:T(8,128)(2,1)S(1)}, u32[]{:S(2)}, u32[]{:S(2)}) collective-permute-start(f16[384,512]{1,0:T(8,128)(2,1)S(1)} %fusion.12), channel_id=1, source_target_pairs={{0,448},{64,0},{128,64},{192,128},{256,192},{320,256},{384,320},{4... | collective-permute-start | bytes 1179656 | tf_op jit(solution)/shard_map/ppermute | solution.py:215
  65.8 5.4 %collective-permute-done.5 = f16[384,512]{1,0:T(8,128)(2,1)S(1)} collective-permute-done((f16[384,512]{1,0:T(8,128)(2,1)S(1)}, f16[384,512]{1,0:T(8,128)(2,1)S(1)}, u32[]{:S(2)}, u32[]{:S(2)}) %collective-permute-start.5) | collective-permute-done | bytes 393248 | tf_op jit(solution)/shard_map/ppermute | solution.py:214
  73.5 4.6 %collective-permute-start.10 = (f16[384,512]{1,0:T(8,128)(2,1)S(1)}, f16[384,512]{1,0:T(8,128)(2,1)S(1)}, u32[]{:S(2)}, u32[]{:S(2)}) collective-permute-start(f16[384,512]{1,0:T(8,128)(2,1)S(1)} %fusion.11), channel_id=1, source_target_pairs={{0,448},{64,0},{128,64},{192,128},{256,192},{320,256},{384,320},{4... | collective-permute-start | bytes 1179656 | tf_op jit(solution)/shard_map/ppermute | solution.py:215
  78.1 4.5 %collective-permute-done.6 = f16[384,512]{1,0:T(8,128)(2,1)S(1)} collective-permute-done((f16[384,512]{1,0:T(8,128)(2,1)S(1)}, f16[384,512]{1,0:T(8,128)(2,1)S(1)}, u32[]{:S(2)}, u32[]{:S(2)}) %collective-permute-start.6) | collective-permute-done | bytes 393248 | tf_op jit(solution)/shard_map/ppermute | solution.py:214
  84.8 4.6 %collective-permute-start.11 = (f16[384,512]{1,0:T(8,128)(2,1)S(1)}, f16[384,512]{1,0:T(8,128)(2,1)S(1)}, u32[]{:S(2)}, u32[]{:S(2)}) collective-permute-start(f16[384,512]{1,0:T(8,128)(2,1)S(1)} %fusion.10), channel_id=1, source_target_pairs={{0,448},{64,0},{128,64},{192,128},{256,192},{320,256},{384,320},{4... | collective-permute-start | bytes 1179656 | tf_op jit(solution)/shard_map/ppermute | solution.py:215
  89.4 3.6 %collective-permute-done.7 = f16[384,512]{1,0:T(8,128)(2,1)S(1)} collective-permute-done((f16[384,512]{1,0:T(8,128)(2,1)S(1)}, f16[384,512]{1,0:T(8,128)(2,1)S(1)}, u32[]{:S(2)}, u32[]{:S(2)}) %collective-permute-start.7) | collective-permute-done | bytes 393248 | tf_op jit(solution)/shard_map/ppermute | solution.py:214
  97.4 5.4 %collective-permute-done.12 = f16[384,512]{1,0:T(8,128)(2,1)S(1)} collective-permute-done((f16[384,512]{1,0:T(8,128)(2,1)S(1)}, f16[384,512]{1,0:T(8,128)(2,1)S(1)}, u32[]{:S(2)}, u32[]{:S(2)}) %collective-permute-start.12) | collective-permute-done | bytes 393248 | tf_op jit(solution)/shard_map/ppermute | solution.py:22
  105.4 5.0 %collective-permute-start.13 = (bf16[384,512]{1,0:T(8,128)(2,1)S(1)}, bf16[384,512]{1,0:T(8,128)(2,1)S(1)}, u32[]{:S(2)}, u32[]{:S(2)}) collective-permute-start(bf16[384,512]{1,0:T(8,128)(2,1)S(1)} %pad_maximum_fusion.2.refs_0_), channel_id=1, source_target_pairs={{0,448},{64,0},{128,64},{192,128},{256,192},{320,256},{384,320},{4... | collective-permute-start | bytes 1179656 | tf_op jit(solution)/shard_map/ppermute | solution.py:232
  115.6 4.6 %collective-permute-start.14 = (bf16[384,512]{1,0:T(8,128)(2,1)S(1)}, bf16[384,512]{1,0:T(8,128)(2,1)S(1)}, u32[]{:S(2)}, u32[]{:S(2)}) collective-permute-start(bf16[384,512]{1,0:T(8,128)(2,1)S(1)} %collective-permute-done.13.refs_1_), channel_id=1, source_target_pairs={{0,448},{64,0},{128,64},{192,128},{256,192},{320,256},{384,320},{4... | collective-permute-start | bytes 1179656 | tf_op jit(solution)/shard_map/ppermute | solution.py:232
  120.2 3.9 %collective-permute-done.17.refs_6_ = bf16[384,512]{1,0:T(8,128)(2,1)S(1)} collective-permute-done((bf16[384,512]{1,0:T(8,128)(2,1)S(1)}, bf16[384,512]{1,0:T(8,128)(2,1)S(1)}, u32[]{:S(2)}, u32[]{:S(2)}) %collective-permute-start.17) | collective-permute-done | bytes 393248 | tf_op jit(solution)/shard_map/ppermute | solution.py:231
  126.1 4.8 %collective-permute-start.15 = (bf16[384,512]{1,0:T(8,128)(2,1)S(1)}, bf16[384,512]{1,0:T(8,128)(2,1)S(1)}, u32[]{:S(2)}, u32[]{:S(2)}) collective-permute-start(bf16[384,512]{1,0:T(8,128)(2,1)S(1)} %collective-permute-done.14.refs_2_), channel_id=1, source_target_pairs={{0,448},{64,0},{128,64},{192,128},{256,192},{320,256},{384,320},{4... | collective-permute-start | bytes 1179656 | tf_op jit(solution)/shard_map/ppermute | solution.py:232
  130.9 5.0 %collective-permute-done.18.refs_5_ = bf16[384,512]{1,0:T(8,128)(2,1)S(1)} collective-permute-done((bf16[384,512]{1,0:T(8,128)(2,1)S(1)}, bf16[384,512]{1,0:T(8,128)(2,1)S(1)}, u32[]{:S(2)}, u32[]{:S(2)}) %collective-permute-start.18) | collective-permute-done | bytes 393248 | tf_op jit(solution)/shard_map/ppermute | solution.py:231
  137.9 4.8 %collective-permute-start.20 = (bf16[384,256]{1,0:T(8,128)(2,1)S(1)}, bf16[384,256]{1,0:T(8,128)(2,1)S(1)}, u32[]{:S(2)}, u32[]{:S(2)}) collective-permute-start(bf16[384,256]{1,0:T(8,128)(2,1)S(1)} %slice.245), channel_id=1, source_target_pairs={{0,448},{64,0},{128,64},{192,128},{256,192},{320,256},{384,320},{4... | collective-permute-start | bytes 589832 | tf_op jit(solution)/shard_map/ppermute | solution.py:236
  148.8 4.8 %collective-permute-start.21 = (bf16[256,512]{1,0:T(8,128)(2,1)S(1)}, bf16[256,512]{1,0:T(8,128)(2,1)S(1)}, u32[]{:S(2)}, u32[]{:S(2)}) collective-permute-start(bf16[256,512]{1,0:T(8,128)(2,1)S(1)} %shard_map.84), channel_id=1, source_target_pairs={{0,2},{2,0},{1,3},{3,1},{4,6},{6,4},{5,7},{7,5},{8,10},{10,8},{9,1... | collective-permute-start | bytes 786440 | tf_op jit(solution)/shard_map/ppermute | solution.py:22
  159.2 12.4 %collective-permute-start.22 = (bf16[8,192,512]{2,1,0:T(8,128)(2,1)S(1)}, bf16[8,192,512]{2,1,0:T(8,128)(2,1)S(1)}, u32[]{:S(2)}, u32[]{:S(2)}) collective-permute-start(bf16[8,192,512]{2,1,0:T(8,128)(2,1)S(1)} %get-tuple-element.42), channel_id=1, source_target_pairs={{0,1},{1,0},{2,3},{3,2},{4,5},{5,4},{6,7},{7,6},{8,9},{9,8},{10,11... | collective-permute-start | bytes 4718600 | tf_op jit(solution)/shard_map/ppermute | solution.py:22
  171.6 4.2 %all-to-all-start.1 = ((bf16[8,32,512]{2,1,0:T(8,128)(2,1)}), bf16[8,32,512]{2,1,0:T(8,128)(2,1)S(1)}, u32[]{:S(2)}, u32[]{:S(2)}) async-start(bf16[8,32,512]{2,1,0:T(8,128)(2,1)} %bitcast.112), calls=%async_computation.1 | async-start | bytes 524288 | tf_op jit(solution)/shard_map/all_to_all | solution.py:249
  176.9 4.2 %shard_map.87 = (bf16[512,512]{1,0:T(8,128)(2,1)}, bf16[512,512]{1,0:T(8,128)(2,1)}, bf16[512,512]{1,0:T(8,128)(2,1)}) custom-call(f32[8,192,512]{2,1,0:T(8,128)} %copy-done, bf16[8,192,512]{2,1,0:T(8,128)(2,1)} %copy-done.1), custom_call_target="tpu_custom_call" | custom-call | tf_op jit(solution)/shard_map/pallas_call | solution.py:160
  181.2 7.0 %all-to-all-done.1 = bf16[8,32,512]{2,1,0:T(8,128)(2,1)S(1)} async-done(((bf16[8,32,512]{2,1,0:T(8,128)(2,1)}), bf16[8,32,512]{2,1,0:T(8,128)(2,1)S(1)}, u32[]{:S(2)}, u32[]{:S(2)}) %all-to-all-start.1) | async-done | bytes 262176 | tf_op jit(solution)/shard_map/all_to_all | solution.py:249
  (93 shorter events, 55.4 us)
Async XLA Ops:
  2.4 24.5 %all-to-all-start = ((bf16[8,32,1024]{2,1,0:T(8,128)(2,1)}), bf16[8,32,1024]{2,1,0:T(8,128)(2,1)S(1)}, u32[]{:S(2)}, u32[]{:S(2)}) async-start(bf16[8,32,1024]{2,1,0:T(8,128)(2,1)} %broadcast_in_dim.2), calls=%async_computation | async-start | bytes 1048576 | tf_op jit(solution)/shard_map/all_to_all | solution.py:183
  10.2 12.9 %collective-permute-start.2 = (bf16[512,512]{0,1:T(8,128)(2,1)S(1)}, bf16[512,512]{0,1:T(8,128)(2,1)S(1)}, u32[]{:S(2)}, u32[]{:S(2)}) collective-permute-start(bf16[512,512]{0,1:T(8,128)(2,1)S(1)} %copy.26), channel_id=1, source_target_pairs={{0,1},{1,0},{2,3},{3,2},{4,5},{5,4},{6,7},{7,6},{8,9},{9,8},{10,11... | collective-permute-start | bytes 1572872 | tf_op jit(solution)/shard_map/ppermute | solution.py:22
  15.9 7.3 %collective-permute-start.1 = (bf16[512,512]{0,1:T(8,128)(2,1)}, bf16[512,512]{0,1:T(8,128)(2,1)}, u32[]{:S(2)}, u32[]{:S(2)}) collective-permute-start(bf16[512,512]{0,1:T(8,128)(2,1)} %copy.25), channel_id=1, source_target_pairs={{0,1},{1,0},{2,3},{3,2},{4,5},{5,4},{6,7},{7,6},{8,9},{9,8},{10,11... | collective-permute-start | bytes 1572872 | tf_op jit(solution)/shard_map/ppermute | solution.py:22
  26.9 17.0 %collective-permute-start = (bf16[256,1024]{1,0:T(8,128)(2,1)S(1)}, bf16[256,1024]{1,0:T(8,128)(2,1)S(1)}, u32[]{:S(2)}, u32[]{:S(2)}) collective-permute-start(bf16[256,1024]{1,0:T(8,128)(2,1)S(1)} %bitcast.98), channel_id=1, source_target_pairs={{0,2},{2,0},{1,3},{3,1},{4,6},{6,4},{5,7},{7,5},{8,10},{10,8},{9,1... | collective-permute-start | bytes 1572872 | tf_op jit(solution)/shard_map/ppermute | solution.py:22
  34.4 24.7 %collective-permute-start.4 = (f16[384,256]{1,0:T(8,128)(2,1)S(1)}, f16[384,256]{1,0:T(8,128)(2,1)S(1)}, u32[]{:S(2)}, u32[]{:S(2)}) collective-permute-start(f16[384,256]{1,0:T(8,128)(2,1)S(1)} %fusion.15), channel_id=1, source_target_pairs={{0,64},{64,128},{128,192},{192,256},{256,320},{320,384},{384,448},... | collective-permute-start | bytes 589832 | tf_op jit(solution)/shard_map/ppermute | solution.py:209
  44.8 16.3 %collective-permute-start.8 = (f16[384,256]{1,0:T(8,128)(2,1)S(1)}, f16[384,256]{1,0:T(8,128)(2,1)S(1)}, u32[]{:S(2)}, u32[]{:S(2)}) collective-permute-start(f16[384,256]{1,0:T(8,128)(2,1)S(1)} %fusion.16), channel_id=1, source_target_pairs={{0,448},{64,0},{128,64},{192,128},{256,192},{320,256},{384,320},{4... | collective-permute-start | bytes 589832 | tf_op jit(solution)/shard_map/ppermute | solution.py:210
  59.2 12.1 %collective-permute-start.5 = (f16[384,512]{1,0:T(8,128)(2,1)S(1)}, f16[384,512]{1,0:T(8,128)(2,1)S(1)}, u32[]{:S(2)}, u32[]{:S(2)}) collective-permute-start(f16[384,512]{1,0:T(8,128)(2,1)S(1)} %fusion.9), channel_id=1, source_target_pairs={{0,64},{64,128},{128,192},{192,256},{256,320},{320,384},{384,448},... | collective-permute-start | bytes 1179656 | tf_op jit(solution)/shard_map/ppermute | solution.py:214
  61.3 12.1 %collective-permute-start.9 = (f16[384,512]{1,0:T(8,128)(2,1)S(1)}, f16[384,512]{1,0:T(8,128)(2,1)S(1)}, u32[]{:S(2)}, u32[]{:S(2)}) collective-permute-start(f16[384,512]{1,0:T(8,128)(2,1)S(1)} %fusion.12), channel_id=1, source_target_pairs={{0,448},{64,0},{128,64},{192,128},{256,192},{320,256},{384,320},{4... | collective-permute-start | bytes 1179656 | tf_op jit(solution)/shard_map/ppermute | solution.py:215
  71.4 11.2 %collective-permute-start.6 = (f16[384,512]{1,0:T(8,128)(2,1)S(1)}, f16[384,512]{1,0:T(8,128)(2,1)S(1)}, u32[]{:S(2)}, u32[]{:S(2)}) collective-permute-start(f16[384,512]{1,0:T(8,128)(2,1)S(1)} %fusion.8), channel_id=1, source_target_pairs={{0,64},{64,128},{128,192},{192,256},{256,320},{320,384},{384,448},... | collective-permute-start | bytes 1179656 | tf_op jit(solution)/shard_map/ppermute | solution.py:214
  73.5 11.2 %collective-permute-start.10 = (f16[384,512]{1,0:T(8,128)(2,1)S(1)}, f16[384,512]{1,0:T(8,128)(2,1)S(1)}, u32[]{:S(2)}, u32[]{:S(2)}) collective-permute-start(f16[384,512]{1,0:T(8,128)(2,1)S(1)} %fusion.11), channel_id=1, source_target_pairs={{0,448},{64,0},{128,64},{192,128},{256,192},{320,256},{384,320},{4... | collective-permute-start | bytes 1179656 | tf_op jit(solution)/shard_map/ppermute | solution.py:215
  82.7 10.2 %collective-permute-start.7 = (f16[384,512]{1,0:T(8,128)(2,1)S(1)}, f16[384,512]{1,0:T(8,128)(2,1)S(1)}, u32[]{:S(2)}, u32[]{:S(2)}) collective-permute-start(f16[384,512]{1,0:T(8,128)(2,1)S(1)} %fusion.7), channel_id=1, source_target_pairs={{0,64},{64,128},{128,192},{192,256},{256,320},{320,384},{384,448},... | collective-permute-start | bytes 1179656 | tf_op jit(solution)/shard_map/ppermute | solution.py:214
  84.8 9.3 %collective-permute-start.11 = (f16[384,512]{1,0:T(8,128)(2,1)S(1)}, f16[384,512]{1,0:T(8,128)(2,1)S(1)}, u32[]{:S(2)}, u32[]{:S(2)}) collective-permute-start(f16[384,512]{1,0:T(8,128)(2,1)S(1)} %fusion.10), channel_id=1, source_target_pairs={{0,448},{64,0},{128,64},{192,128},{256,192},{320,256},{384,320},{4... | collective-permute-start | bytes 1179656 | tf_op jit(solution)/shard_map/ppermute | solution.py:215
  94.3 8.5 %collective-permute-start.12 = (f16[384,512]{1,0:T(8,128)(2,1)S(1)}, f16[384,512]{1,0:T(8,128)(2,1)S(1)}, u32[]{:S(2)}, u32[]{:S(2)}) collective-permute-start(f16[384,512]{1,0:T(8,128)(2,1)S(1)} %fusion.34), channel_id=1, source_target_pairs={{0,32},{32,0},{1,33},{33,1},{2,34},{34,2},{3,35},{35,3},{4,36},{36... | collective-permute-start | bytes 1179656 | tf_op jit(solution)/shard_map/ppermute | solution.py:22
  103.5 10.2 %collective-permute-start.16 = (bf16[384,512]{1,0:T(8,128)(2,1)S(1)}, bf16[384,512]{1,0:T(8,128)(2,1)S(1)}, u32[]{:S(2)}, u32[]{:S(2)}) collective-permute-start(bf16[384,512]{1,0:T(8,128)(2,1)S(1)} %pad_maximum_fusion.2.refs_0_), channel_id=1, source_target_pairs={{0,64},{64,128},{128,192},{192,256},{256,320},{320,384},{384,448},... | collective-permute-start | bytes 1179656 | tf_op jit(solution)/shard_map/ppermute | solution.py:231
  105.4 10.2 %collective-permute-start.13 = (bf16[384,512]{1,0:T(8,128)(2,1)S(1)}, bf16[384,512]{1,0:T(8,128)(2,1)S(1)}, u32[]{:S(2)}, u32[]{:S(2)}) collective-permute-start(bf16[384,512]{1,0:T(8,128)(2,1)S(1)} %pad_maximum_fusion.2.refs_0_), channel_id=1, source_target_pairs={{0,448},{64,0},{128,64},{192,128},{256,192},{320,256},{384,320},{4... | collective-permute-start | bytes 1179656 | tf_op jit(solution)/shard_map/ppermute | solution.py:232
  113.7 10.4 %collective-permute-start.17 = (bf16[384,512]{1,0:T(8,128)(2,1)S(1)}, bf16[384,512]{1,0:T(8,128)(2,1)S(1)}, u32[]{:S(2)}, u32[]{:S(2)}) collective-permute-start(bf16[384,512]{1,0:T(8,128)(2,1)S(1)} %collective-permute-done.16.refs_7_), channel_id=1, source_target_pairs={{0,64},{64,128},{128,192},{192,256},{256,320},{320,384},{384,448},... | collective-permute-start | bytes 1179656 | tf_op jit(solution)/shard_map/ppermute | solution.py:231
  115.6 10.4 %collective-permute-start.14 = (bf16[384,512]{1,0:T(8,128)(2,1)S(1)}, bf16[384,512]{1,0:T(8,128)(2,1)S(1)}, u32[]{:S(2)}, u32[]{:S(2)}) collective-permute-start(bf16[384,512]{1,0:T(8,128)(2,1)S(1)} %collective-permute-done.13.refs_1_), channel_id=1, source_target_pairs={{0,448},{64,0},{128,64},{192,128},{256,192},{320,256},{384,320},{4... | collective-permute-start | bytes 1179656 | tf_op jit(solution)/shard_map/ppermute | solution.py:232
  124.1 11.8 %collective-permute-start.18 = (bf16[384,512]{1,0:T(8,128)(2,1)S(1)}, bf16[384,512]{1,0:T(8,128)(2,1)S(1)}, u32[]{:S(2)}, u32[]{:S(2)}) collective-permute-start(bf16[384,512]{1,0:T(8,128)(2,1)S(1)} %collective-permute-done.17.refs_6_), channel_id=1, source_target_pairs={{0,64},{64,128},{128,192},{192,256},{256,320},{320,384},{384,448},... | collective-permute-start | bytes 1179656 | tf_op jit(solution)/shard_map/ppermute | solution.py:231
  126.1 11.8 %collective-permute-start.15 = (bf16[384,512]{1,0:T(8,128)(2,1)S(1)}, bf16[384,512]{1,0:T(8,128)(2,1)S(1)}, u32[]{:S(2)}, u32[]{:S(2)}) collective-permute-start(bf16[384,512]{1,0:T(8,128)(2,1)S(1)} %collective-permute-done.14.refs_2_), channel_id=1, source_target_pairs={{0,448},{64,0},{128,64},{192,128},{256,192},{320,256},{384,320},{4... | collective-permute-start | bytes 1179656 | tf_op jit(solution)/shard_map/ppermute | solution.py:232
  136.0 10.0 %collective-permute-start.19 = (bf16[384,256]{1,0:T(8,128)(2,1)S(1)}, bf16[384,256]{1,0:T(8,128)(2,1)S(1)}, u32[]{:S(2)}, u32[]{:S(2)}) collective-permute-start(bf16[384,256]{1,0:T(8,128)(2,1)S(1)} %slice.244), channel_id=1, source_target_pairs={{0,64},{64,128},{128,192},{192,256},{256,320},{320,384},{384,448},... | collective-permute-start | bytes 589832 | tf_op jit(solution)/shard_map/ppermute | solution.py:235
  137.9 9.5 %collective-permute-start.20 = (bf16[384,256]{1,0:T(8,128)(2,1)S(1)}, bf16[384,256]{1,0:T(8,128)(2,1)S(1)}, u32[]{:S(2)}, u32[]{:S(2)}) collective-permute-start(bf16[384,256]{1,0:T(8,128)(2,1)S(1)} %slice.245), channel_id=1, source_target_pairs={{0,448},{64,0},{128,64},{192,128},{256,192},{320,256},{384,320},{4... | collective-permute-start | bytes 589832 | tf_op jit(solution)/shard_map/ppermute | solution.py:236
  148.8 9.6 %collective-permute-start.21 = (bf16[256,512]{1,0:T(8,128)(2,1)S(1)}, bf16[256,512]{1,0:T(8,128)(2,1)S(1)}, u32[]{:S(2)}, u32[]{:S(2)}) collective-permute-start(bf16[256,512]{1,0:T(8,128)(2,1)S(1)} %shard_map.84), channel_id=1, source_target_pairs={{0,2},{2,0},{1,3},{3,1},{4,6},{6,4},{5,7},{7,5},{8,10},{10,8},{9,1... | collective-permute-start | bytes 786440 | tf_op jit(solution)/shard_map/ppermute | solution.py:22
  159.2 16.6 %collective-permute-start.22 = (bf16[8,192,512]{2,1,0:T(8,128)(2,1)S(1)}, bf16[8,192,512]{2,1,0:T(8,128)(2,1)S(1)}, u32[]{:S(2)}, u32[]{:S(2)}) collective-permute-start(bf16[8,192,512]{2,1,0:T(8,128)(2,1)S(1)} %get-tuple-element.42), channel_id=1, source_target_pairs={{0,1},{1,0},{2,3},{3,2},{4,5},{5,4},{6,7},{7,6},{8,9},{9,8},{10,11... | collective-permute-start | bytes 4718600 | tf_op jit(solution)/shard_map/ppermute | solution.py:22
  171.6 16.6 %all-to-all-start.1 = ((bf16[8,32,512]{2,1,0:T(8,128)(2,1)}), bf16[8,32,512]{2,1,0:T(8,128)(2,1)S(1)}, u32[]{:S(2)}, u32[]{:S(2)}) async-start(bf16[8,32,512]{2,1,0:T(8,128)(2,1)} %bitcast.112), calls=%async_computation.1 | async-start | bytes 524288 | tf_op jit(solution)/shard_map/all_to_all | solution.py:249
  (6 other events, 44.9 us)

commit v5 on v2

v5 whole, which is shorter than its diff:
```python
import functools

import jax
import jax.numpy as jnp
from jax import lax
from jax.experimental import pallas as pl
from jax.experimental.pallas import tpu as pltpu
from jax.sharding import Mesh
from jax.sharding import PartitionSpec as P

AXES = ("z", "xl", "y", "xh", "core")
GX, GY = ("z", "xl"), ("y", "xh", "core")
SCALE = 16.0
F32, BF16, F16 = jnp.float32, jnp.bfloat16, jnp.float16


def dot(a, b, ca, cb):
    return lax.dot_general(a, b, (((ca,), (cb,)), ((), ())), preferred_element_type=F32)


def swap(x, axis):
    return lax.ppermute(x, axis, [(0, 1), (1, 0)])


def tie(*arrays):
    return lax.optimization_barrier(arrays)


def turn(x, by):
    n = x.shape[0]
    return lax.dynamic_slice_in_dim(jnp.concatenate([x, x], axis=0), by, n, axis=0)


def input_kernel(nz, at, *refs):
    chunks, (own_ref, oth_ref, out_ref) = refs[:nz], refs[nz:]
    n, h, step = out_ref.shape[0], own_ref.shape[1], chunks[0].shape[0] // 2
    total = jnp.zeros(out_ref.shape, F32)
    for k in range(nz):
        for i, ref in enumerate((own_ref, oth_ref)):
            deltas = chunks[k][i * step : i * step + h, at : at + n]
            total += lax.dot_general(
                deltas, ref[k], (((0,), (0,)), ((), ())), preferred_element_type=F32
            )
    out_ref[...] = total.astype(out_ref.dtype)


def input_grads(chunks, own, oth, at, n, dtype):
    return pl.pallas_call(
        functools.partial(input_kernel, len(chunks), at),
        out_shape=jax.ShapeDtypeStruct((n, own.shape[2]), dtype),
        compiler_params=pltpu.CompilerParams(vmem_limit_bytes=40 * 2**20),
    )(*chunks, own, oth)


def grads_kernel(order, zf, *refs):
    nz = len(order)
    chunks, (got_ref, x_ref, c_ref, xo_ref, co_ref, gate_ref, up_ref, down_ref, sums) = refs[:nz], refs[nz:]
    z = lax.axis_index("z")
    n = 2 * zf
    for k in range(nz):
        gu = jnp.dot(chunks[k][:n, :], x_ref[...], preferred_element_type=F32)
        gu += jnp.dot(got_ref[k, :n, :], xo_ref[...], preferred_element_type=F32)
        dn = jnp.dot(chunks[k][n : n + zf, :], c_ref[...], preferred_element_type=F32)
        dn += jnp.dot(got_ref[k, n:, :], co_ref[...], preferred_element_type=F32)
        at = lax.rem(z + order[k], nz)
        sums[at, :n, :] = gu.astype(BF16)
        sums[at, n:, :] = dn.astype(BF16)
    for i in range(0, nz, 2):
        at = pl.ds(i * zf, 2 * zf)
        gate_ref[:, at] = jnp.concatenate([sums[i, :zf, :], sums[i + 1, :zf, :]], axis=0).T
        up_ref[:, at] = jnp.concatenate([sums[i, zf:n, :], sums[i + 1, zf:n, :]], axis=0).T
        down_ref[at, :] = jnp.concatenate([sums[i, n:, :], sums[i + 1, n:, :]], axis=0)


def weight_grads(chunks, order, got, tokens, zf):
    nz, width = len(chunks), tokens[0].shape[1]
    return pl.pallas_call(
        functools.partial(grads_kernel, order, zf),
        out_shape=[
            jax.ShapeDtypeStruct((width, nz * zf), BF16),
            jax.ShapeDtypeStruct((width, nz * zf), BF16),
            jax.ShapeDtypeStruct((nz * zf, width), BF16),
        ],
        scratch_shapes=[pltpu.VMEM((nz, 3 * zf, width), BF16)],
        compiler_params=pltpu.CompilerParams(vmem_limit_bytes=40 * 2**20),
    )(*chunks, got, *tokens)


def per_device(nz, ny, x, wg, wu, wd, c):
    rows, width = x.shape
    fwidth = wg.shape[1]
    zf = fwidth // nz
    z = lax.axis_index("z")
    right = [(i, (i + 1) % nz) for i in range(nz)]
    left = [(i, (i - 1) % nz) for i in range(nz)]

    pair = jnp.concatenate([x, c], axis=1)
    pair = jnp.broadcast_to(pair[None], (ny,) + pair.shape)
    pair = lax.all_to_all(pair, "y", 0, 0, tiled=True).reshape(ny * rows, 2 * width)
    pair, wg_oth, wu_oth, wd_oth = tie(pair, swap(wg, "core"), swap(wu, "core"), swap(wd, "core"))
    other = swap(pair, "xh")
    part_tokens = pair.shape[0]
    x0, c0 = pair[:, :width], pair[:, width:]
    half = 2 * part_tokens

    def by_z(*weights):
        return turn(jnp.stack([w.reshape(nz, zf, width) for w in weights], axis=1), z).reshape(nz, -1, width)

    gu_own, gu_oth = by_z(wg.T, wu.T), by_z(wg_oth.T, wu_oth.T)
    d_own, d_oth = by_z(wd), by_z(wd_oth)
    far = nz // 2

    def part_far(t, u):
        halves = [(gu_own, t), (d_own, u), (gu_oth, t), (d_oth, u)]
        return jnp.concatenate([dot(w[far], v, 1, 1) for w, v in halves], axis=0) * SCALE

    def products(t, u):
        pairs = ((gu_own, t), (d_own, u), (gu_oth, t), (d_oth, u))
        return [(dot(w.reshape(-1, width), v, 1, 1) * SCALE).reshape(nz, -1, part_tokens) for w, v in pairs]

    first = products(x0, c0)
    other, *first = tie(other, *first)
    x1, c1 = other[:, :width], other[:, width:]
    xs, cs = jnp.concatenate([x0, x1], axis=0), jnp.concatenate([c0, c1], axis=0)
    parts = list(zip(first, products(x1, c1)))

    def half_part(i, k):
        return jnp.concatenate([p[i][k] for p in parts], axis=0)

    def part(k):
        return jnp.concatenate([half_part(0, k), half_part(1, k)], axis=1)

    r = lax.ppermute(part_far(x0, c0).astype(F16), "z", right).astype(F32)
    l = lax.ppermute(half_part(1, far).astype(F16), "z", left).astype(F32)
    r = jnp.pad(r, ((0, 0), (0, part_tokens)))
    l = jnp.pad(l, ((0, 0), (part_tokens, 0)))
    for k in range(far - 1, 0, -1):
        r = lax.ppermute((part(k) + r).astype(F16), "z", right).astype(F32)
        l = lax.ppermute((part(nz - k) + l).astype(F16), "z", left).astype(F32)
    total = part(0) + r + l
    got = swap(total.astype(F16), "xl")
    tokens_oth = swap(jnp.stack([xs, cs]), "core")
    got, tokens_oth = tie(got, tokens_oth)
    total = ((total + got.astype(F32)) * (1.0 / SCALE)).reshape(2, 3, zf, half)
    gate, upper, hidden_grad = total[:, 0], total[:, 1], total[:, 2]

    sig = jax.nn.sigmoid(gate)
    hidden = (gate * sig * upper).astype(BF16)
    gate_delta = (hidden_grad * upper * sig * (1.0 + gate * (1.0 - sig))).astype(BF16)
    up_delta = (hidden_grad * gate * sig).astype(BF16)

    chunk = [None] * nz
    chunk[0] = jnp.stack([gate_delta, up_delta, hidden], axis=1).reshape(6 * zf, half)
    for k in range(1, far):
        chunk[nz - k] = lax.ppermute(chunk[(nz - k + 1) % nz], "z", right)
        chunk[k] = lax.ppermute(chunk[k - 1], "z", left)
    chunk[far] = jnp.concatenate(
        [
            lax.ppermute(chunk[far + 1][:, :part_tokens], "z", right),
            lax.ppermute(chunk[far - 1][:, part_tokens:], "z", left),
        ],
        axis=1,
    )

    order = [0] + [j for i in range(1, far) for j in (nz - i, i)] + [far]
    deltas = jnp.stack([chunk[k][3 * zf :] for k in order[:-1]])
    chunk[far], deltas = tie(chunk[far], deltas)
    send = input_grads(chunk, gu_own, gu_oth, part_tokens, part_tokens, BF16)
    send, *chunk = tie(send, *chunk)
    got = swap(send, "xh")
    total = input_grads(chunk, gu_own, gu_oth, 0, part_tokens, F32)
    deltas = jnp.concatenate([deltas, chunk[far][None, 3 * zf :]], axis=0)
    got, total, deltas = tie(got, total, deltas)
    deltas = swap(deltas, "core")
    total = (total + got.astype(F32)).astype(BF16).reshape(ny, rows, width)
    recv = lax.all_to_all(total, "y", 0, 0, tiled=True)
    tokens = (xs, cs, tokens_oth[0], tokens_oth[1])
    gate_grad, up_grad, down_grad = weight_grads([chunk[k] for k in order], order, deltas, tokens, zf)
    recv, gate_grad, up_grad, down_grad = tie(recv, gate_grad, up_grad, down_grad)
    input_grad = recv.astype(F32).sum(0).astype(BF16)
    return (input_grad, gate_grad, up_grad, down_grad)


def solution(mesh):
    nz, ny = mesh.shape["gx"] // 2, mesh.shape["gy"] // 4
    grid = Mesh(mesh.devices.reshape(nz, 2, ny, 2, 2), AXES)
    in_specs = (P(GY, GX), P(GX, GY), P(GX, GY), P(GY, GX), P(GY, GX))
    out_specs = (P(GY, GX), P(GX, GY), P(GX, GY), P(GY, GX))
    return jax.shard_map(
        lambda *args: per_device(nz, ny, *args),
        mesh=grid,
        in_specs=in_specs,
        out_specs=out_specs,
        check_vma=False,
    )
```

time: 211 us -> 189 us (0.90)
  waiting for transfers between devices: 70.2 us -> 42.9 us
  starting transfers between devices: 103 us -> 114 us
  Pallas kernels: 0 us -> 8.12 us
  local copies, waits for them, and re-layouts: 11.9 us -> 5 us
  matrix products: 9.26 us -> 4.05 us
    all_to_all x2, waiting for transfers between devices: 28.2 us -> 5.53 us  [the longest x1 5.18 us: per_device(): recv = lax.all_to_all(total, 'y', 0, 0, tiled=True)]
    ppermute x6 -> x8, starting transfers between devices: 27.9 us -> 40.3 us  [swap(): return lax.ppermute(x, axis, [(0, 1), (1, 0)])]
    ppermute x3, waiting for transfers between devices: 12 us -> 0.01 us  [per_device(): chunk[k] = lax.ppermute(chunk[k - 1], 'z', left)]
    ppermute x3, waiting for transfers between devices: 0.02 us -> 10.6 us  [per_device(): chunk[nz - k] = lax.ppermute(chunk[(nz - k + 1) % nz], 'z', right)]
    pallas_call x0 -> x3, Pallas kernels: none -> 8.12 us  [the longest x1 5.6 us: weight_grads(): pl.pallas_call(functools.partial(grads_kernel, order, zf), out_shape=[jax...]
    ppermute x4, waiting for transfers between devices: 10.3 us -> 3.27 us  [the longest x1 1.7 us: per_device(): lax.ppermute(chunk[far - 1][:, part_tokens:], 'z', left)]
    ppermute x6 -> x8, waiting for transfers between devices: 6.29 us -> 12.2 us  [swap(): return lax.ppermute(x, axis, [(0, 1), (1, 0)])]
    dot_general x12, matrix products: 9.26 us -> 4.05 us  [dot(): lax.dot_general(a, b, (((ca,), (cb,)), ((), ())), preferred_element_type=...]
  transfers between devices with their start and end apart: 24 -> 26, of which waited for: 12 -> 14; matrix products, arithmetic and copies ran while one was open for 8% -> 9% of each run, Pallas kernels for 0% -> 4%
where the time goes in v5:
time: 189 us; the launch traced here: 188 us
  starting transfers between devices  114 us (60%)
  waiting for transfers between devices  42.9 us (23%)
  other arithmetic  12.5 us (7%)
  Pallas kernels  8.12 us (4%)
  local copies, waits for them, and re-layouts  5 us (3%)
  matrix products  4.05 us (2%)
    ppermute x8, starting transfers between devices, swap(): return lax.ppermute(x, axis, [(0, 1), (1, 0)])  40.3 us
    ppermute x3, starting transfers between devices, per_device(): l = lax.ppermute((part(nz - k) + l).astype(F16), 'z', left).astype(F32)  15.1 us
    ppermute x3, starting transfers between devices, per_device(): chunk[k] = lax.ppermute(chunk[k - 1], 'z', left)  14 us
    ppermute x8, waiting for transfers between devices, swap(): return lax.ppermute(x, axis, [(0, 1), (1, 0)])  12.2 us
    ppermute x1, starting transfers between devices, per_device(): l = lax.ppermute(half_part(1, far).astype(F16), 'z', left).astype(F32)  11.1 us
    ppermute x3, waiting for transfers between devices, per_device(): chunk[nz - k] = lax.ppermute(chunk[(nz - k + 1) % nz], 'z', right)  10.6 us
    ppermute x3, waiting for transfers between devices, per_device(): r = lax.ppermute((part(k) + r).astype(F16), 'z', right).astype(F32)  10.5 us
    all_to_all x1, starting transfers between devices, per_device(): lax.all_to_all(pair, 'y', 0, 0, tiled=True).reshape(ny * rows, 2 * width)  7.65 us
  transfers between devices with their start and end apart: 26, of which 14 were waited for; matrix products, arithmetic and copies ran while one was open for 9% of the time, Pallas kernels for 4%

profile of v5, /device:TPU:1, one launch (start us, length us, event | category | flops | bytes accessed | tf_op | source)
XLA Modules:
  0.0 187.8 jit_solution(15644847242725441990)
XLA Ops:
  2.3 7.7 %all-to-all-start = ((bf16[8,32,1024]{2,1,0:T(8,128)(2,1)}), bf16[8,32,1024]{2,1,0:T(8,128)(2,1)S(1)}, u32[]{:S(2)}, u32[]{:S(2)}) async-start(bf16[8,32,1024]{2,1,0:T(8,128)(2,1)} %broadcast_in_dim.4), calls=%async_computation | async-start | bytes 1048576 | tf_op jit(solution)/shard_map/all_to_all | solution.py:99
  11.0 4.6 %collective-permute-start.1 = (bf16[512,512]{0,1:T(8,128)(2,1)}, bf16[512,512]{0,1:T(8,128)(2,1)}, u32[]{:S(2)}, u32[]{:S(2)}) collective-permute-start(bf16[512,512]{0,1:T(8,128)(2,1)} %copy.20), channel_id=1, source_target_pairs={{0,1},{1,0},{2,3},{3,2},{4,5},{5,4},{6,7},{7,6},{8,9},{9,8},{10,11... | collective-permute-start | bytes 1572872 | tf_op jit(solution)/shard_map/ppermute | solution.py:22
  26.6 8.0 %collective-permute-start.3 = (bf16[256,1024]{1,0:T(8,128)(2,1)S(1)}, bf16[256,1024]{1,0:T(8,128)(2,1)S(1)}, u32[]{:S(2)}, u32[]{:S(2)}) collective-permute-start(bf16[256,1024]{1,0:T(8,128)(2,1)S(1)} %bitcast.150), channel_id=1, source_target_pairs={{0,2},{2,0},{1,3},{3,1},{4,6},{6,4},{5,7},{7,5},{8,10},{10,8},{9,1... | collective-permute-start | bytes 1572872 | tf_op jit(solution)/shard_map/ppermute | solution.py:22
  36.8 4.0 %collective-permute-start.4 = (f16[384,256]{1,0:T(8,128)(2,1)S(1)}, f16[384,256]{1,0:T(8,128)(2,1)S(1)}, u32[]{:S(2)}, u32[]{:S(2)}) collective-permute-start(f16[384,256]{1,0:T(8,128)(2,1)S(1)} %fusion.15), channel_id=1, source_target_pairs={{0,64},{64,128},{128,192},{192,256},{256,320},{320,384},{384,448},... | collective-permute-start | bytes 589832 | tf_op jit(solution)/shard_map/ppermute | solution.py:133
  42.4 3.5 %collective-permute-done.3 = bf16[256,1024]{1,0:T(8,128)(2,1)S(1)} collective-permute-done((bf16[256,1024]{1,0:T(8,128)(2,1)S(1)}, bf16[256,1024]{1,0:T(8,128)(2,1)S(1)}, u32[]{:S(2)}, u32[]{:S(2)}) %collective-permute-start.3) | collective-permute-done | bytes 524320 | tf_op jit(solution)/shard_map/ppermute | solution.py:22
  47.8 11.1 %collective-permute-start.8 = (f16[384,256]{1,0:T(8,128)(2,1)S(1)}, f16[384,256]{1,0:T(8,128)(2,1)S(1)}, u32[]{:S(2)}, u32[]{:S(2)}) collective-permute-start(f16[384,256]{1,0:T(8,128)(2,1)S(1)} %pad_maximum_fusion.6), channel_id=1, source_target_pairs={{0,448},{64,0},{128,64},{192,128},{256,192},{320,256},{384,320},{4... | collective-permute-start | bytes 589832 | tf_op jit(solution)/shard_map/ppermute | solution.py:134
  61.9 5.3 %collective-permute-start.9 = (f16[384,512]{1,0:T(8,128)(2,1)S(1)}, f16[384,512]{1,0:T(8,128)(2,1)S(1)}, u32[]{:S(2)}, u32[]{:S(2)}) collective-permute-start(f16[384,512]{1,0:T(8,128)(2,1)S(1)} %fusion.12), channel_id=1, source_target_pairs={{0,448},{64,0},{128,64},{192,128},{256,192},{320,256},{384,320},{4... | collective-permute-start | bytes 1179656 | tf_op jit(solution)/shard_map/ppermute | solution.py:139
  67.3 4.1 %collective-permute-done.5 = f16[384,512]{1,0:T(8,128)(2,1)S(1)} collective-permute-done((f16[384,512]{1,0:T(8,128)(2,1)S(1)}, f16[384,512]{1,0:T(8,128)(2,1)S(1)}, u32[]{:S(2)}, u32[]{:S(2)}) %collective-permute-start.5) | collective-permute-done | bytes 393248 | tf_op jit(solution)/shard_map/ppermute | solution.py:138
  73.6 5.2 %collective-permute-start.10 = (f16[384,512]{1,0:T(8,128)(2,1)S(1)}, f16[384,512]{1,0:T(8,128)(2,1)S(1)}, u32[]{:S(2)}, u32[]{:S(2)}) collective-permute-start(f16[384,512]{1,0:T(8,128)(2,1)S(1)} %fusion.11), channel_id=1, source_target_pairs={{0,448},{64,0},{128,64},{192,128},{256,192},{320,256},{384,320},{4... | collective-permute-start | bytes 1179656 | tf_op jit(solution)/shard_map/ppermute | solution.py:139
  80.0 5.4 %collective-permute-start.13 = (bf16[2,512,512]{2,1,0:T(8,128)(2,1)S(1)}, bf16[2,512,512]{2,1,0:T(8,128)(2,1)S(1)}, u32[]{:S(2)}, u32[]{:S(2)}) collective-permute-start(bf16[2,512,512]{2,1,0:T(8,128)(2,1)S(1)} %pad_maximum_fusion.1), channel_id=1, source_target_pairs={{0,1},{1,0},{2,3},{3,2},{4,5},{5,4},{6,7},{7,6},{8,9},{9,8},{10,11... | collective-permute-start | bytes 3145736 | tf_op jit(solution)/shard_map/ppermute | solution.py:22
  87.6 4.6 %collective-permute-start.11 = (f16[384,512]{1,0:T(8,128)(2,1)S(1)}, f16[384,512]{1,0:T(8,128)(2,1)S(1)}, u32[]{:S(2)}, u32[]{:S(2)}) collective-permute-start(f16[384,512]{1,0:T(8,128)(2,1)S(1)} %fusion.10), channel_id=1, source_target_pairs={{0,448},{64,0},{128,64},{192,128},{256,192},{320,256},{384,320},{4... | collective-permute-start | bytes 1179656 | tf_op jit(solution)/shard_map/ppermute | solution.py:139
  92.2 6.4 %collective-permute-done.7 = f16[384,512]{1,0:T(8,128)(2,1)S(1)} collective-permute-done((f16[384,512]{1,0:T(8,128)(2,1)S(1)}, f16[384,512]{1,0:T(8,128)(2,1)S(1)}, u32[]{:S(2)}, u32[]{:S(2)}) %collective-permute-start.7) | collective-permute-done | bytes 393248 | tf_op jit(solution)/shard_map/ppermute | solution.py:138
  102.7 7.3 %collective-permute-done.12 = f16[384,512]{1,0:T(8,128)(2,1)S(1)} collective-permute-done((f16[384,512]{1,0:T(8,128)(2,1)S(1)}, f16[384,512]{1,0:T(8,128)(2,1)S(1)}, u32[]{:S(2)}, u32[]{:S(2)}) %collective-permute-start.12) | collective-permute-done | bytes 393248 | tf_op jit(solution)/shard_map/ppermute | solution.py:22
  112.4 4.9 %collective-permute-start.14 = (bf16[384,512]{1,0:T(8,128)(2,1)S(1)}, bf16[384,512]{1,0:T(8,128)(2,1)S(1)}, u32[]{:S(2)}, u32[]{:S(2)}) collective-permute-start(bf16[384,512]{1,0:T(8,128)(2,1)S(1)} %bitcast.146), channel_id=1, source_target_pairs={{0,448},{64,0},{128,64},{192,128},{256,192},{320,256},{384,320},{4... | collective-permute-start | bytes 1179656 | tf_op jit(solution)/shard_map/ppermute | solution.py:156
  117.3 4.2 %collective-permute-done.17.refs_7_.refs_1_ = bf16[384,512]{1,0:T(8,128)(2,1)S(1)} collective-permute-done((bf16[384,512]{1,0:T(8,128)(2,1)S(1)}, bf16[384,512]{1,0:T(8,128)(2,1)S(1)}, u32[]{:S(2)}, u32[]{:S(2)}) %collective-permute-start.17) | collective-permute-done | bytes 393248 | tf_op jit(solution)/shard_map/ppermute | solution.py:155
  123.4 4.6 %collective-permute-start.15 = (bf16[384,512]{1,0:T(8,128)(2,1)S(1)}, bf16[384,512]{1,0:T(8,128)(2,1)S(1)}, u32[]{:S(2)}, u32[]{:S(2)}) collective-permute-start(bf16[384,512]{1,0:T(8,128)(2,1)S(1)} %collective-permute-done.14.refs_1_.refs_2_), channel_id=1, source_target_pairs={{0,448},{64,0},{128,64},{192,128},{256,192},{320,256},{384,320},{4... | collective-permute-start | bytes 1179656 | tf_op jit(solution)/shard_map/ppermute | solution.py:156
  128.1 3.2 %collective-permute-done.18.refs_6_.refs_3_ = bf16[384,512]{1,0:T(8,128)(2,1)S(1)} collective-permute-done((bf16[384,512]{1,0:T(8,128)(2,1)S(1)}, bf16[384,512]{1,0:T(8,128)(2,1)S(1)}, u32[]{:S(2)}, u32[]{:S(2)}) %collective-permute-start.18) | collective-permute-done | bytes 393248 | tf_op jit(solution)/shard_map/ppermute | solution.py:155
  133.2 4.6 %collective-permute-start.16 = (bf16[384,512]{1,0:T(8,128)(2,1)S(1)}, bf16[384,512]{1,0:T(8,128)(2,1)S(1)}, u32[]{:S(2)}, u32[]{:S(2)}) collective-permute-start(bf16[384,512]{1,0:T(8,128)(2,1)S(1)} %collective-permute-done.15.refs_2_.refs_4_), channel_id=1, source_target_pairs={{0,448},{64,0},{128,64},{192,128},{256,192},{320,256},{384,320},{4... | collective-permute-start | bytes 1179656 | tf_op jit(solution)/shard_map/ppermute | solution.py:156
  142.9 4.6 %collective-permute-start.21 = (bf16[384,256]{1,0:T(8,128)(2,1)S(1)}, bf16[384,256]{1,0:T(8,128)(2,1)S(1)}, u32[]{:S(2)}, u32[]{:S(2)}) collective-permute-start(bf16[384,256]{1,0:T(8,128)(2,1)S(1)} %slice.413), channel_id=1, source_target_pairs={{0,448},{64,0},{128,64},{192,128},{256,192},{320,256},{384,320},{4... | collective-permute-start | bytes 589832 | tf_op jit(solution)/shard_map/ppermute | solution.py:160
  151.6 4.6 %collective-permute-start.22 = (bf16[256,512]{1,0:T(8,128)(2,1)S(1)}, bf16[256,512]{1,0:T(8,128)(2,1)S(1)}, u32[]{:S(2)}, u32[]{:S(2)}) collective-permute-start(bf16[256,512]{1,0:T(8,128)(2,1)S(1)} %shard_map.84), channel_id=1, source_target_pairs={{0,2},{2,0},{1,3},{3,1},{4,6},{6,4},{5,7},{7,5},{8,10},{10,8},{9,1... | collective-permute-start | bytes 786440 | tf_op jit(solution)/shard_map/ppermute | solution.py:22
  160.2 10.2 %collective-permute-start.23 = (bf16[8,192,512]{2,1,0:T(8,128)(2,1)}, bf16[8,192,512]{2,1,0:T(8,128)(2,1)}, u32[]{:S(2)}, u32[]{:S(2)}) collective-permute-start(bf16[8,192,512]{2,1,0:T(8,128)(2,1)} %pad_maximum_fusion), channel_id=1, source_target_pairs={{0,1},{1,0},{2,3},{3,2},{4,5},{5,4},{6,7},{7,6},{8,9},{9,8},{10,11... | collective-permute-start | bytes 4718600 | tf_op jit(solution)/shard_map/ppermute | solution.py:22
  171.2 3.5 %all-to-all-start.1 = ((bf16[8,32,512]{2,1,0:T(8,128)(2,1)}), bf16[8,32,512]{2,1,0:T(8,128)(2,1)S(1)}, u32[]{:S(2)}, u32[]{:S(2)}) async-start(bf16[8,32,512]{2,1,0:T(8,128)(2,1)} %bitcast.170), calls=%async_computation.1 | async-start | bytes 524288 | tf_op jit(solution)/shard_map/all_to_all | solution.py:176
  176.3 5.6 %shard_map.86 = (bf16[512,512]{1,0:T(8,128)(2,1)}, bf16[512,512]{1,0:T(8,128)(2,1)}, bf16[512,512]{1,0:T(8,128)(2,1)}) custom-call(bf16[384,512]{1,0:T(8,128)(2,1)S(1)} %bitcast.149, bf16[384,512]{1,0:T(8,128)(2,1)S(1)} %collective-permute-done.17.refs_7_.refs_1_, bf16[384,512]{1,0:T(8,128)(2,1)S(1)} %collective-permute-done.14.refs_1_.refs_2_, ...), custom_call_target="tpu_custom_call" | custom-call | tf_op jit(solution)/shard_map/pallas_call | solution.py:77
  181.9 5.2 %all-to-all-done.1 = bf16[8,32,512]{2,1,0:T(8,128)(2,1)S(1)} async-done(((bf16[8,32,512]{2,1,0:T(8,128)(2,1)}), bf16[8,32,512]{2,1,0:T(8,128)(2,1)S(1)}, u32[]{:S(2)}, u32[]{:S(2)}) %all-to-all-start.1) | async-done | bytes 262176 | tf_op jit(solution)/shard_map/all_to_all | solution.py:176
  (112 shorter events, 53.9 us)
Async XLA Ops:
  2.3 22.4 %all-to-all-start = ((bf16[8,32,1024]{2,1,0:T(8,128)(2,1)}), bf16[8,32,1024]{2,1,0:T(8,128)(2,1)S(1)}, u32[]{:S(2)}, u32[]{:S(2)}) async-start(bf16[8,32,1024]{2,1,0:T(8,128)(2,1)} %broadcast_in_dim.4), calls=%async_computation | async-start | bytes 1048576 | tf_op jit(solution)/shard_map/all_to_all | solution.py:99
  11.0 13.4 %collective-permute-start.1 = (bf16[512,512]{0,1:T(8,128)(2,1)}, bf16[512,512]{0,1:T(8,128)(2,1)}, u32[]{:S(2)}, u32[]{:S(2)}) collective-permute-start(bf16[512,512]{0,1:T(8,128)(2,1)} %copy.20), channel_id=1, source_target_pairs={{0,1},{1,0},{2,3},{3,2},{4,5},{5,4},{6,7},{7,6},{8,9},{9,8},{10,11... | collective-permute-start | bytes 1572872 | tf_op jit(solution)/shard_map/ppermute | solution.py:22
  16.7 7.7 %collective-permute-start = (bf16[512,512]{0,1:T(8,128)(2,1)}, bf16[512,512]{0,1:T(8,128)(2,1)}, u32[]{:S(2)}, u32[]{:S(2)}) collective-permute-start(bf16[512,512]{0,1:T(8,128)(2,1)} %copy.19), channel_id=1, source_target_pairs={{0,1},{1,0},{2,3},{3,2},{4,5},{5,4},{6,7},{7,6},{8,9},{9,8},{10,11... | collective-permute-start | bytes 1572872 | tf_op jit(solution)/shard_map/ppermute | solution.py:22
  26.6 19.3 %collective-permute-start.3 = (bf16[256,1024]{1,0:T(8,128)(2,1)S(1)}, bf16[256,1024]{1,0:T(8,128)(2,1)S(1)}, u32[]{:S(2)}, u32[]{:S(2)}) collective-permute-start(bf16[256,1024]{1,0:T(8,128)(2,1)S(1)} %bitcast.150), channel_id=1, source_target_pairs={{0,2},{2,0},{1,3},{3,1},{4,6},{6,4},{5,7},{7,5},{8,10},{10,8},{9,1... | collective-permute-start | bytes 1572872 | tf_op jit(solution)/shard_map/ppermute | solution.py:22
  36.8 22.5 %collective-permute-start.4 = (f16[384,256]{1,0:T(8,128)(2,1)S(1)}, f16[384,256]{1,0:T(8,128)(2,1)S(1)}, u32[]{:S(2)}, u32[]{:S(2)}) collective-permute-start(f16[384,256]{1,0:T(8,128)(2,1)S(1)} %fusion.15), channel_id=1, source_target_pairs={{0,64},{64,128},{128,192},{192,256},{256,320},{320,384},{384,448},... | collective-permute-start | bytes 589832 | tf_op jit(solution)/shard_map/ppermute | solution.py:133
  47.8 14.0 %collective-permute-start.8 = (f16[384,256]{1,0:T(8,128)(2,1)S(1)}, f16[384,256]{1,0:T(8,128)(2,1)S(1)}, u32[]{:S(2)}, u32[]{:S(2)}) collective-permute-start(f16[384,256]{1,0:T(8,128)(2,1)S(1)} %pad_maximum_fusion.6), channel_id=1, source_target_pairs={{0,448},{64,0},{128,64},{192,128},{256,192},{320,256},{384,320},{4... | collective-permute-start | bytes 589832 | tf_op jit(solution)/shard_map/ppermute | solution.py:134
  59.3 12.1 %collective-permute-start.5 = (f16[384,512]{1,0:T(8,128)(2,1)S(1)}, f16[384,512]{1,0:T(8,128)(2,1)S(1)}, u32[]{:S(2)}, u32[]{:S(2)}) collective-permute-start(f16[384,512]{1,0:T(8,128)(2,1)S(1)} %fusion.9), channel_id=1, source_target_pairs={{0,64},{64,128},{128,192},{192,256},{256,320},{320,384},{384,448},... | collective-permute-start | bytes 1179656 | tf_op jit(solution)/shard_map/ppermute | solution.py:138
  61.9 11.5 %collective-permute-start.9 = (f16[384,512]{1,0:T(8,128)(2,1)S(1)}, f16[384,512]{1,0:T(8,128)(2,1)S(1)}, u32[]{:S(2)}, u32[]{:S(2)}) collective-permute-start(f16[384,512]{1,0:T(8,128)(2,1)S(1)} %fusion.12), channel_id=1, source_target_pairs={{0,448},{64,0},{128,64},{192,128},{256,192},{320,256},{384,320},{4... | collective-permute-start | bytes 1179656 | tf_op jit(solution)/shard_map/ppermute | solution.py:139
  71.5 13.9 %collective-permute-start.6 = (f16[384,512]{1,0:T(8,128)(2,1)S(1)}, f16[384,512]{1,0:T(8,128)(2,1)S(1)}, u32[]{:S(2)}, u32[]{:S(2)}) collective-permute-start(f16[384,512]{1,0:T(8,128)(2,1)S(1)} %fusion.8), channel_id=1, source_target_pairs={{0,64},{64,128},{128,192},{192,256},{256,320},{320,384},{384,448},... | collective-permute-start | bytes 1179656 | tf_op jit(solution)/shard_map/ppermute | solution.py:138
  73.6 13.9 %collective-permute-start.10 = (f16[384,512]{1,0:T(8,128)(2,1)S(1)}, f16[384,512]{1,0:T(8,128)(2,1)S(1)}, u32[]{:S(2)}, u32[]{:S(2)}) collective-permute-start(f16[384,512]{1,0:T(8,128)(2,1)S(1)} %fusion.11), channel_id=1, source_target_pairs={{0,448},{64,0},{128,64},{192,128},{256,192},{320,256},{384,320},{4... | collective-permute-start | bytes 1179656 | tf_op jit(solution)/shard_map/ppermute | solution.py:139
  80.0 22.6 %collective-permute-start.13 = (bf16[2,512,512]{2,1,0:T(8,128)(2,1)S(1)}, bf16[2,512,512]{2,1,0:T(8,128)(2,1)S(1)}, u32[]{:S(2)}, u32[]{:S(2)}) collective-permute-start(bf16[2,512,512]{2,1,0:T(8,128)(2,1)S(1)} %pad_maximum_fusion.1), channel_id=1, source_target_pairs={{0,1},{1,0},{2,3},{3,2},{4,5},{5,4},{6,7},{7,6},{8,9},{9,8},{10,11... | collective-permute-start | bytes 3145736 | tf_op jit(solution)/shard_map/ppermute | solution.py:22
  85.5 13.0 %collective-permute-start.7 = (f16[384,512]{1,0:T(8,128)(2,1)S(1)}, f16[384,512]{1,0:T(8,128)(2,1)S(1)}, u32[]{:S(2)}, u32[]{:S(2)}) collective-permute-start(f16[384,512]{1,0:T(8,128)(2,1)S(1)} %fusion.7), channel_id=1, source_target_pairs={{0,64},{64,128},{128,192},{192,256},{256,320},{320,384},{384,448},... | collective-permute-start | bytes 1179656 | tf_op jit(solution)/shard_map/ppermute | solution.py:138
  87.6 11.8 %collective-permute-start.11 = (f16[384,512]{1,0:T(8,128)(2,1)S(1)}, f16[384,512]{1,0:T(8,128)(2,1)S(1)}, u32[]{:S(2)}, u32[]{:S(2)}) collective-permute-start(f16[384,512]{1,0:T(8,128)(2,1)S(1)} %fusion.10), channel_id=1, source_target_pairs={{0,448},{64,0},{128,64},{192,128},{256,192},{320,256},{384,320},{4... | collective-permute-start | bytes 1179656 | tf_op jit(solution)/shard_map/ppermute | solution.py:139
  99.6 10.4 %collective-permute-start.12 = (f16[384,512]{1,0:T(8,128)(2,1)S(1)}, f16[384,512]{1,0:T(8,128)(2,1)S(1)}, u32[]{:S(2)}, u32[]{:S(2)}) collective-permute-start(f16[384,512]{1,0:T(8,128)(2,1)S(1)} %fusion.40), channel_id=1, source_target_pairs={{0,32},{32,0},{1,33},{33,1},{2,34},{34,2},{3,35},{35,3},{4,36},{36... | collective-permute-start | bytes 1179656 | tf_op jit(solution)/shard_map/ppermute | solution.py:22
  110.4 11.1 %collective-permute-start.17 = (bf16[384,512]{1,0:T(8,128)(2,1)S(1)}, bf16[384,512]{1,0:T(8,128)(2,1)S(1)}, u32[]{:S(2)}, u32[]{:S(2)}) collective-permute-start(bf16[384,512]{1,0:T(8,128)(2,1)S(1)} %bitcast.145), channel_id=1, source_target_pairs={{0,64},{64,128},{128,192},{192,256},{256,320},{320,384},{384,448},... | collective-permute-start | bytes 1179656 | tf_op jit(solution)/shard_map/ppermute | solution.py:155
  112.4 11.1 %collective-permute-start.14 = (bf16[384,512]{1,0:T(8,128)(2,1)S(1)}, bf16[384,512]{1,0:T(8,128)(2,1)S(1)}, u32[]{:S(2)}, u32[]{:S(2)}) collective-permute-start(bf16[384,512]{1,0:T(8,128)(2,1)S(1)} %bitcast.146), channel_id=1, source_target_pairs={{0,448},{64,0},{128,64},{192,128},{256,192},{320,256},{384,320},{4... | collective-permute-start | bytes 1179656 | tf_op jit(solution)/shard_map/ppermute | solution.py:156
  121.5 9.7 %collective-permute-start.18 = (bf16[384,512]{1,0:T(8,128)(2,1)S(1)}, bf16[384,512]{1,0:T(8,128)(2,1)S(1)}, u32[]{:S(2)}, u32[]{:S(2)}) collective-permute-start(bf16[384,512]{1,0:T(8,128)(2,1)S(1)} %collective-permute-done.17.refs_7_.refs_1_), channel_id=1, source_target_pairs={{0,64},{64,128},{128,192},{192,256},{256,320},{320,384},{384,448},... | collective-permute-start | bytes 1179656 | tf_op jit(solution)/shard_map/ppermute | solution.py:155
  123.4 9.7 %collective-permute-start.15 = (bf16[384,512]{1,0:T(8,128)(2,1)S(1)}, bf16[384,512]{1,0:T(8,128)(2,1)S(1)}, u32[]{:S(2)}, u32[]{:S(2)}) collective-permute-start(bf16[384,512]{1,0:T(8,128)(2,1)S(1)} %collective-permute-done.14.refs_1_.refs_2_), channel_id=1, source_target_pairs={{0,448},{64,0},{128,64},{192,128},{256,192},{320,256},{384,320},{4... | collective-permute-start | bytes 1179656 | tf_op jit(solution)/shard_map/ppermute | solution.py:156
  131.2 9.7 %collective-permute-start.19 = (bf16[384,512]{1,0:T(8,128)(2,1)S(1)}, bf16[384,512]{1,0:T(8,128)(2,1)S(1)}, u32[]{:S(2)}, u32[]{:S(2)}) collective-permute-start(bf16[384,512]{1,0:T(8,128)(2,1)S(1)} %collective-permute-done.18.refs_6_.refs_3_), channel_id=1, source_target_pairs={{0,64},{64,128},{128,192},{192,256},{256,320},{320,384},{384,448},... | collective-permute-start | bytes 1179656 | tf_op jit(solution)/shard_map/ppermute | solution.py:155
  133.2 9.7 %collective-permute-start.16 = (bf16[384,512]{1,0:T(8,128)(2,1)S(1)}, bf16[384,512]{1,0:T(8,128)(2,1)S(1)}, u32[]{:S(2)}, u32[]{:S(2)}) collective-permute-start(bf16[384,512]{1,0:T(8,128)(2,1)S(1)} %collective-permute-done.15.refs_2_.refs_4_), channel_id=1, source_target_pairs={{0,448},{64,0},{128,64},{192,128},{256,192},{320,256},{384,320},{4... | collective-permute-start | bytes 1179656 | tf_op jit(solution)/shard_map/ppermute | solution.py:156
  141.0 7.6 %collective-permute-start.20 = (bf16[384,256]{1,0:T(8,128)(2,1)S(1)}, bf16[384,256]{1,0:T(8,128)(2,1)S(1)}, u32[]{:S(2)}, u32[]{:S(2)}) collective-permute-start(bf16[384,256]{1,0:T(8,128)(2,1)S(1)} %slice.412), channel_id=1, source_target_pairs={{0,64},{64,128},{128,192},{192,256},{256,320},{320,384},{384,448},... | collective-permute-start | bytes 589832 | tf_op jit(solution)/shard_map/ppermute | solution.py:159
  151.6 8.6 %collective-permute-start.22 = (bf16[256,512]{1,0:T(8,128)(2,1)S(1)}, bf16[256,512]{1,0:T(8,128)(2,1)S(1)}, u32[]{:S(2)}, u32[]{:S(2)}) collective-permute-start(bf16[256,512]{1,0:T(8,128)(2,1)S(1)} %shard_map.84), channel_id=1, source_target_pairs={{0,2},{2,0},{1,3},{3,1},{4,6},{6,4},{5,7},{7,5},{8,10},{10,8},{9,1... | collective-permute-start | bytes 786440 | tf_op jit(solution)/shard_map/ppermute | solution.py:22
  160.2 16.0 %collective-permute-start.23 = (bf16[8,192,512]{2,1,0:T(8,128)(2,1)}, bf16[8,192,512]{2,1,0:T(8,128)(2,1)}, u32[]{:S(2)}, u32[]{:S(2)}) collective-permute-start(bf16[8,192,512]{2,1,0:T(8,128)(2,1)} %pad_maximum_fusion), channel_id=1, source_target_pairs={{0,1},{1,0},{2,3},{3,2},{4,5},{5,4},{6,7},{7,6},{8,9},{9,8},{10,11... | collective-permute-start | bytes 4718600 | tf_op jit(solution)/shard_map/ppermute | solution.py:22
  171.2 15.9 %all-to-all-start.1 = ((bf16[8,32,512]{2,1,0:T(8,128)(2,1)}), bf16[8,32,512]{2,1,0:T(8,128)(2,1)S(1)}, u32[]{:S(2)}, u32[]{:S(2)}) async-start(bf16[8,32,512]{2,1,0:T(8,128)(2,1)} %bitcast.170), calls=%async_computation.1 | async-start | bytes 524288 | tf_op jit(solution)/shard_map/all_to_all | solution.py:176
  (13 other events, 116.7 us)

commit v6 on v5

--- a/solution.py
+++ b/solution.py
@@ -26,9 +26,27 @@
     return lax.optimization_barrier(arrays)
 
 
-def turn(x, by):
-    n = x.shape[0]
-    return lax.dynamic_slice_in_dim(jnp.concatenate([x, x], axis=0), by, n, axis=0)
+def order_kernel(nz, g_ref, u_ref, d_ref, gu_out, d_out):
+    z = lax.axis_index("z")
+    n = d_ref.shape[0] // nz
+    gate, up = g_ref[...].T, u_ref[...].T
+    for i in range(nz):
+        k = lax.rem(i + nz - z, nz)
+        gu_out[k, :n, :] = gate[i * n : (i + 1) * n]
+        gu_out[k, n:, :] = up[i * n : (i + 1) * n]
+        d_out[k, :, :] = d_ref[i * n : (i + 1) * n, :]
+
+
+def in_order(nz, wg, wu, wd):
+    n, width = wd.shape[0] // nz, wd.shape[1]
+    return pl.pallas_call(
+        functools.partial(order_kernel, nz),
+        out_shape=[
+            jax.ShapeDtypeStruct((nz, 2 * n, width), wd.dtype),
+            jax.ShapeDtypeStruct((nz, n, width), wd.dtype),
+        ],
+        compiler_params=pltpu.CompilerParams(vmem_limit_bytes=40 * 2**20),
+    )(wg, wu, wd)
 
 
 def input_kernel(nz, at, *refs):
@@ -97,17 +115,13 @@
     pair = jnp.concatenate([x, c], axis=1)
     pair = jnp.broadcast_to(pair[None], (ny,) + pair.shape)
     pair = lax.all_to_all(pair, "y", 0, 0, tiled=True).reshape(ny * rows, 2 * width)
-    pair, wg_oth, wu_oth, wd_oth = tie(pair, swap(wg, "core"), swap(wu, "core"), swap(wd, "core"))
     other = swap(pair, "xh")
     part_tokens = pair.shape[0]
     x0, c0 = pair[:, :width], pair[:, width:]
     half = 2 * part_tokens
 
-    def by_z(*weights):
-        return turn(jnp.stack([w.reshape(nz, zf, width) for w in weights], axis=1), z).reshape(nz, -1, width)
-
-    gu_own, gu_oth = by_z(wg.T, wu.T), by_z(wg_oth.T, wu_oth.T)
-    d_own, d_oth = by_z(wd), by_z(wd_oth)
+    gu_own, d_own = in_order(nz, wg, wu, wd)
+    gu_oth, d_oth = in_order(nz, swap(wg, "core"), swap(wu, "core"), swap(wd, "core"))
     far = nz // 2
 
     def part_far(t, u):

time: 189 us -> 188 us (level)
  matrix products: 4.05 us -> 11.7 us
  other arithmetic: 12.5 us -> 6.5 us
  starting transfers between devices: 114 us -> 112 us
    dot_general x12, matrix products: 4.05 us -> 11.7 us  [dot(): lax.dot_general(a, b, (((ca,), (cb,)), ((), ())), preferred_element_type=...]
    concatenate x4 -> x0, other arithmetic: 6.2 us -> none  [turn(): jnp.concatenate([x, x], axis=0)]
    ppermute x1, starting transfers between devices: 11.1 us -> 8.59 us  [per_device(): l = lax.ppermute(half_part(1, far).astype(F16), 'z', left).astype(F32)]
    all_to_all x1, waiting for transfers between devices: 0.35 us -> 2.73 us  [per_device(): lax.all_to_all(pair, 'y', 0, 0, tiled=True).reshape(ny * rows, 2 * width)]
    ppermute x8, waiting for transfers between devices: 12.2 us -> 9.96 us  [swap(): return lax.ppermute(x, axis, [(0, 1), (1, 0)])]
  transfers between devices with their start and end apart: 26 -> 26, of which waited for: 14 -> 13; matrix products, arithmetic and copies ran while one was open for 9% -> 10% of each run, Pallas kernels for 4% -> 4%
where the time goes in v6:
time: 188 us; the launch traced here: 186 us
  starting transfers between devices  112 us (60%)
  waiting for transfers between devices  41.6 us (22%)
  matrix products  11.7 us (6%)
  Pallas kernels  8.84 us (5%)
  other arithmetic  6.5 us (3%)
  local copies, waits for them, and re-layouts  4.75 us (3%)
    ppermute x8, starting transfers between devices, swap(): return lax.ppermute(x, axis, [(0, 1), (1, 0)])  41.2 us
    ppermute x3, starting transfers between devices, per_device(): l = lax.ppermute((part(nz - k) + l).astype(F16), 'z', left).astype(F32)  14.9 us
    ppermute x3, starting transfers between devices, per_device(): chunk[k] = lax.ppermute(chunk[k - 1], 'z', left)  13.8 us
    dot_general x12, matrix products, dot(): lax.dot_general(a, b, (((ca,), (cb,)), ((), ())), preferred_element_type=...  11.7 us
    ppermute x3, waiting for transfers between devices, per_device(): r = lax.ppermute((part(k) + r).astype(F16), 'z', right).astype(F32)  10.5 us
    ppermute x3, waiting for transfers between devices, per_device(): chunk[nz - k] = lax.ppermute(chunk[(nz - k + 1) % nz], 'z', right)  10.4 us
    ppermute x8, waiting for transfers between devices, swap(): return lax.ppermute(x, axis, [(0, 1), (1, 0)])  9.96 us
    ppermute x1, starting transfers between devices, per_device(): l = lax.ppermute(half_part(1, far).astype(F16), 'z', left).astype(F32)  8.59 us
  transfers between devices with their start and end apart: 26, of which 13 were waited for; matrix products, arithmetic and copies ran while one was open for 10% of the time, Pallas kernels for 4%

profile of v6, /device:TPU:1, one launch (start us, length us, event | category | flops | bytes accessed | tf_op | source)
XLA Modules:
  0.0 186.4 jit_solution(9489698065266853778)
XLA Ops:
  2.4 7.7 %all-to-all-start = ((bf16[8,32,1024]{2,1,0:T(8,128)(2,1)}), bf16[8,32,1024]{2,1,0:T(8,128)(2,1)}, u32[]{:S(2)}, u32[]{:S(2)}) async-start(bf16[8,32,1024]{2,1,0:T(8,128)(2,1)} %broadcast_in_dim.4), calls=%async_computation | async-start | bytes 1048576 | tf_op jit(solution)/shard_map/all_to_all | solution.py:117
  10.1 5.3 %collective-permute-start.1 = (bf16[512,512]{1,0:T(8,128)(2,1)S(1)}, bf16[512,512]{1,0:T(8,128)(2,1)S(1)}, u32[]{:S(2)}, u32[]{:S(2)}) collective-permute-start(bf16[512,512]{1,0:T(8,128)(2,1)S(1)} %copy-done.12), channel_id=1, source_target_pairs={{0,1},{1,0},{2,3},{3,2},{4,5},{5,4},{6,7},{7,6},{8,9},{9,8},{10,11... | collective-permute-start | bytes 1572872 | tf_op jit(solution)/shard_map/ppermute | solution.py:22
  24.3 8.4 %collective-permute-start = (bf16[256,1024]{1,0:T(8,128)(2,1)}, bf16[256,1024]{1,0:T(8,128)(2,1)S(1)}, u32[]{:S(2)}, u32[]{:S(2)}) collective-permute-start(bf16[256,1024]{1,0:T(8,128)(2,1)} %bitcast), channel_id=1, source_target_pairs={{0,2},{2,0},{1,3},{3,1},{4,6},{6,4},{5,7},{7,5},{8,10},{10,8},{9,1... | collective-permute-start | bytes 1572872 | tf_op jit(solution)/shard_map/ppermute | solution.py:22
  40.2 4.0 %collective-permute-start.4 = (f16[384,256]{1,0:T(8,128)(2,1)S(1)}, f16[384,256]{1,0:T(8,128)(2,1)S(1)}, u32[]{:S(2)}, u32[]{:S(2)}) collective-permute-start(f16[384,256]{1,0:T(8,128)(2,1)S(1)} %fusion.7), channel_id=1, source_target_pairs={{0,64},{64,128},{128,192},{192,256},{256,320},{320,384},{384,448},... | collective-permute-start | bytes 589832 | tf_op jit(solution)/shard_map/ppermute | solution.py:147
  48.9 8.6 %collective-permute-start.8 = (f16[384,256]{1,0:T(8,128)(2,1)S(1)}, f16[384,256]{1,0:T(8,128)(2,1)S(1)}, u32[]{:S(2)}, u32[]{:S(2)}) collective-permute-start(f16[384,256]{1,0:T(8,128)(2,1)S(1)} %pad_maximum_fusion.6), channel_id=1, source_target_pairs={{0,448},{64,0},{128,64},{192,128},{256,192},{320,256},{384,320},{4... | collective-permute-start | bytes 589832 | tf_op jit(solution)/shard_map/ppermute | solution.py:148
  60.9 5.0 %collective-permute-start.9 = (f16[384,512]{1,0:T(8,128)(2,1)S(1)}, f16[384,512]{1,0:T(8,128)(2,1)S(1)}, u32[]{:S(2)}, u32[]{:S(2)}) collective-permute-start(f16[384,512]{1,0:T(8,128)(2,1)S(1)} %fusion.6), channel_id=1, source_target_pairs={{0,448},{64,0},{128,64},{192,128},{256,192},{320,256},{384,320},{4... | collective-permute-start | bytes 1179656 | tf_op jit(solution)/shard_map/ppermute | solution.py:153
  65.9 4.1 %collective-permute-done.5 = f16[384,512]{1,0:T(8,128)(2,1)S(1)} collective-permute-done((f16[384,512]{1,0:T(8,128)(2,1)S(1)}, f16[384,512]{1,0:T(8,128)(2,1)S(1)}, u32[]{:S(2)}, u32[]{:S(2)}) %collective-permute-start.5) | collective-permute-done | bytes 393248 | tf_op jit(solution)/shard_map/ppermute | solution.py:152
  72.3 5.3 %collective-permute-start.10 = (f16[384,512]{1,0:T(8,128)(2,1)S(1)}, f16[384,512]{1,0:T(8,128)(2,1)S(1)}, u32[]{:S(2)}, u32[]{:S(2)}) collective-permute-start(f16[384,512]{1,0:T(8,128)(2,1)S(1)} %fusion.5), channel_id=1, source_target_pairs={{0,448},{64,0},{128,64},{192,128},{256,192},{320,256},{384,320},{4... | collective-permute-start | bytes 1179656 | tf_op jit(solution)/shard_map/ppermute | solution.py:153
  78.8 5.2 %collective-permute-start.13 = (bf16[2,512,512]{2,1,0:T(8,128)(2,1)S(1)}, bf16[2,512,512]{2,1,0:T(8,128)(2,1)}, u32[]{:S(2)}, u32[]{:S(2)}) collective-permute-start(bf16[2,512,512]{2,1,0:T(8,128)(2,1)S(1)} %pad_maximum_fusion.1), channel_id=1, source_target_pairs={{0,1},{1,0},{2,3},{3,2},{4,5},{5,4},{6,7},{7,6},{8,9},{9,8},{10,11... | collective-permute-start | bytes 3145736 | tf_op jit(solution)/shard_map/ppermute | solution.py:22
  86.3 4.6 %collective-permute-start.11 = (f16[384,512]{1,0:T(8,128)(2,1)S(1)}, f16[384,512]{1,0:T(8,128)(2,1)S(1)}, u32[]{:S(2)}, u32[]{:S(2)}) collective-permute-start(f16[384,512]{1,0:T(8,128)(2,1)S(1)} %fusion.4), channel_id=1, source_target_pairs={{0,448},{64,0},{128,64},{192,128},{256,192},{320,256},{384,320},{4... | collective-permute-start | bytes 1179656 | tf_op jit(solution)/shard_map/ppermute | solution.py:153
  90.9 6.3 %collective-permute-done.7 = f16[384,512]{1,0:T(8,128)(2,1)S(1)} collective-permute-done((f16[384,512]{1,0:T(8,128)(2,1)S(1)}, f16[384,512]{1,0:T(8,128)(2,1)S(1)}, u32[]{:S(2)}, u32[]{:S(2)}) %collective-permute-start.7) | collective-permute-done | bytes 393248 | tf_op jit(solution)/shard_map/ppermute | solution.py:152
  101.1 7.5 %collective-permute-done.12 = f16[384,512]{1,0:T(8,128)(2,1)S(1)} collective-permute-done((f16[384,512]{1,0:T(8,128)(2,1)S(1)}, f16[384,512]{1,0:T(8,128)(2,1)S(1)}, u32[]{:S(2)}, u32[]{:S(2)}) %collective-permute-start.12) | collective-permute-done | bytes 393248 | tf_op jit(solution)/shard_map/ppermute | solution.py:22
  110.9 4.7 %collective-permute-start.14 = (bf16[384,512]{1,0:T(8,128)(2,1)S(1)}, bf16[384,512]{1,0:T(8,128)(2,1)S(1)}, u32[]{:S(2)}, u32[]{:S(2)}) collective-permute-start(bf16[384,512]{1,0:T(8,128)(2,1)S(1)} %bitcast.128), channel_id=1, source_target_pairs={{0,448},{64,0},{128,64},{192,128},{256,192},{320,256},{384,320},{4... | collective-permute-start | bytes 1179656 | tf_op jit(solution)/shard_map/ppermute | solution.py:170
  115.7 4.0 %collective-permute-done.17.refs_7_.refs_1_ = bf16[384,512]{1,0:T(8,128)(2,1)S(1)} collective-permute-done((bf16[384,512]{1,0:T(8,128)(2,1)S(1)}, bf16[384,512]{1,0:T(8,128)(2,1)S(1)}, u32[]{:S(2)}, u32[]{:S(2)}) %collective-permute-start.17) | collective-permute-done | bytes 393248 | tf_op jit(solution)/shard_map/ppermute | solution.py:169
  121.7 4.6 %collective-permute-start.15 = (bf16[384,512]{1,0:T(8,128)(2,1)S(1)}, bf16[384,512]{1,0:T(8,128)(2,1)S(1)}, u32[]{:S(2)}, u32[]{:S(2)}) collective-permute-start(bf16[384,512]{1,0:T(8,128)(2,1)S(1)} %collective-permute-done.14.refs_1_.refs_2_), channel_id=1, source_target_pairs={{0,448},{64,0},{128,64},{192,128},{256,192},{320,256},{384,320},{4... | collective-permute-start | bytes 1179656 | tf_op jit(solution)/shard_map/ppermute | solution.py:170
  126.3 3.2 %collective-permute-done.18.refs_6_.refs_3_ = bf16[384,512]{1,0:T(8,128)(2,1)S(1)} collective-permute-done((bf16[384,512]{1,0:T(8,128)(2,1)S(1)}, bf16[384,512]{1,0:T(8,128)(2,1)S(1)}, u32[]{:S(2)}, u32[]{:S(2)}) %collective-permute-start.18) | collective-permute-done | bytes 393248 | tf_op jit(solution)/shard_map/ppermute | solution.py:169
  131.4 4.6 %collective-permute-start.16 = (bf16[384,512]{1,0:T(8,128)(2,1)S(1)}, bf16[384,512]{1,0:T(8,128)(2,1)S(1)}, u32[]{:S(2)}, u32[]{:S(2)}) collective-permute-start(bf16[384,512]{1,0:T(8,128)(2,1)S(1)} %collective-permute-done.15.refs_2_.refs_4_), channel_id=1, source_target_pairs={{0,448},{64,0},{128,64},{192,128},{256,192},{320,256},{384,320},{4... | collective-permute-start | bytes 1179656 | tf_op jit(solution)/shard_map/ppermute | solution.py:170
  136.0 3.2 %collective-permute-done.19.refs_5_ = bf16[384,512]{1,0:T(8,128)(2,1)S(1)} collective-permute-done((bf16[384,512]{1,0:T(8,128)(2,1)S(1)}, bf16[384,512]{1,0:T(8,128)(2,1)S(1)}, u32[]{:S(2)}, u32[]{:S(2)}) %collective-permute-start.19) | collective-permute-done | bytes 393248 | tf_op jit(solution)/shard_map/ppermute | solution.py:169
  141.2 4.6 %collective-permute-start.21 = (bf16[384,256]{1,0:T(8,128)(2,1)S(1)}, bf16[384,256]{1,0:T(8,128)(2,1)S(1)}, u32[]{:S(2)}, u32[]{:S(2)}) collective-permute-start(bf16[384,256]{1,0:T(8,128)(2,1)S(1)} %slice.407), channel_id=1, source_target_pairs={{0,448},{64,0},{128,64},{192,128},{256,192},{320,256},{384,320},{4... | collective-permute-start | bytes 589832 | tf_op jit(solution)/shard_map/ppermute | solution.py:174
  150.0 4.7 %collective-permute-start.22 = (bf16[256,512]{1,0:T(8,128)(2,1)S(1)}, bf16[256,512]{1,0:T(8,128)(2,1)S(1)}, u32[]{:S(2)}, u32[]{:S(2)}) collective-permute-start(bf16[256,512]{1,0:T(8,128)(2,1)S(1)} %shard_map.86), channel_id=1, source_target_pairs={{0,2},{2,0},{1,3},{3,1},{4,6},{6,4},{5,7},{7,5},{8,10},{10,8},{9,1... | collective-permute-start | bytes 786440 | tf_op jit(solution)/shard_map/ppermute | solution.py:22
  158.6 10.4 %collective-permute-start.23 = (bf16[8,192,512]{2,1,0:T(8,128)(2,1)}, bf16[8,192,512]{2,1,0:T(8,128)(2,1)}, u32[]{:S(2)}, u32[]{:S(2)}) collective-permute-start(bf16[8,192,512]{2,1,0:T(8,128)(2,1)} %pad_maximum_fusion), channel_id=1, source_target_pairs={{0,1},{1,0},{2,3},{3,2},{4,5},{5,4},{6,7},{7,6},{8,9},{9,8},{10,11... | collective-permute-start | bytes 4718600 | tf_op jit(solution)/shard_map/ppermute | solution.py:22
  169.9 3.6 %all-to-all-start.1 = ((bf16[8,32,512]{2,1,0:T(8,128)(2,1)}), bf16[8,32,512]{2,1,0:T(8,128)(2,1)S(1)}, u32[]{:S(2)}, u32[]{:S(2)}) async-start(bf16[8,32,512]{2,1,0:T(8,128)(2,1)} %bitcast.141), calls=%async_computation.1 | async-start | bytes 524288 | tf_op jit(solution)/shard_map/all_to_all | solution.py:190
  175.9 5.6 %shard_map.88 = (bf16[512,512]{1,0:T(8,128)(2,1)}, bf16[512,512]{1,0:T(8,128)(2,1)}, bf16[512,512]{1,0:T(8,128)(2,1)}) custom-call(bf16[384,512]{1,0:T(8,128)(2,1)S(1)} %bitcast.131, bf16[384,512]{1,0:T(8,128)(2,1)S(1)} %copy-done.3, bf16[384,512]{1,0:T(8,128)(2,1)S(1)} %copy-done.5, bf16[384,512]{1,0:T(8,128)(2,1)S(1)} %copy-done.7, ...), custom_call_target="tpu_custom_call" | custom-call | tf_op jit(solution)/shard_map/pallas_call | solution.py:95
  181.5 4.2 %all-to-all-done.1 = bf16[8,32,512]{2,1,0:T(8,128)(2,1)S(1)} async-done(((bf16[8,32,512]{2,1,0:T(8,128)(2,1)}), bf16[8,32,512]{2,1,0:T(8,128)(2,1)S(1)}, u32[]{:S(2)}, u32[]{:S(2)}) %all-to-all-start.1) | async-done | bytes 262176 | tf_op jit(solution)/shard_map/all_to_all | solution.py:190
  (113 shorter events, 55.8 us)
Async XLA Ops:
  2.4 21.9 %all-to-all-start = ((bf16[8,32,1024]{2,1,0:T(8,128)(2,1)}), bf16[8,32,1024]{2,1,0:T(8,128)(2,1)}, u32[]{:S(2)}, u32[]{:S(2)}) async-start(bf16[8,32,1024]{2,1,0:T(8,128)(2,1)} %broadcast_in_dim.4), calls=%async_computation | async-start | bytes 1048576 | tf_op jit(solution)/shard_map/all_to_all | solution.py:117
  10.1 10.0 %collective-permute-start.1 = (bf16[512,512]{1,0:T(8,128)(2,1)S(1)}, bf16[512,512]{1,0:T(8,128)(2,1)S(1)}, u32[]{:S(2)}, u32[]{:S(2)}) collective-permute-start(bf16[512,512]{1,0:T(8,128)(2,1)S(1)} %copy-done.12), channel_id=1, source_target_pairs={{0,1},{1,0},{2,3},{3,2},{4,5},{5,4},{6,7},{7,6},{8,9},{9,8},{10,11... | collective-permute-start | bytes 1572872 | tf_op jit(solution)/shard_map/ppermute | solution.py:22
  24.3 22.6 %collective-permute-start = (bf16[256,1024]{1,0:T(8,128)(2,1)}, bf16[256,1024]{1,0:T(8,128)(2,1)S(1)}, u32[]{:S(2)}, u32[]{:S(2)}) collective-permute-start(bf16[256,1024]{1,0:T(8,128)(2,1)} %bitcast), channel_id=1, source_target_pairs={{0,2},{2,0},{1,3},{3,1},{4,6},{6,4},{5,7},{7,5},{8,10},{10,8},{9,1... | collective-permute-start | bytes 1572872 | tf_op jit(solution)/shard_map/ppermute | solution.py:22
  40.2 17.5 %collective-permute-start.4 = (f16[384,256]{1,0:T(8,128)(2,1)S(1)}, f16[384,256]{1,0:T(8,128)(2,1)S(1)}, u32[]{:S(2)}, u32[]{:S(2)}) collective-permute-start(f16[384,256]{1,0:T(8,128)(2,1)S(1)} %fusion.7), channel_id=1, source_target_pairs={{0,64},{64,128},{128,192},{192,256},{256,320},{320,384},{384,448},... | collective-permute-start | bytes 589832 | tf_op jit(solution)/shard_map/ppermute | solution.py:147
  48.9 11.9 %collective-permute-start.8 = (f16[384,256]{1,0:T(8,128)(2,1)S(1)}, f16[384,256]{1,0:T(8,128)(2,1)S(1)}, u32[]{:S(2)}, u32[]{:S(2)}) collective-permute-start(f16[384,256]{1,0:T(8,128)(2,1)S(1)} %pad_maximum_fusion.6), channel_id=1, source_target_pairs={{0,448},{64,0},{128,64},{192,128},{256,192},{320,256},{384,320},{4... | collective-permute-start | bytes 589832 | tf_op jit(solution)/shard_map/ppermute | solution.py:148
  57.8 12.2 %collective-permute-start.5 = (f16[384,512]{1,0:T(8,128)(2,1)S(1)}, f16[384,512]{1,0:T(8,128)(2,1)S(1)}, u32[]{:S(2)}, u32[]{:S(2)}) collective-permute-start(f16[384,512]{1,0:T(8,128)(2,1)S(1)} %fusion.3), channel_id=1, source_target_pairs={{0,64},{64,128},{128,192},{192,256},{256,320},{320,384},{384,448},... | collective-permute-start | bytes 1179656 | tf_op jit(solution)/shard_map/ppermute | solution.py:152
  60.9 11.2 %collective-permute-start.9 = (f16[384,512]{1,0:T(8,128)(2,1)S(1)}, f16[384,512]{1,0:T(8,128)(2,1)S(1)}, u32[]{:S(2)}, u32[]{:S(2)}) collective-permute-start(f16[384,512]{1,0:T(8,128)(2,1)S(1)} %fusion.6), channel_id=1, source_target_pairs={{0,448},{64,0},{128,64},{192,128},{256,192},{320,256},{384,320},{4... | collective-permute-start | bytes 1179656 | tf_op jit(solution)/shard_map/ppermute | solution.py:153
  70.2 13.9 %collective-permute-start.6 = (f16[384,512]{1,0:T(8,128)(2,1)S(1)}, f16[384,512]{1,0:T(8,128)(2,1)S(1)}, u32[]{:S(2)}, u32[]{:S(2)}) collective-permute-start(f16[384,512]{1,0:T(8,128)(2,1)S(1)} %fusion.2), channel_id=1, source_target_pairs={{0,64},{64,128},{128,192},{192,256},{256,320},{320,384},{384,448},... | collective-permute-start | bytes 1179656 | tf_op jit(solution)/shard_map/ppermute | solution.py:152
  72.3 13.8 %collective-permute-start.10 = (f16[384,512]{1,0:T(8,128)(2,1)S(1)}, f16[384,512]{1,0:T(8,128)(2,1)S(1)}, u32[]{:S(2)}, u32[]{:S(2)}) collective-permute-start(f16[384,512]{1,0:T(8,128)(2,1)S(1)} %fusion.5), channel_id=1, source_target_pairs={{0,448},{64,0},{128,64},{192,128},{256,192},{320,256},{384,320},{4... | collective-permute-start | bytes 1179656 | tf_op jit(solution)/shard_map/ppermute | solution.py:153
  78.8 22.2 %collective-permute-start.13 = (bf16[2,512,512]{2,1,0:T(8,128)(2,1)S(1)}, bf16[2,512,512]{2,1,0:T(8,128)(2,1)}, u32[]{:S(2)}, u32[]{:S(2)}) collective-permute-start(bf16[2,512,512]{2,1,0:T(8,128)(2,1)S(1)} %pad_maximum_fusion.1), channel_id=1, source_target_pairs={{0,1},{1,0},{2,3},{3,2},{4,5},{5,4},{6,7},{7,6},{8,9},{9,8},{10,11... | collective-permute-start | bytes 3145736 | tf_op jit(solution)/shard_map/ppermute | solution.py:22
  84.2 13.0 %collective-permute-start.7 = (f16[384,512]{1,0:T(8,128)(2,1)S(1)}, f16[384,512]{1,0:T(8,128)(2,1)S(1)}, u32[]{:S(2)}, u32[]{:S(2)}) collective-permute-start(f16[384,512]{1,0:T(8,128)(2,1)S(1)} %fusion.1), channel_id=1, source_target_pairs={{0,64},{64,128},{128,192},{192,256},{256,320},{320,384},{384,448},... | collective-permute-start | bytes 1179656 | tf_op jit(solution)/shard_map/ppermute | solution.py:152
  86.3 11.7 %collective-permute-start.11 = (f16[384,512]{1,0:T(8,128)(2,1)S(1)}, f16[384,512]{1,0:T(8,128)(2,1)S(1)}, u32[]{:S(2)}, u32[]{:S(2)}) collective-permute-start(f16[384,512]{1,0:T(8,128)(2,1)S(1)} %fusion.4), channel_id=1, source_target_pairs={{0,448},{64,0},{128,64},{192,128},{256,192},{320,256},{384,320},{4... | collective-permute-start | bytes 1179656 | tf_op jit(solution)/shard_map/ppermute | solution.py:153
  98.2 10.4 %collective-permute-start.12 = (f16[384,512]{1,0:T(8,128)(2,1)S(1)}, f16[384,512]{1,0:T(8,128)(2,1)S(1)}, u32[]{:S(2)}, u32[]{:S(2)}) collective-permute-start(f16[384,512]{1,0:T(8,128)(2,1)S(1)} %fusion.40), channel_id=1, source_target_pairs={{0,32},{32,0},{1,33},{33,1},{2,34},{34,2},{3,35},{35,3},{4,36},{36... | collective-permute-start | bytes 1179656 | tf_op jit(solution)/shard_map/ppermute | solution.py:22
  109.0 10.7 %collective-permute-start.17 = (bf16[384,512]{1,0:T(8,128)(2,1)S(1)}, bf16[384,512]{1,0:T(8,128)(2,1)S(1)}, u32[]{:S(2)}, u32[]{:S(2)}) collective-permute-start(bf16[384,512]{1,0:T(8,128)(2,1)S(1)} %bitcast.127), channel_id=1, source_target_pairs={{0,64},{64,128},{128,192},{192,256},{256,320},{320,384},{384,448},... | collective-permute-start | bytes 1179656 | tf_op jit(solution)/shard_map/ppermute | solution.py:169
  110.9 10.7 %collective-permute-start.14 = (bf16[384,512]{1,0:T(8,128)(2,1)S(1)}, bf16[384,512]{1,0:T(8,128)(2,1)S(1)}, u32[]{:S(2)}, u32[]{:S(2)}) collective-permute-start(bf16[384,512]{1,0:T(8,128)(2,1)S(1)} %bitcast.128), channel_id=1, source_target_pairs={{0,448},{64,0},{128,64},{192,128},{256,192},{320,256},{384,320},{4... | collective-permute-start | bytes 1179656 | tf_op jit(solution)/shard_map/ppermute | solution.py:170
  119.7 9.7 %collective-permute-start.18 = (bf16[384,512]{1,0:T(8,128)(2,1)S(1)}, bf16[384,512]{1,0:T(8,128)(2,1)S(1)}, u32[]{:S(2)}, u32[]{:S(2)}) collective-permute-start(bf16[384,512]{1,0:T(8,128)(2,1)S(1)} %collective-permute-done.17.refs_7_.refs_1_), channel_id=1, source_target_pairs={{0,64},{64,128},{128,192},{192,256},{256,320},{320,384},{384,448},... | collective-permute-start | bytes 1179656 | tf_op jit(solution)/shard_map/ppermute | solution.py:169
  121.7 9.7 %collective-permute-start.15 = (bf16[384,512]{1,0:T(8,128)(2,1)S(1)}, bf16[384,512]{1,0:T(8,128)(2,1)S(1)}, u32[]{:S(2)}, u32[]{:S(2)}) collective-permute-start(bf16[384,512]{1,0:T(8,128)(2,1)S(1)} %collective-permute-done.14.refs_1_.refs_2_), channel_id=1, source_target_pairs={{0,448},{64,0},{128,64},{192,128},{256,192},{320,256},{384,320},{4... | collective-permute-start | bytes 1179656 | tf_op jit(solution)/shard_map/ppermute | solution.py:170
  129.4 9.7 %collective-permute-start.19 = (bf16[384,512]{1,0:T(8,128)(2,1)S(1)}, bf16[384,512]{1,0:T(8,128)(2,1)S(1)}, u32[]{:S(2)}, u32[]{:S(2)}) collective-permute-start(bf16[384,512]{1,0:T(8,128)(2,1)S(1)} %collective-permute-done.18.refs_6_.refs_3_), channel_id=1, source_target_pairs={{0,64},{64,128},{128,192},{192,256},{256,320},{320,384},{384,448},... | collective-permute-start | bytes 1179656 | tf_op jit(solution)/shard_map/ppermute | solution.py:169
  131.4 9.7 %collective-permute-start.16 = (bf16[384,512]{1,0:T(8,128)(2,1)S(1)}, bf16[384,512]{1,0:T(8,128)(2,1)S(1)}, u32[]{:S(2)}, u32[]{:S(2)}) collective-permute-start(bf16[384,512]{1,0:T(8,128)(2,1)S(1)} %collective-permute-done.15.refs_2_.refs_4_), channel_id=1, source_target_pairs={{0,448},{64,0},{128,64},{192,128},{256,192},{320,256},{384,320},{4... | collective-permute-start | bytes 1179656 | tf_op jit(solution)/shard_map/ppermute | solution.py:170
  139.2 7.7 %collective-permute-start.20 = (bf16[384,256]{1,0:T(8,128)(2,1)S(1)}, bf16[384,256]{1,0:T(8,128)(2,1)S(1)}, u32[]{:S(2)}, u32[]{:S(2)}) collective-permute-start(bf16[384,256]{1,0:T(8,128)(2,1)S(1)} %slice.406), channel_id=1, source_target_pairs={{0,64},{64,128},{128,192},{192,256},{256,320},{320,384},{384,448},... | collective-permute-start | bytes 589832 | tf_op jit(solution)/shard_map/ppermute | solution.py:173
  141.2 7.5 %collective-permute-start.21 = (bf16[384,256]{1,0:T(8,128)(2,1)S(1)}, bf16[384,256]{1,0:T(8,128)(2,1)S(1)}, u32[]{:S(2)}, u32[]{:S(2)}) collective-permute-start(bf16[384,256]{1,0:T(8,128)(2,1)S(1)} %slice.407), channel_id=1, source_target_pairs={{0,448},{64,0},{128,64},{192,128},{256,192},{320,256},{384,320},{4... | collective-permute-start | bytes 589832 | tf_op jit(solution)/shard_map/ppermute | solution.py:174
  150.0 8.6 %collective-permute-start.22 = (bf16[256,512]{1,0:T(8,128)(2,1)S(1)}, bf16[256,512]{1,0:T(8,128)(2,1)S(1)}, u32[]{:S(2)}, u32[]{:S(2)}) collective-permute-start(bf16[256,512]{1,0:T(8,128)(2,1)S(1)} %shard_map.86), channel_id=1, source_target_pairs={{0,2},{2,0},{1,3},{3,1},{4,6},{6,4},{5,7},{7,5},{8,10},{10,8},{9,1... | collective-permute-start | bytes 786440 | tf_op jit(solution)/shard_map/ppermute | solution.py:22
  158.6 16.1 %collective-permute-start.23 = (bf16[8,192,512]{2,1,0:T(8,128)(2,1)}, bf16[8,192,512]{2,1,0:T(8,128)(2,1)}, u32[]{:S(2)}, u32[]{:S(2)}) collective-permute-start(bf16[8,192,512]{2,1,0:T(8,128)(2,1)} %pad_maximum_fusion), channel_id=1, source_target_pairs={{0,1},{1,0},{2,3},{3,2},{4,5},{5,4},{6,7},{7,6},{8,9},{9,8},{10,11... | collective-permute-start | bytes 4718600 | tf_op jit(solution)/shard_map/ppermute | solution.py:22
  169.9 15.9 %all-to-all-start.1 = ((bf16[8,32,512]{2,1,0:T(8,128)(2,1)}), bf16[8,32,512]{2,1,0:T(8,128)(2,1)S(1)}, u32[]{:S(2)}, u32[]{:S(2)}) async-start(bf16[8,32,512]{2,1,0:T(8,128)(2,1)} %bitcast.141), calls=%async_computation.1 | async-start | bytes 524288 | tf_op jit(solution)/shard_map/all_to_all | solution.py:190
  (17 other events, 206.9 us)

commit v7 on v6

--- a/solution.py
+++ b/solution.py
@@ -45,7 +45,7 @@
             jax.ShapeDtypeStruct((nz, 2 * n, width), wd.dtype),
             jax.ShapeDtypeStruct((nz, n, width), wd.dtype),
         ],
-        compiler_params=pltpu.CompilerParams(vmem_limit_bytes=40 * 2**20),
+        compiler_params=pltpu.CompilerParams(vmem_limit_bytes=16 * 2**20),
     )(wg, wu, wd)
 
 
@@ -66,20 +66,20 @@
     return pl.pallas_call(
         functools.partial(input_kernel, len(chunks), at),
         out_shape=jax.ShapeDtypeStruct((n, own.shape[2]), dtype),
-        compiler_params=pltpu.CompilerParams(vmem_limit_bytes=40 * 2**20),
+        compiler_params=pltpu.CompilerParams(vmem_limit_bytes=16 * 2**20),
     )(*chunks, own, oth)
 
 
 def grads_kernel(order, zf, *refs):
     nz = len(order)
-    chunks, (got_ref, x_ref, c_ref, xo_ref, co_ref, gate_ref, up_ref, down_ref, sums) = refs[:nz], refs[nz:]
+    chunks, (got_ref, own_ref, oth_ref, gate_ref, up_ref, down_ref, sums) = refs[:nz], refs[nz:]
     z = lax.axis_index("z")
     n = 2 * zf
     for k in range(nz):
-        gu = jnp.dot(chunks[k][:n, :], x_ref[...], preferred_element_type=F32)
-        gu += jnp.dot(got_ref[k, :n, :], xo_ref[...], preferred_element_type=F32)
-        dn = jnp.dot(chunks[k][n : n + zf, :], c_ref[...], preferred_element_type=F32)
-        dn += jnp.dot(got_ref[k, n:, :], co_ref[...], preferred_element_type=F32)
+        gu = jnp.dot(chunks[k][:n, :], own_ref[0], preferred_element_type=F32)
+        gu += jnp.dot(got_ref[k, :n, :], oth_ref[0], preferred_element_type=F32)
+        dn = jnp.dot(chunks[k][n : n + zf, :], own_ref[1], preferred_element_type=F32)
+        dn += jnp.dot(got_ref[k, n:, :], oth_ref[1], preferred_element_type=F32)
         at = lax.rem(z + order[k], nz)
         sums[at, :n, :] = gu.astype(BF16)
         sums[at, n:, :] = dn.astype(BF16)
@@ -91,7 +91,7 @@
 
 
 def weight_grads(chunks, order, got, tokens, zf):
-    nz, width = len(chunks), tokens[0].shape[1]
+    nz, width = len(chunks), tokens[0].shape[2]
     return pl.pallas_call(
         functools.partial(grads_kernel, order, zf),
         out_shape=[
@@ -100,7 +100,7 @@
             jax.ShapeDtypeStruct((nz * zf, width), BF16),
         ],
         scratch_shapes=[pltpu.VMEM((nz, 3 * zf, width), BF16)],
-        compiler_params=pltpu.CompilerParams(vmem_limit_bytes=40 * 2**20),
+        compiler_params=pltpu.CompilerParams(vmem_limit_bytes=16 * 2**20),
     )(*chunks, got, *tokens)
 
 
@@ -153,7 +153,8 @@
         l = lax.ppermute((part(nz - k) + l).astype(F16), "z", left).astype(F32)
     total = part(0) + r + l
     got = swap(total.astype(F16), "xl")
-    tokens_oth = swap(jnp.stack([xs, cs]), "core")
+    tokens_own = jnp.stack([xs, cs])
+    tokens_oth = swap(tokens_own, "core")
     got, tokens_oth = tie(got, tokens_oth)
     total = ((total + got.astype(F32)) * (1.0 / SCALE)).reshape(2, 3, zf, half)
     gate, upper, hidden_grad = total[:, 0], total[:, 1], total[:, 2]
@@ -188,7 +189,7 @@
     deltas = swap(deltas, "core")
     total = (total + got.astype(F32)).astype(BF16).reshape(ny, rows, width)
     recv = lax.all_to_all(total, "y", 0, 0, tiled=True)
-    tokens = (xs, cs, tokens_oth[0], tokens_oth[1])
+    tokens = (tokens_own, tokens_oth)
     gate_grad, up_grad, down_grad = weight_grads([chunk[k] for k in order], order, deltas, tokens, zf)
     recv, gate_grad, up_grad, down_grad = tie(recv, gate_grad, up_grad, down_grad)
     input_grad = recv.astype(F32).sum(0).astype(BF16)

time: 188 us -> 186 us (0.989)
  waiting for transfers between devices: 41.6 us -> 39.2 us
    unnamed x36 -> x40, local copies, waits for them, and re-layouts: 1.19 us -> 3.58 us
  transfers between devices with their start and end apart: 26 -> 26, of which waited for: 13 -> 14; matrix products, arithmetic and copies ran while one was open for 10% -> 9% of each run, Pallas kernels for 4% -> 4%
where the time goes in v7:
time: 186 us; the launch traced here: 185 us
  starting transfers between devices  113 us (61%)
  waiting for transfers between devices  39.2 us (21%)
  matrix products  11.7 us (6%)
  Pallas kernels  8.84 us (5%)
  local copies, waits for them, and re-layouts  5.82 us (3%)
  other arithmetic  5.28 us (3%)
    ppermute x8, starting transfers between devices, swap(): return lax.ppermute(x, axis, [(0, 1), (1, 0)])  42.1 us
    ppermute x3, starting transfers between devices, per_device(): l = lax.ppermute((part(nz - k) + l).astype(F16), 'z', left).astype(F32)  14.9 us
    ppermute x3, starting transfers between devices, per_device(): chunk[k] = lax.ppermute(chunk[k - 1], 'z', left)  13.9 us
    dot_general x12, matrix products, dot(): lax.dot_general(a, b, (((ca,), (cb,)), ((), ())), preferred_element_type=...  11.7 us
    ppermute x3, waiting for transfers between devices, per_device(): chunk[nz - k] = lax.ppermute(chunk[(nz - k + 1) % nz], 'z', right)  9.72 us
    ppermute x3, waiting for transfers between devices, per_device(): r = lax.ppermute((part(k) + r).astype(F16), 'z', right).astype(F32)  9.44 us
    ppermute x1, starting transfers between devices, per_device(): l = lax.ppermute(half_part(1, far).astype(F16), 'z', left).astype(F32)  8.59 us
    ppermute x8, waiting for transfers between devices, swap(): return lax.ppermute(x, axis, [(0, 1), (1, 0)])  8.19 us
  transfers between devices with their start and end apart: 26, of which 14 were waited for; matrix products, arithmetic and copies ran while one was open for 9% of the time, Pallas kernels for 4%

profile of v7, /device:TPU:1, one launch (start us, length us, event | category | flops | bytes accessed | tf_op | source)
XLA Modules:
  0.0 185.1 jit_solution(2959796953345178178)
XLA Ops:
  2.4 7.7 %all-to-all-start = ((bf16[8,32,1024]{2,1,0:T(8,128)(2,1)}), bf16[8,32,1024]{2,1,0:T(8,128)(2,1)}, u32[]{:S(2)}, u32[]{:S(2)}) async-start(bf16[8,32,1024]{2,1,0:T(8,128)(2,1)} %broadcast_in_dim.4), calls=%async_computation | async-start | bytes 1048576 | tf_op jit(solution)/shard_map/all_to_all | solution.py:117
  10.1 5.3 %collective-permute-start.1 = (bf16[512,512]{1,0:T(8,128)(2,1)S(1)}, bf16[512,512]{1,0:T(8,128)(2,1)S(1)}, u32[]{:S(2)}, u32[]{:S(2)}) collective-permute-start(bf16[512,512]{1,0:T(8,128)(2,1)S(1)} %copy-done.14), channel_id=1, source_target_pairs={{0,1},{1,0},{2,3},{3,2},{4,5},{5,4},{6,7},{7,6},{8,9},{9,8},{10,11... | collective-permute-start | bytes 1572872 | tf_op jit(solution)/shard_map/ppermute | solution.py:22
  24.3 8.4 %collective-permute-start = (bf16[256,1024]{1,0:T(8,128)(2,1)}, bf16[256,1024]{1,0:T(8,128)(2,1)S(1)}, u32[]{:S(2)}, u32[]{:S(2)}) collective-permute-start(bf16[256,1024]{1,0:T(8,128)(2,1)} %bitcast), channel_id=1, source_target_pairs={{0,2},{2,0},{1,3},{3,1},{4,6},{6,4},{5,7},{7,5},{8,10},{10,8},{9,1... | collective-permute-start | bytes 1572872 | tf_op jit(solution)/shard_map/ppermute | solution.py:22
  40.2 4.0 %collective-permute-start.4 = (f16[384,256]{1,0:T(8,128)(2,1)S(1)}, f16[384,256]{1,0:T(8,128)(2,1)S(1)}, u32[]{:S(2)}, u32[]{:S(2)}) collective-permute-start(f16[384,256]{1,0:T(8,128)(2,1)S(1)} %fusion.7), channel_id=1, source_target_pairs={{0,64},{64,128},{128,192},{192,256},{256,320},{320,384},{384,448},... | collective-permute-start | bytes 589832 | tf_op jit(solution)/shard_map/ppermute | solution.py:147
  48.9 8.6 %collective-permute-start.8 = (f16[384,256]{1,0:T(8,128)(2,1)S(1)}, f16[384,256]{1,0:T(8,128)(2,1)S(1)}, u32[]{:S(2)}, u32[]{:S(2)}) collective-permute-start(f16[384,256]{1,0:T(8,128)(2,1)S(1)} %pad_maximum_fusion.4), channel_id=1, source_target_pairs={{0,448},{64,0},{128,64},{192,128},{256,192},{320,256},{384,320},{4... | collective-permute-start | bytes 589832 | tf_op jit(solution)/shard_map/ppermute | solution.py:148
  60.9 5.0 %collective-permute-start.9 = (f16[384,512]{1,0:T(8,128)(2,1)S(1)}, f16[384,512]{1,0:T(8,128)(2,1)S(1)}, u32[]{:S(2)}, u32[]{:S(2)}) collective-permute-start(f16[384,512]{1,0:T(8,128)(2,1)S(1)} %fusion.6), channel_id=1, source_target_pairs={{0,448},{64,0},{128,64},{192,128},{256,192},{320,256},{384,320},{4... | collective-permute-start | bytes 1179656 | tf_op jit(solution)/shard_map/ppermute | solution.py:153
  66.0 4.1 %collective-permute-done.5 = f16[384,512]{1,0:T(8,128)(2,1)S(1)} collective-permute-done((f16[384,512]{1,0:T(8,128)(2,1)S(1)}, f16[384,512]{1,0:T(8,128)(2,1)S(1)}, u32[]{:S(2)}, u32[]{:S(2)}) %collective-permute-start.5) | collective-permute-done | bytes 393248 | tf_op jit(solution)/shard_map/ppermute | solution.py:152
  72.3 5.3 %collective-permute-start.10 = (f16[384,512]{1,0:T(8,128)(2,1)S(1)}, f16[384,512]{1,0:T(8,128)(2,1)S(1)}, u32[]{:S(2)}, u32[]{:S(2)}) collective-permute-start(f16[384,512]{1,0:T(8,128)(2,1)S(1)} %fusion.5), channel_id=1, source_target_pairs={{0,448},{64,0},{128,64},{192,128},{256,192},{320,256},{384,320},{4... | collective-permute-start | bytes 1179656 | tf_op jit(solution)/shard_map/ppermute | solution.py:153
  77.8 5.2 %collective-permute-start.13 = (bf16[2,512,512]{2,1,0:T(8,128)(2,1)S(1)}, bf16[2,512,512]{2,1,0:T(8,128)(2,1)S(1)}, u32[]{:S(2)}, u32[]{:S(2)}) collective-permute-start(bf16[2,512,512]{2,1,0:T(8,128)(2,1)S(1)} %pad_maximum_fusion.1.refs_9_), channel_id=1, source_target_pairs={{0,1},{1,0},{2,3},{3,2},{4,5},{5,4},{6,7},{7,6},{8,9},{9,8},{10,11... | collective-permute-start | bytes 3145736 | tf_op jit(solution)/shard_map/ppermute | solution.py:22
  85.2 4.6 %collective-permute-start.11 = (f16[384,512]{1,0:T(8,128)(2,1)S(1)}, f16[384,512]{1,0:T(8,128)(2,1)S(1)}, u32[]{:S(2)}, u32[]{:S(2)}) collective-permute-start(f16[384,512]{1,0:T(8,128)(2,1)S(1)} %fusion.4), channel_id=1, source_target_pairs={{0,448},{64,0},{128,64},{192,128},{256,192},{320,256},{384,320},{4... | collective-permute-start | bytes 1179656 | tf_op jit(solution)/shard_map/ppermute | solution.py:153
  89.8 5.3 %collective-permute-done.7 = f16[384,512]{1,0:T(8,128)(2,1)S(1)} collective-permute-done((f16[384,512]{1,0:T(8,128)(2,1)S(1)}, f16[384,512]{1,0:T(8,128)(2,1)S(1)}, u32[]{:S(2)}, u32[]{:S(2)}) %collective-permute-start.7) | collective-permute-done | bytes 393248 | tf_op jit(solution)/shard_map/ppermute | solution.py:152
  99.9 5.4 %collective-permute-done.12 = f16[384,512]{1,0:T(8,128)(2,1)S(1)} collective-permute-done((f16[384,512]{1,0:T(8,128)(2,1)S(1)}, f16[384,512]{1,0:T(8,128)(2,1)S(1)}, u32[]{:S(2)}, u32[]{:S(2)}) %collective-permute-start.12) | collective-permute-done | bytes 393248 | tf_op jit(solution)/shard_map/ppermute | solution.py:22
  107.7 4.8 %collective-permute-start.14 = (bf16[384,512]{1,0:T(8,128)(2,1)S(1)}, bf16[384,512]{1,0:T(8,128)(2,1)S(1)}, u32[]{:S(2)}, u32[]{:S(2)}) collective-permute-start(bf16[384,512]{1,0:T(8,128)(2,1)S(1)} %bitcast.124), channel_id=1, source_target_pairs={{0,448},{64,0},{128,64},{192,128},{256,192},{320,256},{384,320},{4... | collective-permute-start | bytes 1179656 | tf_op jit(solution)/shard_map/ppermute | solution.py:171
  112.5 3.2 %collective-permute-done.17.refs_7_.refs_1_ = bf16[384,512]{1,0:T(8,128)(2,1)S(1)} collective-permute-done((bf16[384,512]{1,0:T(8,128)(2,1)S(1)}, bf16[384,512]{1,0:T(8,128)(2,1)S(1)}, u32[]{:S(2)}, u32[]{:S(2)}) %collective-permute-start.17) | collective-permute-done | bytes 393248 | tf_op jit(solution)/shard_map/ppermute | solution.py:170
  117.6 4.6 %collective-permute-start.15 = (bf16[384,512]{1,0:T(8,128)(2,1)S(1)}, bf16[384,512]{1,0:T(8,128)(2,1)S(1)}, u32[]{:S(2)}, u32[]{:S(2)}) collective-permute-start(bf16[384,512]{1,0:T(8,128)(2,1)S(1)} %collective-permute-done.14.refs_1_.refs_2_), channel_id=1, source_target_pairs={{0,448},{64,0},{128,64},{192,128},{256,192},{320,256},{384,320},{4... | collective-permute-start | bytes 1179656 | tf_op jit(solution)/shard_map/ppermute | solution.py:171
  122.3 3.2 %collective-permute-done.18.refs_6_.refs_3_ = bf16[384,512]{1,0:T(8,128)(2,1)S(1)} collective-permute-done((bf16[384,512]{1,0:T(8,128)(2,1)S(1)}, bf16[384,512]{1,0:T(8,128)(2,1)S(1)}, u32[]{:S(2)}, u32[]{:S(2)}) %collective-permute-start.18) | collective-permute-done | bytes 393248 | tf_op jit(solution)/shard_map/ppermute | solution.py:170
  127.4 4.6 %collective-permute-start.16 = (bf16[384,512]{1,0:T(8,128)(2,1)S(1)}, bf16[384,512]{1,0:T(8,128)(2,1)S(1)}, u32[]{:S(2)}, u32[]{:S(2)}) collective-permute-start(bf16[384,512]{1,0:T(8,128)(2,1)S(1)} %collective-permute-done.15.refs_2_.refs_4_), channel_id=1, source_target_pairs={{0,448},{64,0},{128,64},{192,128},{256,192},{320,256},{384,320},{4... | collective-permute-start | bytes 1179656 | tf_op jit(solution)/shard_map/ppermute | solution.py:171
  132.0 3.4 %collective-permute-done.19.refs_5_ = bf16[384,512]{1,0:T(8,128)(2,1)S(1)} collective-permute-done((bf16[384,512]{1,0:T(8,128)(2,1)S(1)}, bf16[384,512]{1,0:T(8,128)(2,1)S(1)}, u32[]{:S(2)}, u32[]{:S(2)}) %collective-permute-start.19) | collective-permute-done | bytes 393248 | tf_op jit(solution)/shard_map/ppermute | solution.py:170
  137.4 4.8 %collective-permute-start.21 = (bf16[384,256]{1,0:T(8,128)(2,1)S(1)}, bf16[384,256]{1,0:T(8,128)(2,1)S(1)}, u32[]{:S(2)}, u32[]{:S(2)}) collective-permute-start(bf16[384,256]{1,0:T(8,128)(2,1)S(1)} %slice.399), channel_id=1, source_target_pairs={{0,448},{64,0},{128,64},{192,128},{256,192},{320,256},{384,320},{4... | collective-permute-start | bytes 589832 | tf_op jit(solution)/shard_map/ppermute | solution.py:175
  147.7 4.3 %collective-permute-start.22 = (bf16[256,512]{1,0:T(8,128)(2,1)S(1)}, bf16[256,512]{1,0:T(8,128)(2,1)S(1)}, u32[]{:S(2)}, u32[]{:S(2)}) collective-permute-start(bf16[256,512]{1,0:T(8,128)(2,1)S(1)} %shard_map.86), channel_id=1, source_target_pairs={{0,2},{2,0},{1,3},{3,1},{4,6},{6,4},{5,7},{7,5},{8,10},{10,8},{9,1... | collective-permute-start | bytes 786440 | tf_op jit(solution)/shard_map/ppermute | solution.py:22
  156.3 11.6 %collective-permute-start.23 = (bf16[8,192,512]{2,1,0:T(8,128)(2,1)}, bf16[8,192,512]{2,1,0:T(8,128)(2,1)}, u32[]{:S(2)}, u32[]{:S(2)}) collective-permute-start(bf16[8,192,512]{2,1,0:T(8,128)(2,1)} %pad_maximum_fusion), channel_id=1, source_target_pairs={{0,1},{1,0},{2,3},{3,2},{4,5},{5,4},{6,7},{7,6},{8,9},{9,8},{10,11... | collective-permute-start | bytes 4718600 | tf_op jit(solution)/shard_map/ppermute | solution.py:22
  168.7 3.4 %all-to-all-start.1 = ((bf16[8,32,512]{2,1,0:T(8,128)(2,1)}), bf16[8,32,512]{2,1,0:T(8,128)(2,1)S(1)}, u32[]{:S(2)}, u32[]{:S(2)}) async-start(bf16[8,32,512]{2,1,0:T(8,128)(2,1)} %bitcast.137), calls=%async_computation.1 | async-start | bytes 524288 | tf_op jit(solution)/shard_map/all_to_all | solution.py:191
  174.6 5.6 %shard_map.88 = (bf16[512,512]{1,0:T(8,128)(2,1)}, bf16[512,512]{1,0:T(8,128)(2,1)}, bf16[512,512]{1,0:T(8,128)(2,1)}) custom-call(bf16[384,512]{1,0:T(8,128)(2,1)S(1)} %bitcast.127, bf16[384,512]{1,0:T(8,128)(2,1)S(1)} %copy-done.3, bf16[384,512]{1,0:T(8,128)(2,1)S(1)} %copy-done.5, bf16[384,512]{1,0:T(8,128)(2,1)S(1)} %copy-done.7, ...), custom_call_target="tpu_custom_call" | custom-call | tf_op jit(solution)/shard_map/pallas_call | solution.py:95
  180.2 4.2 %all-to-all-done.1 = bf16[8,32,512]{2,1,0:T(8,128)(2,1)S(1)} async-done(((bf16[8,32,512]{2,1,0:T(8,128)(2,1)}), bf16[8,32,512]{2,1,0:T(8,128)(2,1)S(1)}, u32[]{:S(2)}, u32[]{:S(2)}) %all-to-all-start.1) | async-done | bytes 262176 | tf_op jit(solution)/shard_map/all_to_all | solution.py:191
  (116 shorter events, 57.1 us)
Async XLA Ops:
  2.4 21.9 %all-to-all-start = ((bf16[8,32,1024]{2,1,0:T(8,128)(2,1)}), bf16[8,32,1024]{2,1,0:T(8,128)(2,1)}, u32[]{:S(2)}, u32[]{:S(2)}) async-start(bf16[8,32,1024]{2,1,0:T(8,128)(2,1)} %broadcast_in_dim.4), calls=%async_computation | async-start | bytes 1048576 | tf_op jit(solution)/shard_map/all_to_all | solution.py:117
  10.1 10.0 %collective-permute-start.1 = (bf16[512,512]{1,0:T(8,128)(2,1)S(1)}, bf16[512,512]{1,0:T(8,128)(2,1)S(1)}, u32[]{:S(2)}, u32[]{:S(2)}) collective-permute-start(bf16[512,512]{1,0:T(8,128)(2,1)S(1)} %copy-done.14), channel_id=1, source_target_pairs={{0,1},{1,0},{2,3},{3,2},{4,5},{5,4},{6,7},{7,6},{8,9},{9,8},{10,11... | collective-permute-start | bytes 1572872 | tf_op jit(solution)/shard_map/ppermute | solution.py:22
  24.3 22.6 %collective-permute-start = (bf16[256,1024]{1,0:T(8,128)(2,1)}, bf16[256,1024]{1,0:T(8,128)(2,1)S(1)}, u32[]{:S(2)}, u32[]{:S(2)}) collective-permute-start(bf16[256,1024]{1,0:T(8,128)(2,1)} %bitcast), channel_id=1, source_target_pairs={{0,2},{2,0},{1,3},{3,1},{4,6},{6,4},{5,7},{7,5},{8,10},{10,8},{9,1... | collective-permute-start | bytes 1572872 | tf_op jit(solution)/shard_map/ppermute | solution.py:22
  40.2 17.5 %collective-permute-start.4 = (f16[384,256]{1,0:T(8,128)(2,1)S(1)}, f16[384,256]{1,0:T(8,128)(2,1)S(1)}, u32[]{:S(2)}, u32[]{:S(2)}) collective-permute-start(f16[384,256]{1,0:T(8,128)(2,1)S(1)} %fusion.7), channel_id=1, source_target_pairs={{0,64},{64,128},{128,192},{192,256},{256,320},{320,384},{384,448},... | collective-permute-start | bytes 589832 | tf_op jit(solution)/shard_map/ppermute | solution.py:147
  48.9 11.9 %collective-permute-start.8 = (f16[384,256]{1,0:T(8,128)(2,1)S(1)}, f16[384,256]{1,0:T(8,128)(2,1)S(1)}, u32[]{:S(2)}, u32[]{:S(2)}) collective-permute-start(f16[384,256]{1,0:T(8,128)(2,1)S(1)} %pad_maximum_fusion.4), channel_id=1, source_target_pairs={{0,448},{64,0},{128,64},{192,128},{256,192},{320,256},{384,320},{4... | collective-permute-start | bytes 589832 | tf_op jit(solution)/shard_map/ppermute | solution.py:148
  57.8 12.2 %collective-permute-start.5 = (f16[384,512]{1,0:T(8,128)(2,1)S(1)}, f16[384,512]{1,0:T(8,128)(2,1)S(1)}, u32[]{:S(2)}, u32[]{:S(2)}) collective-permute-start(f16[384,512]{1,0:T(8,128)(2,1)S(1)} %fusion.3), channel_id=1, source_target_pairs={{0,64},{64,128},{128,192},{192,256},{256,320},{320,384},{384,448},... | collective-permute-start | bytes 1179656 | tf_op jit(solution)/shard_map/ppermute | solution.py:152
  60.9 11.3 %collective-permute-start.9 = (f16[384,512]{1,0:T(8,128)(2,1)S(1)}, f16[384,512]{1,0:T(8,128)(2,1)S(1)}, u32[]{:S(2)}, u32[]{:S(2)}) collective-permute-start(f16[384,512]{1,0:T(8,128)(2,1)S(1)} %fusion.6), channel_id=1, source_target_pairs={{0,448},{64,0},{128,64},{192,128},{256,192},{320,256},{384,320},{4... | collective-permute-start | bytes 1179656 | tf_op jit(solution)/shard_map/ppermute | solution.py:153
  70.2 12.9 %collective-permute-start.6 = (f16[384,512]{1,0:T(8,128)(2,1)S(1)}, f16[384,512]{1,0:T(8,128)(2,1)S(1)}, u32[]{:S(2)}, u32[]{:S(2)}) collective-permute-start(f16[384,512]{1,0:T(8,128)(2,1)S(1)} %fusion.2), channel_id=1, source_target_pairs={{0,64},{64,128},{128,192},{192,256},{256,320},{320,384},{384,448},... | collective-permute-start | bytes 1179656 | tf_op jit(solution)/shard_map/ppermute | solution.py:152
  72.3 12.8 %collective-permute-start.10 = (f16[384,512]{1,0:T(8,128)(2,1)S(1)}, f16[384,512]{1,0:T(8,128)(2,1)S(1)}, u32[]{:S(2)}, u32[]{:S(2)}) collective-permute-start(f16[384,512]{1,0:T(8,128)(2,1)S(1)} %fusion.5), channel_id=1, source_target_pairs={{0,448},{64,0},{128,64},{192,128},{256,192},{320,256},{384,320},{4... | collective-permute-start | bytes 1179656 | tf_op jit(solution)/shard_map/ppermute | solution.py:153
  77.8 21.1 %collective-permute-start.13 = (bf16[2,512,512]{2,1,0:T(8,128)(2,1)S(1)}, bf16[2,512,512]{2,1,0:T(8,128)(2,1)S(1)}, u32[]{:S(2)}, u32[]{:S(2)}) collective-permute-start(bf16[2,512,512]{2,1,0:T(8,128)(2,1)S(1)} %pad_maximum_fusion.1.refs_9_), channel_id=1, source_target_pairs={{0,1},{1,0},{2,3},{3,2},{4,5},{5,4},{6,7},{7,6},{8,9},{9,8},{10,11... | collective-permute-start | bytes 3145736 | tf_op jit(solution)/shard_map/ppermute | solution.py:22
  83.2 11.9 %collective-permute-start.7 = (f16[384,512]{1,0:T(8,128)(2,1)S(1)}, f16[384,512]{1,0:T(8,128)(2,1)S(1)}, u32[]{:S(2)}, u32[]{:S(2)}) collective-permute-start(f16[384,512]{1,0:T(8,128)(2,1)S(1)} %fusion.1), channel_id=1, source_target_pairs={{0,64},{64,128},{128,192},{192,256},{256,320},{320,384},{384,448},... | collective-permute-start | bytes 1179656 | tf_op jit(solution)/shard_map/ppermute | solution.py:152
  85.2 10.7 %collective-permute-start.11 = (f16[384,512]{1,0:T(8,128)(2,1)S(1)}, f16[384,512]{1,0:T(8,128)(2,1)S(1)}, u32[]{:S(2)}, u32[]{:S(2)}) collective-permute-start(f16[384,512]{1,0:T(8,128)(2,1)S(1)} %fusion.4), channel_id=1, source_target_pairs={{0,448},{64,0},{128,64},{192,128},{256,192},{320,256},{384,320},{4... | collective-permute-start | bytes 1179656 | tf_op jit(solution)/shard_map/ppermute | solution.py:153
  96.1 9.3 %collective-permute-start.12 = (f16[384,512]{1,0:T(8,128)(2,1)S(1)}, f16[384,512]{1,0:T(8,128)(2,1)S(1)}, u32[]{:S(2)}, u32[]{:S(2)}) collective-permute-start(f16[384,512]{1,0:T(8,128)(2,1)S(1)} %fusion.38), channel_id=1, source_target_pairs={{0,32},{32,0},{1,33},{33,1},{2,34},{34,2},{3,35},{35,3},{4,36},{36... | collective-permute-start | bytes 1179656 | tf_op jit(solution)/shard_map/ppermute | solution.py:22
  105.8 9.9 %collective-permute-start.17 = (bf16[384,512]{1,0:T(8,128)(2,1)S(1)}, bf16[384,512]{1,0:T(8,128)(2,1)S(1)}, u32[]{:S(2)}, u32[]{:S(2)}) collective-permute-start(bf16[384,512]{1,0:T(8,128)(2,1)S(1)} %bitcast.123), channel_id=1, source_target_pairs={{0,64},{64,128},{128,192},{192,256},{256,320},{320,384},{384,448},... | collective-permute-start | bytes 1179656 | tf_op jit(solution)/shard_map/ppermute | solution.py:170
  107.7 9.9 %collective-permute-start.14 = (bf16[384,512]{1,0:T(8,128)(2,1)S(1)}, bf16[384,512]{1,0:T(8,128)(2,1)S(1)}, u32[]{:S(2)}, u32[]{:S(2)}) collective-permute-start(bf16[384,512]{1,0:T(8,128)(2,1)S(1)} %bitcast.124), channel_id=1, source_target_pairs={{0,448},{64,0},{128,64},{192,128},{256,192},{320,256},{384,320},{4... | collective-permute-start | bytes 1179656 | tf_op jit(solution)/shard_map/ppermute | solution.py:171
  115.7 9.7 %collective-permute-start.18 = (bf16[384,512]{1,0:T(8,128)(2,1)S(1)}, bf16[384,512]{1,0:T(8,128)(2,1)S(1)}, u32[]{:S(2)}, u32[]{:S(2)}) collective-permute-start(bf16[384,512]{1,0:T(8,128)(2,1)S(1)} %collective-permute-done.17.refs_7_.refs_1_), channel_id=1, source_target_pairs={{0,64},{64,128},{128,192},{192,256},{256,320},{320,384},{384,448},... | collective-permute-start | bytes 1179656 | tf_op jit(solution)/shard_map/ppermute | solution.py:170
  117.6 9.7 %collective-permute-start.15 = (bf16[384,512]{1,0:T(8,128)(2,1)S(1)}, bf16[384,512]{1,0:T(8,128)(2,1)S(1)}, u32[]{:S(2)}, u32[]{:S(2)}) collective-permute-start(bf16[384,512]{1,0:T(8,128)(2,1)S(1)} %collective-permute-done.14.refs_1_.refs_2_), channel_id=1, source_target_pairs={{0,448},{64,0},{128,64},{192,128},{256,192},{320,256},{384,320},{4... | collective-permute-start | bytes 1179656 | tf_op jit(solution)/shard_map/ppermute | solution.py:171
  125.4 10.0 %collective-permute-start.19 = (bf16[384,512]{1,0:T(8,128)(2,1)S(1)}, bf16[384,512]{1,0:T(8,128)(2,1)S(1)}, u32[]{:S(2)}, u32[]{:S(2)}) collective-permute-start(bf16[384,512]{1,0:T(8,128)(2,1)S(1)} %collective-permute-done.18.refs_6_.refs_3_), channel_id=1, source_target_pairs={{0,64},{64,128},{128,192},{192,256},{256,320},{320,384},{384,448},... | collective-permute-start | bytes 1179656 | tf_op jit(solution)/shard_map/ppermute | solution.py:170
  127.4 10.0 %collective-permute-start.16 = (bf16[384,512]{1,0:T(8,128)(2,1)S(1)}, bf16[384,512]{1,0:T(8,128)(2,1)S(1)}, u32[]{:S(2)}, u32[]{:S(2)}) collective-permute-start(bf16[384,512]{1,0:T(8,128)(2,1)S(1)} %collective-permute-done.15.refs_2_.refs_4_), channel_id=1, source_target_pairs={{0,448},{64,0},{128,64},{192,128},{256,192},{320,256},{384,320},{4... | collective-permute-start | bytes 1179656 | tf_op jit(solution)/shard_map/ppermute | solution.py:171
  135.4 8.9 %collective-permute-start.20 = (bf16[384,256]{1,0:T(8,128)(2,1)S(1)}, bf16[384,256]{1,0:T(8,128)(2,1)S(1)}, u32[]{:S(2)}, u32[]{:S(2)}) collective-permute-start(bf16[384,256]{1,0:T(8,128)(2,1)S(1)} %slice.398), channel_id=1, source_target_pairs={{0,64},{64,128},{128,192},{192,256},{256,320},{320,384},{384,448},... | collective-permute-start | bytes 589832 | tf_op jit(solution)/shard_map/ppermute | solution.py:174
  137.4 9.0 %collective-permute-start.21 = (bf16[384,256]{1,0:T(8,128)(2,1)S(1)}, bf16[384,256]{1,0:T(8,128)(2,1)S(1)}, u32[]{:S(2)}, u32[]{:S(2)}) collective-permute-start(bf16[384,256]{1,0:T(8,128)(2,1)S(1)} %slice.399), channel_id=1, source_target_pairs={{0,448},{64,0},{128,64},{192,128},{256,192},{320,256},{384,320},{4... | collective-permute-start | bytes 589832 | tf_op jit(solution)/shard_map/ppermute | solution.py:175
  147.7 8.6 %collective-permute-start.22 = (bf16[256,512]{1,0:T(8,128)(2,1)S(1)}, bf16[256,512]{1,0:T(8,128)(2,1)S(1)}, u32[]{:S(2)}, u32[]{:S(2)}) collective-permute-start(bf16[256,512]{1,0:T(8,128)(2,1)S(1)} %shard_map.86), channel_id=1, source_target_pairs={{0,2},{2,0},{1,3},{3,1},{4,6},{6,4},{5,7},{7,5},{8,10},{10,8},{9,1... | collective-permute-start | bytes 786440 | tf_op jit(solution)/shard_map/ppermute | solution.py:22
  156.3 15.8 %collective-permute-start.23 = (bf16[8,192,512]{2,1,0:T(8,128)(2,1)}, bf16[8,192,512]{2,1,0:T(8,128)(2,1)}, u32[]{:S(2)}, u32[]{:S(2)}) collective-permute-start(bf16[8,192,512]{2,1,0:T(8,128)(2,1)} %pad_maximum_fusion), channel_id=1, source_target_pairs={{0,1},{1,0},{2,3},{3,2},{4,5},{5,4},{6,7},{7,6},{8,9},{9,8},{10,11... | collective-permute-start | bytes 4718600 | tf_op jit(solution)/shard_map/ppermute | solution.py:22
  168.7 15.7 %all-to-all-start.1 = ((bf16[8,32,512]{2,1,0:T(8,128)(2,1)}), bf16[8,32,512]{2,1,0:T(8,128)(2,1)S(1)}, u32[]{:S(2)}, u32[]{:S(2)}) async-start(bf16[8,32,512]{2,1,0:T(8,128)(2,1)} %bitcast.137), calls=%async_computation.1 | async-start | bytes 524288 | tf_op jit(solution)/shard_map/all_to_all | solution.py:191
  (19 other events, 286.0 us)

commit v8 on v7

--- a/solution.py
+++ b/solution.py
@@ -49,23 +49,23 @@
     )(wg, wu, wd)
 
 
-def input_kernel(nz, at, *refs):
-    chunks, (own_ref, oth_ref, out_ref) = refs[:nz], refs[nz:]
+def input_kernel(order, at, *refs):
+    chunks, (own_ref, oth_ref, out_ref) = refs[: len(refs) - 3], refs[len(refs) - 3 :]
     n, h, step = out_ref.shape[0], own_ref.shape[1], chunks[0].shape[0] // 2
     total = jnp.zeros(out_ref.shape, F32)
-    for k in range(nz):
+    for k, chunk in zip(order, chunks):
         for i, ref in enumerate((own_ref, oth_ref)):
-            deltas = chunks[k][i * step : i * step + h, at : at + n]
+            deltas = chunk[i * step : i * step + h, at : at + n]
             total += lax.dot_general(
                 deltas, ref[k], (((0,), (0,)), ((), ())), preferred_element_type=F32
             )
-    out_ref[...] = total.astype(out_ref.dtype)
-
-
-def input_grads(chunks, own, oth, at, n, dtype):
+    out_ref[...] = total
+
+
+def input_grads(chunks, order, own, oth, at, n):
     return pl.pallas_call(
-        functools.partial(input_kernel, len(chunks), at),
-        out_shape=jax.ShapeDtypeStruct((n, own.shape[2]), dtype),
+        functools.partial(input_kernel, order, at),
+        out_shape=jax.ShapeDtypeStruct((n, own.shape[2]), F32),
         compiler_params=pltpu.CompilerParams(vmem_limit_bytes=16 * 2**20),
     )(*chunks, own, oth)
 
@@ -179,11 +179,13 @@
 
     order = [0] + [j for i in range(1, far) for j in (nz - i, i)] + [far]
     deltas = jnp.stack([chunk[k][3 * zf :] for k in order[:-1]])
-    chunk[far], deltas = tie(chunk[far], deltas)
-    send = input_grads(chunk, gu_own, gu_oth, part_tokens, part_tokens, BF16)
-    send, *chunk = tie(send, *chunk)
+    send = input_grads([chunk[k] for k in order[:-1]], order, gu_own, gu_oth, part_tokens, part_tokens)
+    chunk[far], deltas, send = tie(chunk[far], deltas, send)
+    for i, w in enumerate((gu_own, gu_oth)):
+        send = send + dot(chunk[far][3 * zf * i : 3 * zf * i + 2 * zf, part_tokens:], w[far], 0, 0)
+    send, *chunk = tie(send.astype(BF16), *chunk)
     got = swap(send, "xh")
-    total = input_grads(chunk, gu_own, gu_oth, 0, part_tokens, F32)
+    total = input_grads([chunk[k] for k in order], order, gu_own, gu_oth, 0, part_tokens)
     deltas = jnp.concatenate([deltas, chunk[far][None, 3 * zf :]], axis=0)
     got, total, deltas = tie(got, total, deltas)
     deltas = swap(deltas, "core")

time: 186 us -> 190 us (1.022)
    ppermute x3, waiting for transfers between devices: 9.72 us -> 0.33 us  [per_device(): chunk[nz - k] = lax.ppermute(chunk[(nz - k + 1) % nz], 'z', right)]
    ppermute x3, waiting for transfers between devices: 0.01 us -> 8.64 us  [per_device(): chunk[k] = lax.ppermute(chunk[k - 1], 'z', left)]
    ppermute x1, waiting for transfers between devices: 2.05 us -> 5.61 us  [per_device(): lax.ppermute(chunk[far + 1][:, :part_tokens], 'z', right)]
    dot_general x12 -> x14, matrix products: 11.7 us -> 12.2 us  [dot(): lax.dot_general(a, b, (((ca,), (cb,)), ((), ())), preferred_element_type=...]
  transfers between devices with their start and end apart: 26 -> 26, of which waited for: 14 -> 15; matrix products, arithmetic and copies ran while one was open for 9% -> 9% of each run, Pallas kernels for 4% -> 5%
where the time goes in v8:
time: 190 us; the launch traced here: 189 us
  starting transfers between devices  114 us (60%)
  waiting for transfers between devices  40.8 us (21%)
  matrix products  12.2 us (6%)
  Pallas kernels  8.68 us (5%)
  local copies, waits for them, and re-layouts  5.82 us (3%)
  other arithmetic  5.45 us (3%)
    ppermute x8, starting transfers between devices, swap(): return lax.ppermute(x, axis, [(0, 1), (1, 0)])  42.7 us
    ppermute x3, starting transfers between devices, per_device(): l = lax.ppermute((part(nz - k) + l).astype(F16), 'z', left).astype(F32)  14.9 us
    ppermute x3, starting transfers between devices, per_device(): chunk[k] = lax.ppermute(chunk[k - 1], 'z', left)  14.8 us
    dot_general x14, matrix products, dot(): lax.dot_general(a, b, (((ca,), (cb,)), ((), ())), preferred_element_type=...  12.2 us
    ppermute x3, waiting for transfers between devices, per_device(): r = lax.ppermute((part(k) + r).astype(F16), 'z', right).astype(F32)  9.44 us
    ppermute x3, waiting for transfers between devices, per_device(): chunk[k] = lax.ppermute(chunk[k - 1], 'z', left)  8.64 us
    ppermute x1, starting transfers between devices, per_device(): l = lax.ppermute(half_part(1, far).astype(F16), 'z', left).astype(F32)  8.59 us
    ppermute x8, waiting for transfers between devices, swap(): return lax.ppermute(x, axis, [(0, 1), (1, 0)])  8.18 us
  transfers between devices with their start and end apart: 26, of which 15 were waited for; matrix products, arithmetic and copies ran while one was open for 9% of the time, Pallas kernels for 5%

profile of v8, /device:TPU:1, one launch (start us, length us, event | category | flops | bytes accessed | tf_op | source)
XLA Modules:
  0.0 188.7 jit_solution(3199210504606766058)
XLA Ops:
  2.4 7.7 %all-to-all-start = ((bf16[8,32,1024]{2,1,0:T(8,128)(2,1)}), bf16[8,32,1024]{2,1,0:T(8,128)(2,1)}, u32[]{:S(2)}, u32[]{:S(2)}) async-start(bf16[8,32,1024]{2,1,0:T(8,128)(2,1)} %broadcast_in_dim.4), calls=%async_computation | async-start | bytes 1048576 | tf_op jit(solution)/shard_map/all_to_all | solution.py:117
  10.1 5.3 %collective-permute-start.1 = (bf16[512,512]{1,0:T(8,128)(2,1)S(1)}, bf16[512,512]{1,0:T(8,128)(2,1)S(1)}, u32[]{:S(2)}, u32[]{:S(2)}) collective-permute-start(bf16[512,512]{1,0:T(8,128)(2,1)S(1)} %copy-done.14), channel_id=1, source_target_pairs={{0,1},{1,0},{2,3},{3,2},{4,5},{5,4},{6,7},{7,6},{8,9},{9,8},{10,11... | collective-permute-start | bytes 1572872 | tf_op jit(solution)/shard_map/ppermute | solution.py:22
  24.3 8.4 %collective-permute-start = (bf16[256,1024]{1,0:T(8,128)(2,1)}, bf16[256,1024]{1,0:T(8,128)(2,1)S(1)}, u32[]{:S(2)}, u32[]{:S(2)}) collective-permute-start(bf16[256,1024]{1,0:T(8,128)(2,1)} %bitcast), channel_id=1, source_target_pairs={{0,2},{2,0},{1,3},{3,1},{4,6},{6,4},{5,7},{7,5},{8,10},{10,8},{9,1... | collective-permute-start | bytes 1572872 | tf_op jit(solution)/shard_map/ppermute | solution.py:22
  40.2 4.0 %collective-permute-start.4 = (f16[384,256]{1,0:T(8,128)(2,1)S(1)}, f16[384,256]{1,0:T(8,128)(2,1)S(1)}, u32[]{:S(2)}, u32[]{:S(2)}) collective-permute-start(f16[384,256]{1,0:T(8,128)(2,1)S(1)} %fusion.7), channel_id=1, source_target_pairs={{0,64},{64,128},{128,192},{192,256},{256,320},{320,384},{384,448},... | collective-permute-start | bytes 589832 | tf_op jit(solution)/shard_map/ppermute | solution.py:147
  48.9 8.6 %collective-permute-start.8 = (f16[384,256]{1,0:T(8,128)(2,1)S(1)}, f16[384,256]{1,0:T(8,128)(2,1)S(1)}, u32[]{:S(2)}, u32[]{:S(2)}) collective-permute-start(f16[384,256]{1,0:T(8,128)(2,1)S(1)} %pad_maximum_fusion.4), channel_id=1, source_target_pairs={{0,448},{64,0},{128,64},{192,128},{256,192},{320,256},{384,320},{4... | collective-permute-start | bytes 589832 | tf_op jit(solution)/shard_map/ppermute | solution.py:148
  60.9 5.0 %collective-permute-start.9 = (f16[384,512]{1,0:T(8,128)(2,1)S(1)}, f16[384,512]{1,0:T(8,128)(2,1)S(1)}, u32[]{:S(2)}, u32[]{:S(2)}) collective-permute-start(f16[384,512]{1,0:T(8,128)(2,1)S(1)} %fusion.6), channel_id=1, source_target_pairs={{0,448},{64,0},{128,64},{192,128},{256,192},{320,256},{384,320},{4... | collective-permute-start | bytes 1179656 | tf_op jit(solution)/shard_map/ppermute | solution.py:153
  66.0 4.1 %collective-permute-done.5 = f16[384,512]{1,0:T(8,128)(2,1)S(1)} collective-permute-done((f16[384,512]{1,0:T(8,128)(2,1)S(1)}, f16[384,512]{1,0:T(8,128)(2,1)S(1)}, u32[]{:S(2)}, u32[]{:S(2)}) %collective-permute-start.5) | collective-permute-done | bytes 393248 | tf_op jit(solution)/shard_map/ppermute | solution.py:152
  72.3 5.3 %collective-permute-start.10 = (f16[384,512]{1,0:T(8,128)(2,1)S(1)}, f16[384,512]{1,0:T(8,128)(2,1)S(1)}, u32[]{:S(2)}, u32[]{:S(2)}) collective-permute-start(f16[384,512]{1,0:T(8,128)(2,1)S(1)} %fusion.5), channel_id=1, source_target_pairs={{0,448},{64,0},{128,64},{192,128},{256,192},{320,256},{384,320},{4... | collective-permute-start | bytes 1179656 | tf_op jit(solution)/shard_map/ppermute | solution.py:153
  77.8 5.2 %collective-permute-start.13 = (bf16[2,512,512]{2,1,0:T(8,128)(2,1)S(1)}, bf16[2,512,512]{2,1,0:T(8,128)(2,1)S(1)}, u32[]{:S(2)}, u32[]{:S(2)}) collective-permute-start(bf16[2,512,512]{2,1,0:T(8,128)(2,1)S(1)} %pad_maximum_fusion.1.refs_9_), channel_id=1, source_target_pairs={{0,1},{1,0},{2,3},{3,2},{4,5},{5,4},{6,7},{7,6},{8,9},{9,8},{10,11... | collective-permute-start | bytes 3145736 | tf_op jit(solution)/shard_map/ppermute | solution.py:22
  85.2 4.6 %collective-permute-start.11 = (f16[384,512]{1,0:T(8,128)(2,1)S(1)}, f16[384,512]{1,0:T(8,128)(2,1)S(1)}, u32[]{:S(2)}, u32[]{:S(2)}) collective-permute-start(f16[384,512]{1,0:T(8,128)(2,1)S(1)} %fusion.4), channel_id=1, source_target_pairs={{0,448},{64,0},{128,64},{192,128},{256,192},{320,256},{384,320},{4... | collective-permute-start | bytes 1179656 | tf_op jit(solution)/shard_map/ppermute | solution.py:153
  89.8 5.3 %collective-permute-done.7 = f16[384,512]{1,0:T(8,128)(2,1)S(1)} collective-permute-done((f16[384,512]{1,0:T(8,128)(2,1)S(1)}, f16[384,512]{1,0:T(8,128)(2,1)S(1)}, u32[]{:S(2)}, u32[]{:S(2)}) %collective-permute-start.7) | collective-permute-done | bytes 393248 | tf_op jit(solution)/shard_map/ppermute | solution.py:152
  96.1 2.9 %collective-permute-start.12 = (f16[384,512]{1,0:T(8,128)(2,1)S(1)}, f16[384,512]{1,0:T(8,128)(2,1)S(1)}, u32[]{:S(2)}, u32[]{:S(2)}) collective-permute-start(f16[384,512]{1,0:T(8,128)(2,1)S(1)} %fusion.46), channel_id=1, source_target_pairs={{0,32},{32,0},{1,33},{33,1},{2,34},{34,2},{3,35},{35,3},{4,36},{36... | collective-permute-start | bytes 1179656 | tf_op jit(solution)/shard_map/ppermute | solution.py:22
  99.9 5.4 %collective-permute-done.12 = f16[384,512]{1,0:T(8,128)(2,1)S(1)} collective-permute-done((f16[384,512]{1,0:T(8,128)(2,1)S(1)}, f16[384,512]{1,0:T(8,128)(2,1)S(1)}, u32[]{:S(2)}, u32[]{:S(2)}) %collective-permute-start.12) | collective-permute-done | bytes 393248 | tf_op jit(solution)/shard_map/ppermute | solution.py:22
  105.8 4.8 %collective-permute-start.18 = (bf16[384,512]{1,0:T(8,128)(2,1)S(1)}, bf16[384,512]{1,0:T(8,128)(2,1)S(1)}, u32[]{:S(2)}, u32[]{:S(2)}) collective-permute-start(bf16[384,512]{1,0:T(8,128)(2,1)S(1)} %bitcast.127), channel_id=1, source_target_pairs={{0,448},{64,0},{128,64},{192,128},{256,192},{320,256},{384,320},{4... | collective-permute-start | bytes 1179656 | tf_op jit(solution)/shard_map/ppermute | solution.py:171
  115.2 5.0 %collective-permute-start.19 = (bf16[384,512]{1,0:T(8,128)(2,1)S(1)}, bf16[384,512]{1,0:T(8,128)(2,1)S(1)}, u32[]{:S(2)}, u32[]{:S(2)}) collective-permute-start(bf16[384,512]{1,0:T(8,128)(2,1)S(1)} %collective-permute-done.18.refs_2_), channel_id=1, source_target_pairs={{0,448},{64,0},{128,64},{192,128},{256,192},{320,256},{384,320},{4... | collective-permute-start | bytes 1179656 | tf_op jit(solution)/shard_map/ppermute | solution.py:171
  125.0 5.0 %collective-permute-start.20 = (bf16[384,512]{1,0:T(8,128)(2,1)S(1)}, bf16[384,512]{1,0:T(8,128)(2,1)S(1)}, u32[]{:S(2)}, u32[]{:S(2)}) collective-permute-start(bf16[384,512]{1,0:T(8,128)(2,1)S(1)} %collective-permute-done.19.refs_4_), channel_id=1, source_target_pairs={{0,448},{64,0},{128,64},{192,128},{256,192},{320,256},{384,320},{4... | collective-permute-start | bytes 1179656 | tf_op jit(solution)/shard_map/ppermute | solution.py:171
  132.0 3.2 %collective-permute-done.20.refs_6_ = bf16[384,512]{1,0:T(8,128)(2,1)S(1)} collective-permute-done((bf16[384,512]{1,0:T(8,128)(2,1)S(1)}, bf16[384,512]{1,0:T(8,128)(2,1)S(1)}, u32[]{:S(2)}, u32[]{:S(2)}) %collective-permute-start.20) | collective-permute-done | bytes 393248 | tf_op jit(solution)/shard_map/ppermute | solution.py:171
  135.2 5.0 %collective-permute-start.21 = (bf16[384,256]{1,0:T(8,128)(2,1)S(1)}, bf16[384,256]{1,0:T(8,128)(2,1)S(1)}, u32[]{:S(2)}, u32[]{:S(2)}) collective-permute-start(bf16[384,256]{1,0:T(8,128)(2,1)S(1)} %slice.409), channel_id=1, source_target_pairs={{0,448},{64,0},{128,64},{192,128},{256,192},{320,256},{384,320},{4... | collective-permute-start | bytes 589832 | tf_op jit(solution)/shard_map/ppermute | solution.py:175
  144.4 5.6 %collective-permute-done.17 = bf16[384,256]{1,0:T(8,128)(2,1)S(1)} collective-permute-done((bf16[384,256]{1,0:T(8,128)(2,1)S(1)}, bf16[384,256]{1,0:T(8,128)(2,1)S(1)}, u32[]{:S(2)}, u32[]{:S(2)}) %collective-permute-start.17) | collective-permute-done | bytes 196640 | tf_op jit(solution)/shard_map/ppermute | solution.py:174
  150.7 4.4 %collective-permute-start.22 = (bf16[256,512]{1,0:T(8,128)(2,1)S(1)}, bf16[256,512]{1,0:T(8,128)(2,1)S(1)}, u32[]{:S(2)}, u32[]{:S(2)}) collective-permute-start(bf16[256,512]{1,0:T(8,128)(2,1)S(1)} %add_convert_fusion.1), channel_id=1, source_target_pairs={{0,2},{2,0},{1,3},{3,1},{4,6},{6,4},{5,7},{7,5},{8,10},{10,8},{9,1... | collective-permute-start | bytes 786440 | tf_op jit(solution)/shard_map/ppermute | solution.py:22
  159.4 12.2 %collective-permute-start.23 = (bf16[8,192,512]{2,1,0:T(8,128)(2,1)}, bf16[8,192,512]{2,1,0:T(8,128)(2,1)}, u32[]{:S(2)}, u32[]{:S(2)}) collective-permute-start(bf16[8,192,512]{2,1,0:T(8,128)(2,1)} %pad_maximum_fusion), channel_id=1, source_target_pairs={{0,1},{1,0},{2,3},{3,2},{4,5},{5,4},{6,7},{7,6},{8,9},{9,8},{10,11... | collective-permute-start | bytes 4718600 | tf_op jit(solution)/shard_map/ppermute | solution.py:22
  172.3 3.4 %all-to-all-start.1 = ((bf16[8,32,512]{2,1,0:T(8,128)(2,1)}), bf16[8,32,512]{2,1,0:T(8,128)(2,1)S(1)}, u32[]{:S(2)}, u32[]{:S(2)}) async-start(bf16[8,32,512]{2,1,0:T(8,128)(2,1)} %bitcast.141), calls=%async_computation.1 | async-start | bytes 524288 | tf_op jit(solution)/shard_map/all_to_all | solution.py:193
  178.3 5.6 %shard_map.88 = (bf16[512,512]{1,0:T(8,128)(2,1)}, bf16[512,512]{1,0:T(8,128)(2,1)}, bf16[512,512]{1,0:T(8,128)(2,1)}) custom-call(bf16[384,512]{1,0:T(8,128)(2,1)S(1)} %bitcast.131, bf16[384,512]{1,0:T(8,128)(2,1)S(1)} %copy-done.5, bf16[384,512]{1,0:T(8,128)(2,1)S(1)} %copy-done.3, bf16[384,512]{1,0:T(8,128)(2,1)S(1)} %copy-done.9, ...), custom_call_target="tpu_custom_call" | custom-call | tf_op jit(solution)/shard_map/pallas_call | solution.py:95
  183.9 4.2 %all-to-all-done.1 = bf16[8,32,512]{2,1,0:T(8,128)(2,1)S(1)} async-done(((bf16[8,32,512]{2,1,0:T(8,128)(2,1)}), bf16[8,32,512]{2,1,0:T(8,128)(2,1)S(1)}, u32[]{:S(2)}, u32[]{:S(2)}) %all-to-all-start.1) | async-done | bytes 262176 | tf_op jit(solution)/shard_map/all_to_all | solution.py:193
  (119 shorter events, 57.2 us)
Async XLA Ops:
  2.4 21.9 %all-to-all-start = ((bf16[8,32,1024]{2,1,0:T(8,128)(2,1)}), bf16[8,32,1024]{2,1,0:T(8,128)(2,1)}, u32[]{:S(2)}, u32[]{:S(2)}) async-start(bf16[8,32,1024]{2,1,0:T(8,128)(2,1)} %broadcast_in_dim.4), calls=%async_computation | async-start | bytes 1048576 | tf_op jit(solution)/shard_map/all_to_all | solution.py:117
  10.1 10.0 %collective-permute-start.1 = (bf16[512,512]{1,0:T(8,128)(2,1)S(1)}, bf16[512,512]{1,0:T(8,128)(2,1)S(1)}, u32[]{:S(2)}, u32[]{:S(2)}) collective-permute-start(bf16[512,512]{1,0:T(8,128)(2,1)S(1)} %copy-done.14), channel_id=1, source_target_pairs={{0,1},{1,0},{2,3},{3,2},{4,5},{5,4},{6,7},{7,6},{8,9},{9,8},{10,11... | collective-permute-start | bytes 1572872 | tf_op jit(solution)/shard_map/ppermute | solution.py:22
  24.3 22.6 %collective-permute-start = (bf16[256,1024]{1,0:T(8,128)(2,1)}, bf16[256,1024]{1,0:T(8,128)(2,1)S(1)}, u32[]{:S(2)}, u32[]{:S(2)}) collective-permute-start(bf16[256,1024]{1,0:T(8,128)(2,1)} %bitcast), channel_id=1, source_target_pairs={{0,2},{2,0},{1,3},{3,1},{4,6},{6,4},{5,7},{7,5},{8,10},{10,8},{9,1... | collective-permute-start | bytes 1572872 | tf_op jit(solution)/shard_map/ppermute | solution.py:22
  40.2 17.5 %collective-permute-start.4 = (f16[384,256]{1,0:T(8,128)(2,1)S(1)}, f16[384,256]{1,0:T(8,128)(2,1)S(1)}, u32[]{:S(2)}, u32[]{:S(2)}) collective-permute-start(f16[384,256]{1,0:T(8,128)(2,1)S(1)} %fusion.7), channel_id=1, source_target_pairs={{0,64},{64,128},{128,192},{192,256},{256,320},{320,384},{384,448},... | collective-permute-start | bytes 589832 | tf_op jit(solution)/shard_map/ppermute | solution.py:147
  48.9 11.9 %collective-permute-start.8 = (f16[384,256]{1,0:T(8,128)(2,1)S(1)}, f16[384,256]{1,0:T(8,128)(2,1)S(1)}, u32[]{:S(2)}, u32[]{:S(2)}) collective-permute-start(f16[384,256]{1,0:T(8,128)(2,1)S(1)} %pad_maximum_fusion.4), channel_id=1, source_target_pairs={{0,448},{64,0},{128,64},{192,128},{256,192},{320,256},{384,320},{4... | collective-permute-start | bytes 589832 | tf_op jit(solution)/shard_map/ppermute | solution.py:148
  57.8 12.2 %collective-permute-start.5 = (f16[384,512]{1,0:T(8,128)(2,1)S(1)}, f16[384,512]{1,0:T(8,128)(2,1)S(1)}, u32[]{:S(2)}, u32[]{:S(2)}) collective-permute-start(f16[384,512]{1,0:T(8,128)(2,1)S(1)} %fusion.3), channel_id=1, source_target_pairs={{0,64},{64,128},{128,192},{192,256},{256,320},{320,384},{384,448},... | collective-permute-start | bytes 1179656 | tf_op jit(solution)/shard_map/ppermute | solution.py:152
  60.9 11.3 %collective-permute-start.9 = (f16[384,512]{1,0:T(8,128)(2,1)S(1)}, f16[384,512]{1,0:T(8,128)(2,1)S(1)}, u32[]{:S(2)}, u32[]{:S(2)}) collective-permute-start(f16[384,512]{1,0:T(8,128)(2,1)S(1)} %fusion.6), channel_id=1, source_target_pairs={{0,448},{64,0},{128,64},{192,128},{256,192},{320,256},{384,320},{4... | collective-permute-start | bytes 1179656 | tf_op jit(solution)/shard_map/ppermute | solution.py:153
  70.2 12.9 %collective-permute-start.6 = (f16[384,512]{1,0:T(8,128)(2,1)S(1)}, f16[384,512]{1,0:T(8,128)(2,1)S(1)}, u32[]{:S(2)}, u32[]{:S(2)}) collective-permute-start(f16[384,512]{1,0:T(8,128)(2,1)S(1)} %fusion.2), channel_id=1, source_target_pairs={{0,64},{64,128},{128,192},{192,256},{256,320},{320,384},{384,448},... | collective-permute-start | bytes 1179656 | tf_op jit(solution)/shard_map/ppermute | solution.py:152
  72.3 12.8 %collective-permute-start.10 = (f16[384,512]{1,0:T(8,128)(2,1)S(1)}, f16[384,512]{1,0:T(8,128)(2,1)S(1)}, u32[]{:S(2)}, u32[]{:S(2)}) collective-permute-start(f16[384,512]{1,0:T(8,128)(2,1)S(1)} %fusion.5), channel_id=1, source_target_pairs={{0,448},{64,0},{128,64},{192,128},{256,192},{320,256},{384,320},{4... | collective-permute-start | bytes 1179656 | tf_op jit(solution)/shard_map/ppermute | solution.py:153
  77.8 21.1 %collective-permute-start.13 = (bf16[2,512,512]{2,1,0:T(8,128)(2,1)S(1)}, bf16[2,512,512]{2,1,0:T(8,128)(2,1)S(1)}, u32[]{:S(2)}, u32[]{:S(2)}) collective-permute-start(bf16[2,512,512]{2,1,0:T(8,128)(2,1)S(1)} %pad_maximum_fusion.1.refs_9_), channel_id=1, source_target_pairs={{0,1},{1,0},{2,3},{3,2},{4,5},{5,4},{6,7},{7,6},{8,9},{9,8},{10,11... | collective-permute-start | bytes 3145736 | tf_op jit(solution)/shard_map/ppermute | solution.py:22
  83.2 11.9 %collective-permute-start.7 = (f16[384,512]{1,0:T(8,128)(2,1)S(1)}, f16[384,512]{1,0:T(8,128)(2,1)S(1)}, u32[]{:S(2)}, u32[]{:S(2)}) collective-permute-start(f16[384,512]{1,0:T(8,128)(2,1)S(1)} %fusion.1), channel_id=1, source_target_pairs={{0,64},{64,128},{128,192},{192,256},{256,320},{320,384},{384,448},... | collective-permute-start | bytes 1179656 | tf_op jit(solution)/shard_map/ppermute | solution.py:152
  85.2 10.7 %collective-permute-start.11 = (f16[384,512]{1,0:T(8,128)(2,1)S(1)}, f16[384,512]{1,0:T(8,128)(2,1)S(1)}, u32[]{:S(2)}, u32[]{:S(2)}) collective-permute-start(f16[384,512]{1,0:T(8,128)(2,1)S(1)} %fusion.4), channel_id=1, source_target_pairs={{0,448},{64,0},{128,64},{192,128},{256,192},{320,256},{384,320},{4... | collective-permute-start | bytes 1179656 | tf_op jit(solution)/shard_map/ppermute | solution.py:153
  96.1 9.3 %collective-permute-start.12 = (f16[384,512]{1,0:T(8,128)(2,1)S(1)}, f16[384,512]{1,0:T(8,128)(2,1)S(1)}, u32[]{:S(2)}, u32[]{:S(2)}) collective-permute-start(f16[384,512]{1,0:T(8,128)(2,1)S(1)} %fusion.46), channel_id=1, source_target_pairs={{0,32},{32,0},{1,33},{33,1},{2,34},{34,2},{3,35},{35,3},{4,36},{36... | collective-permute-start | bytes 1179656 | tf_op jit(solution)/shard_map/ppermute | solution.py:22
  105.8 9.5 %collective-permute-start.18 = (bf16[384,512]{1,0:T(8,128)(2,1)S(1)}, bf16[384,512]{1,0:T(8,128)(2,1)S(1)}, u32[]{:S(2)}, u32[]{:S(2)}) collective-permute-start(bf16[384,512]{1,0:T(8,128)(2,1)S(1)} %bitcast.127), channel_id=1, source_target_pairs={{0,448},{64,0},{128,64},{192,128},{256,192},{320,256},{384,320},{4... | collective-permute-start | bytes 1179656 | tf_op jit(solution)/shard_map/ppermute | solution.py:171
  110.5 9.7 %collective-permute-start.14 = (bf16[384,512]{1,0:T(8,128)(2,1)S(1)}, bf16[384,512]{1,0:T(8,128)(2,1)S(1)}, u32[]{:S(2)}, u32[]{:S(2)}) collective-permute-start(bf16[384,512]{1,0:T(8,128)(2,1)S(1)} %bitcast.128), channel_id=1, source_target_pairs={{0,64},{64,128},{128,192},{192,256},{256,320},{320,384},{384,448},... | collective-permute-start | bytes 1179656 | tf_op jit(solution)/shard_map/ppermute | solution.py:170
  115.2 9.7 %collective-permute-start.19 = (bf16[384,512]{1,0:T(8,128)(2,1)S(1)}, bf16[384,512]{1,0:T(8,128)(2,1)S(1)}, u32[]{:S(2)}, u32[]{:S(2)}) collective-permute-start(bf16[384,512]{1,0:T(8,128)(2,1)S(1)} %collective-permute-done.18.refs_2_), channel_id=1, source_target_pairs={{0,448},{64,0},{128,64},{192,128},{256,192},{320,256},{384,320},{4... | collective-permute-start | bytes 1179656 | tf_op jit(solution)/shard_map/ppermute | solution.py:171
  120.3 9.7 %collective-permute-start.15 = (bf16[384,512]{1,0:T(8,128)(2,1)S(1)}, bf16[384,512]{1,0:T(8,128)(2,1)S(1)}, u32[]{:S(2)}, u32[]{:S(2)}) collective-permute-start(bf16[384,512]{1,0:T(8,128)(2,1)S(1)} %collective-permute-done.14.refs_1_), channel_id=1, source_target_pairs={{0,64},{64,128},{128,192},{192,256},{256,320},{320,384},{384,448},... | collective-permute-start | bytes 1179656 | tf_op jit(solution)/shard_map/ppermute | solution.py:170
  125.0 10.2 %collective-permute-start.20 = (bf16[384,512]{1,0:T(8,128)(2,1)S(1)}, bf16[384,512]{1,0:T(8,128)(2,1)S(1)}, u32[]{:S(2)}, u32[]{:S(2)}) collective-permute-start(bf16[384,512]{1,0:T(8,128)(2,1)S(1)} %collective-permute-done.19.refs_4_), channel_id=1, source_target_pairs={{0,448},{64,0},{128,64},{192,128},{256,192},{320,256},{384,320},{4... | collective-permute-start | bytes 1179656 | tf_op jit(solution)/shard_map/ppermute | solution.py:171
  130.0 10.5 %collective-permute-start.16 = (bf16[384,512]{1,0:T(8,128)(2,1)S(1)}, bf16[384,512]{1,0:T(8,128)(2,1)S(1)}, u32[]{:S(2)}, u32[]{:S(2)}) collective-permute-start(bf16[384,512]{1,0:T(8,128)(2,1)S(1)} %collective-permute-done.15.refs_3_), channel_id=1, source_target_pairs={{0,64},{64,128},{128,192},{192,256},{256,320},{320,384},{384,448},... | collective-permute-start | bytes 1179656 | tf_op jit(solution)/shard_map/ppermute | solution.py:170
  135.2 9.2 %collective-permute-start.21 = (bf16[384,256]{1,0:T(8,128)(2,1)S(1)}, bf16[384,256]{1,0:T(8,128)(2,1)S(1)}, u32[]{:S(2)}, u32[]{:S(2)}) collective-permute-start(bf16[384,256]{1,0:T(8,128)(2,1)S(1)} %slice.409), channel_id=1, source_target_pairs={{0,448},{64,0},{128,64},{192,128},{256,192},{320,256},{384,320},{4... | collective-permute-start | bytes 589832 | tf_op jit(solution)/shard_map/ppermute | solution.py:175
  140.5 9.5 %collective-permute-start.17 = (bf16[384,256]{1,0:T(8,128)(2,1)S(1)}, bf16[384,256]{1,0:T(8,128)(2,1)S(1)}, u32[]{:S(2)}, u32[]{:S(2)}) collective-permute-start(bf16[384,256]{1,0:T(8,128)(2,1)S(1)} %slice.408), channel_id=1, source_target_pairs={{0,64},{64,128},{128,192},{192,256},{256,320},{320,384},{384,448},... | collective-permute-start | bytes 589832 | tf_op jit(solution)/shard_map/ppermute | solution.py:174
  150.7 8.6 %collective-permute-start.22 = (bf16[256,512]{1,0:T(8,128)(2,1)S(1)}, bf16[256,512]{1,0:T(8,128)(2,1)S(1)}, u32[]{:S(2)}, u32[]{:S(2)}) collective-permute-start(bf16[256,512]{1,0:T(8,128)(2,1)S(1)} %add_convert_fusion.1), channel_id=1, source_target_pairs={{0,2},{2,0},{1,3},{3,1},{4,6},{6,4},{5,7},{7,5},{8,10},{10,8},{9,1... | collective-permute-start | bytes 786440 | tf_op jit(solution)/shard_map/ppermute | solution.py:22
  159.4 16.4 %collective-permute-start.23 = (bf16[8,192,512]{2,1,0:T(8,128)(2,1)}, bf16[8,192,512]{2,1,0:T(8,128)(2,1)}, u32[]{:S(2)}, u32[]{:S(2)}) collective-permute-start(bf16[8,192,512]{2,1,0:T(8,128)(2,1)} %pad_maximum_fusion), channel_id=1, source_target_pairs={{0,1},{1,0},{2,3},{3,2},{4,5},{5,4},{6,7},{7,6},{8,9},{9,8},{10,11... | collective-permute-start | bytes 4718600 | tf_op jit(solution)/shard_map/ppermute | solution.py:22
  172.3 15.7 %all-to-all-start.1 = ((bf16[8,32,512]{2,1,0:T(8,128)(2,1)}), bf16[8,32,512]{2,1,0:T(8,128)(2,1)S(1)}, u32[]{:S(2)}, u32[]{:S(2)}) async-start(bf16[8,32,512]{2,1,0:T(8,128)(2,1)} %bitcast.141), calls=%async_computation.1 | async-start | bytes 524288 | tf_op jit(solution)/shard_map/all_to_all | solution.py:193
  (19 other events, 287.2 us)
